TPU v7x, 32 devices: a whole 2x2x4 slice. The times are simulated.
32 devices in a mesh: narrow: 4 (over y, core), wide: 8 (over z, x).
Axes of the slice: x: 2, y: 2, z: 4, core: 2. Of those that a mesh axis runs over, the one named last changes fastest.
Arguments:
- vis_pixels: bfloat16 [8192, 1536], P(('narrow', 'wide')), may hold values from -6 to 6
- target: bfloat16 [86016, 1536], P(('narrow', 'wide')), may hold values from -6 to 6
- clip_lens: int32 [32, 3], P(('narrow', 'wide')), may hold values from 0 to 2592, as said below
- vis_index: int32 [32, 256], P(('narrow', 'wide')), may hold values from 0 to 2687, as said below
- params_enc: float32 [8564736], P('wide'), may hold values from -2 to 2
- m_enc: float32 [8564736], P('wide'), may hold values from -2.670288e-05 to 2.670288e-05
- v_enc: float32 [8564736], P('wide'), may hold values from 1.20378065e-11 to 4.8114637e-11
- params_dec: float32 [2367488], P('wide'), may hold values from -2 to 2
- m_dec: float32 [2367488], P('wide'), may hold values from -2.670288e-05 to 2.670288e-05
- v_dec: float32 [2367488], P('wide'), may hold values from 1.20378065e-11 to 4.8114637e-11
Outputs:
- loss_sum: float32 [], replicated
- masked_count: float32 [], replicated
- grad_norm: float32 [], replicated
- new_m_enc: float32 [8564736], P('wide')
- new_v_enc: float32 [8564736], P('wide')
- new_params_enc: float32 [8564736], P('wide')
- new_m_dec: float32 [2367488], P('wide')
- new_v_dec: float32 [2367488], P('wide')
- new_params_dec: float32 [2367488], P('wide')
Inputs may be any that keep to these rules, and one draw needn't show every extreme that they name: `clip_lens`: row p is one of (2592, 0, 0), (800, 1568, 0), (800, 800, 800): the clips packed on device p in order, 0 for no clip; every pattern occurs in every draw. `vis_index`: row p lists, clip by clip and within a clip frame by frame, the pack positions of the visible tubelets: a clip of 8 frames of S cells shows the same K cells in every frame (K = 10, 20, 32 for S = 100, 196, 324), increasing within a frame; the remaining slots hold 2687.
All inputs are finite; a program needn't handle non-finite values.
Results may differ from a plain program's by a relative error of at most 0.0005.
The roundings to bfloat16 on the way count: a program that leaves them out, or rounds other values in their place, can miss the bound.
Values may be sent and summed in bfloat16 or wider, within the bound.
No kernel may reach another device: no remote copies, remote signals or barrier semaphores. Data moves between devices by JAX's collectives and lax.ppermute only.
A program may use at most 512 MiB of HBM per device.

v0:
```python
import math

import jax
import jax.numpy as jnp
from jax import lax
from jax.sharding import PartitionSpec as P

D = 768
HEADS = 12
FF = 3072
DD = 384
DHEADS = 6
DFF = 1536
PIX = 1536
QB = 896
STEP = 10


learn_rate = 0.05
BETA_ONE = 0.9
BETA_TWO = 0.95
EPSILON = 1e-08
weight_decay = 0.05
clip_norm = 0.05


def plain_round(value):
    return lax.optimization_barrier(value.astype(jnp.bfloat16)).astype(jnp.float32)


def round_value(value):

    def keep_forward(given):
        return (plain_round(given), None)

    def pass_backward(kept, grad):
        return (grad,)

    rounding = jax.custom_vjp(plain_round)
    rounding.defvjp(keep_forward, pass_backward)
    return rounding(value)


def round_grad(value):

    def unchanged(given):
        return given

    def keep_forward(given):
        return (given, None)

    def round_backward(kept, grad):
        return (plain_round(grad),)

    passing = jax.custom_vjp(unchanged)
    passing.defvjp(keep_forward, round_backward)
    return passing(value)


def product(left, right):
    return jnp.dot(left, right, preferred_element_type=jnp.float32)


def product_sum(form, left, right):
    return jnp.einsum(form, left, right, preferred_element_type=jnp.float32)


def unpack(vector, extents):
    pieces = []
    offset = 0
    for extent in extents:
        length = math.prod(extent)
        pieces.append(vector[offset : offset + length].reshape(extent))
        offset = offset + length
    return pieces


def encoder_shapes():
    return [
        (PIX, D),
        (D,),
        (D,),
        (D,),
        (D, 3 * D),
        (D,),
        (D,),
        (D, D),
        (D,),
        (D,),
        (D,),
        (D, FF),
        (FF,),
        (FF, D),
        (D,),
        (D,),
        (D,),
        (D, DD),
    ]


def decoder_shapes():
    return [
        (DD,),
        (DD,),
        (DD,),
        (DD, 3 * DD),
        (DD,),
        (DD,),
        (DD, DD),
        (DD,),
        (DD,),
        (DD,),
        (DD, DFF),
        (DFF,),
        (DFF, DD),
        (DD,),
        (DD,),
        (DD,),
        (DD, PIX),
        (PIX,),
    ]


def layer_norm(stream, scale_vec, offset_vec):
    center = stream - jnp.mean(stream, axis=-1, keepdims=True)
    spread = jnp.mean(center * center, axis=-1, keepdims=True)
    return center * lax.rsqrt(spread + 1e-06) * scale_vec + offset_vec


def sinusoid(places, columns):
    half_width = columns // 2
    frequency = jnp.exp(
        jnp.arange(half_width, dtype=jnp.float32) * (-math.log(10000.0) / half_width)
    )
    angles = places[:, None] * frequency[None, :]
    return jnp.concatenate([jnp.sin(angles), jnp.cos(angles)], axis=1)


def layout(lengths, visible, row_count):
    positions = jnp.arange(row_count, dtype=jnp.int32)
    clip_ends = jnp.cumsum(lengths)
    starts = clip_ends - lengths
    segment = jnp.sum((positions[:, None] >= clip_ends[None, :]).astype(jnp.int32), axis=1)
    member = segment[:, None] == jnp.arange(3, dtype=jnp.int32)[None, :]
    clip_begin = jnp.sum(jnp.where(member, starts[None, :], 0), axis=1)
    clip_place = (positions - clip_begin).astype(jnp.float32)
    pack_total = clip_ends[2]
    slot_live = (visible < pack_total).astype(jnp.float32)
    shown_flag = jnp.zeros((row_count,), jnp.float32).at[visible].add(slot_live)
    counted = jnp.where(positions < pack_total, 1.0 - shown_flag, 0.0)
    return (segment, clip_place, slot_live, shown_flag, counted)


def attend(queries, key_rows, value_rows, labels_all, head_count, block_rows):
    row_count, columns = queries.shape
    head_size = columns // head_count
    block_count = row_count // block_rows
    queries = queries.reshape(block_count, block_rows, head_count, head_size)
    row_labels = labels_all.reshape(block_count, block_rows)
    key_rows = key_rows.reshape(-1, head_count, head_size)
    value_rows = value_rows.reshape(-1, head_count, head_size)

    def one_block(couple):
        query_block, labels = couple
        scores = product_sum("qhd,khd->hqk", query_block, key_rows) * (1.0 / math.sqrt(head_size))
        allowed = labels[None, :, None] == labels_all[None, None, :]
        scores = jnp.where(allowed, scores, -1e30)
        highest = jnp.max(scores, axis=-1, keepdims=True)
        soft_weights = jnp.exp(scores - highest)
        soft_weights = soft_weights / jnp.sum(soft_weights, axis=-1, keepdims=True)
        mixture = product_sum("hqk,khd->qhd", round_value(soft_weights), value_rows)
        return mixture.reshape(block_rows, columns)

    return lax.map(jax.checkpoint(one_block), (queries, row_labels)).reshape(row_count, columns)


def transformer_block(stream, weights, segment, head_count, block_rows):
    columns = stream.shape[1]
    normed = layer_norm(stream, weights[0], weights[1])
    bias_row = jnp.concatenate([weights[3], jnp.zeros_like(weights[3]), weights[4]])
    packed = round_grad(product(round_value(normed), weights[2]) + bias_row)
    queries = round_value(packed[:, :columns])
    key_rows = round_value(packed[:, columns : 2 * columns])
    value_rows = round_value(packed[:, 2 * columns :])
    mixture = attend(queries, key_rows, value_rows, segment, head_count, block_rows)
    stream = stream + product(round_value(mixture), weights[5]) + weights[6]
    normed = layer_norm(stream, weights[7], weights[8])
    hidden = jax.nn.gelu(product(round_value(normed), weights[9]) + weights[10], approximate=False)
    return stream + product(round_value(hidden), weights[11]) + weights[12]


def pack_loss(enc_vector, dec_vector, pixels, targets, lengths, visible):
    row_count = targets.shape[0]
    slot_count = pixels.shape[0]
    segment, clip_place, slot_live, shown_flag, counted = layout(lengths, visible, row_count)
    encoder = unpack(enc_vector, encoder_shapes())
    decoder = unpack(dec_vector, decoder_shapes())
    tokens = (
        product(round_value(pixels.astype(jnp.float32)), encoder[0])
        + encoder[1]
        + sinusoid(clip_place[visible], D)
    )
    tokens = transformer_block(tokens, encoder[2:15], segment[visible], HEADS, slot_count)
    latent = product(round_value(layer_norm(tokens, encoder[15], encoder[16])), encoder[17])
    placed = jnp.zeros((row_count, DD), jnp.float32).at[visible].add(latent * slot_live[:, None])
    stream = placed + (1.0 - shown_flag)[:, None] * decoder[0][None, :] + sinusoid(clip_place, DD)
    stream = transformer_block(stream, decoder[1:14], segment, DHEADS, QB)
    predicted = (
        product(round_value(layer_norm(stream, decoder[14], decoder[15])), decoder[16])
        + decoder[17]
    )
    raw_rows = targets.astype(jnp.float32)
    center = raw_rows - jnp.mean(raw_rows, axis=1, keepdims=True)
    goal_norm = center * lax.rsqrt(jnp.mean(center * center, axis=1, keepdims=True) + 1e-06)
    errors = jnp.mean((predicted - goal_norm) ** 2, axis=1)
    return jnp.sum(errors * counted)


def adamw_update(master, gradient, moment_one, moment_two, clip_scale):
    gradient = gradient * clip_scale
    moment_one = BETA_ONE * moment_one + (1.0 - BETA_ONE) * gradient
    moment_two = BETA_TWO * moment_two + (1.0 - BETA_TWO) * gradient * gradient
    first_hat = moment_one / (1.0 - BETA_ONE**STEP)
    second_hat = moment_two / (1.0 - BETA_TWO**STEP)
    updated = master - learn_rate * (
        first_hat / (jnp.sqrt(second_hat) + EPSILON) + weight_decay * master
    )
    return (moment_one, moment_two, updated)


def body(
    vis_pixels, target, clip_lens, vis_index, params_enc, m_enc, v_enc, params_dec, m_dec, v_dec
):
    lengths = clip_lens[0]
    visible = vis_index[0]
    count_here = jnp.sum(layout(lengths, visible, target.shape[0])[4])

    def local_loss(enc_vector, dec_vector):
        return pack_loss(enc_vector, dec_vector, vis_pixels, target, lengths, visible)

    enc_full = lax.all_gather(params_enc.astype(jnp.bfloat16), "wide", axis=0, tiled=True)
    dec_full = lax.all_gather(params_dec.astype(jnp.bfloat16), "wide", axis=0, tiled=True)
    loss_here = local_loss(enc_full.astype(jnp.float32), dec_full.astype(jnp.float32))
    loss_sum, masked_count = lax.psum((loss_here, count_here), ("narrow", "wide"))
    cotangent = 1.0 / masked_count
    enc_again = lax.all_gather(params_enc.astype(jnp.bfloat16), "wide", axis=0, tiled=True)
    dec_again = lax.all_gather(params_dec.astype(jnp.bfloat16), "wide", axis=0, tiled=True)
    unused_loss, pull_again = jax.vjp(
        local_loss, enc_again.astype(jnp.float32), dec_again.astype(jnp.float32)
    )
    grad_enc, grad_dec = pull_again(cotangent)
    grad_dec = lax.psum_scatter(grad_dec, "wide", scatter_dimension=0, tiled=True)
    grad_enc = lax.psum_scatter(grad_enc, "wide", scatter_dimension=0, tiled=True)
    grad_enc, grad_dec = (
        lax.psum_scatter(grad_enc, "narrow", scatter_dimension=0, tiled=True),
        lax.psum_scatter(grad_dec, "narrow", scatter_dimension=0, tiled=True),
    )
    grad_enc, grad_dec = (
        lax.all_gather(grad_enc, "narrow", axis=0, tiled=True),
        lax.all_gather(grad_dec, "narrow", axis=0, tiled=True),
    )
    squares = jnp.sum(grad_enc * grad_enc) + jnp.sum(grad_dec * grad_dec)
    squares = lax.psum(squares, "wide")
    grad_norm = jnp.sqrt(squares)
    clip_scale = jnp.minimum(1.0, clip_norm / (grad_norm + 1e-06))
    enc_one, enc_two, enc_new = adamw_update(params_enc, grad_enc, m_enc, v_enc, clip_scale)
    dec_one, dec_two, dec_new = adamw_update(params_dec, grad_dec, m_dec, v_dec, clip_scale)
    return (loss_sum, masked_count, grad_norm, enc_one, enc_two, enc_new, dec_one, dec_two, dec_new)


def solution(mesh):
    placed = (
        P(("narrow", "wide"), None),
        P(("narrow", "wide"), None),
        P(("narrow", "wide"), None),
        P(("narrow", "wide"), None),
        P("wide"),
        P("wide"),
        P("wide"),
        P("wide"),
        P("wide"),
        P("wide"),
    )
    return jax.shard_map(
        body,
        mesh=mesh,
        in_specs=placed,
        out_specs=(P(), P(), P(), P("wide"), P("wide"), P("wide"), P("wide"), P("wide"), P("wide")),
        check_vma=False,
    )
```

profile of v0, /device:TPU:0, one launch (start us, length us, event | category | flops | bytes accessed | tf_op | source)
XLA Modules:
  0.0 4696.5 jit_solution(237235835854350473)
XLA Ops:
  129.0 615.9 %all-gather.10.cloned.1.call-done = bf16[8,1,1070592]{2,1,0:T(2,128)(2,1)} async-done(((bf16[1,1,1070592]{2,1,0:T(2,128)(2,1)}), bf16[8,1,1070592]{2,1,0:T(2,128)(2,1)}) %all-gather.10.cloned.1.call-update) | async-done | bytes 17129488 | tf_op jit(solution)/shard_map/all_gather | solution.py:241
  744.9 309.2 %reduce.6 = bf16[8,1070592]{1,0:T(8,128)(2,1)} reduce(bf16[8,1,1070592]{2,1,0:T(2,128)(2,1)} %all-gather.10.cloned.1.call-done, bf16[]{:T(256)} %constant.491), dimensions={1}, to_apply=%all-gather.reduce_sub_computation | reduce | bytes 34258944 | tf_op jit(solution)/shard_map/all_gather | solution.py:241
  1054.0 37.4 reshape.880
  1223.9 228.1 %while.12 = (s32[]{:T(128)}, bf16[3,896,384]{2,1,0:T(8,128)(2,1)}, s32[3,896]{1,0:T(4,128)}, s32[2688]{0:T(1024)}, bf16[3,896,6,64]{1,3,2,0:T(8,128)(2,1)}, /*in...) while((s32[]{:T(128)}, bf16[3,896,384]{2,1,0:T(8,128)(2,1)}, ...), condition=%wide.region_18.19_spmd, body=%wide.region_15.18_spmd.sunk | while | flops 3788491264 | bytes 186547312 | solution.py:174
  1254.9 28.2 divide_convert_fusion.7
  1330.9 28.2 divide_convert_fusion.7
  1406.8 28.2 divide_convert_fusion.7
  1453.6 226.7 %while.13 = (s32[]{:T(128)}, bf16[3,896,384]{2,1,0:T(8,128)(2,1)}, s32[3,896]{1,0:T(4,128)}, s32[1,1,2688]{2,1,0:T(1,128)S(1)}, bf16[3,896,6,64]{1,3,2,0:T(8,128...) while((s32[]{:T(128)}, bf16[3,896,384]{2,1,0:T(8,128)(2,1)}, ...), condition=%wide.region_33.34_spmd, body=%wide.region_30.33_spmd.sunk | while | flops 3788491264 | bytes 186568816 | solution.py:174
  1484.0 28.2 divide_convert_fusion.8
  1559.3 28.2 divide_convert_fusion.8
  1691.1 42.0 fusion.80
  1740.0 41.9 multiply_convert_fusion
  1802.5 39.8 all-reduce.46
  1958.8 805.4 %while.56 = (s32[]{:T(128)}, f32[2688,6,64]{0,2,1:T(8,128)}, f32[2688,6,64]{0,2,1:T(8,128)}, f32[3,896,6,64]{1,0,3,2:T(4,128)}, bf16[3,896,6,64]{1,3,2,0:T(8,128...) while((s32[]{:T(128)}, f32[2688,6,64]{0,2,1:T(8,128)}, ...), condition=%wide.region_48.49_spmd.clone, body=%wide.region_42.48_spmd.clone.sunk | while | flops 9731850240 | bytes 712320256 | solution.py:174
  2006.8 53.6 %convert_reduce_fusion.7 = (f32[6,896]{1,0:T(8,128)S(1)}, pred[6,896,2688]{2,1,0:T(32,128)(4,1)}, f32[6,896]{1,0:T(8,128)S(1)}, f32[6,896,2688]{2,1,0:T(8,128)}) fusion(f32[6,896]{1,0:T(8,128)S(1)} %get-tuple-element.922, f32[6,896,2688]{2,1,0:T(8,128)} %get-tuple-element.923, pred[896,2688]{1,0:T(8,128)(4,1)S(1)} %broadcast_compare_fusion.10, ...), kind=kOutput, calls=%fused_computation.49.clone.1 | convolution fusion | flops 1979733504 | bytes 135303168 | tf_op jit(solution)/shard_map/transpose(jvp())/while/body/eval_jaxpr/checkpoint/hqk,khd->qhd/dot_general | solution.py:65
  2060.4 67.6 %fusion.372 = (f32[6,896]{1,0:T(8,128)S(1)}, f32[6,896,2688]{2,1,0:T(8,128)}, bf16[6,896,2688]{2,1,0:T(8,128)(2,1)}) fusion(f32[6,896]{1,0:T(8,128)S(1)} %get-tuple-element.922, f32[6,896,2688]{2,1,0:T(8,128)} %get-tuple-element.923, pred[896,2688]{1,0:T(8,128)(4,1)S(1)} %broadcast_compare_fusion.10, f32[6,896]{1,0:T(8,128)S(1)} %neg.109, ...), kind=kLoop, calls=%fused_computation.359.clone.1 | loop fusion | flops 130050816 | bytes 204804096 | tf_op jit(solution)/shard_map/transpose(jvp())/while/body/eval_jaxpr/checkpoint/reduce_sum | solution.py:169
  2140.2 28.9 fusion.375
  2169.2 29.5 fusion.373
  2274.3 53.6 %convert_reduce_fusion.7 = (f32[6,896]{1,0:T(8,128)S(1)}, pred[6,896,2688]{2,1,0:T(32,128)(4,1)}, f32[6,896]{1,0:T(8,128)S(1)}, f32[6,896,2688]{2,1,0:T(8,128)}) fusion(f32[6,896]{1,0:T(8,128)S(1)} %get-tuple-element.922, f32[6,896,2688]{2,1,0:T(8,128)} %get-tuple-element.923, pred[896,2688]{1,0:T(8,128)(4,1)S(1)} %broadcast_compare_fusion.10, ...), kind=kOutput, calls=%fused_computation.49.clone.1 | convolution fusion | flops 1979733504 | bytes 135303168 | tf_op jit(solution)/shard_map/transpose(jvp())/while/body/eval_jaxpr/checkpoint/hqk,khd->qhd/dot_general | solution.py:65
  2327.9 67.6 %fusion.372 = (f32[6,896]{1,0:T(8,128)S(1)}, f32[6,896,2688]{2,1,0:T(8,128)}, bf16[6,896,2688]{2,1,0:T(8,128)(2,1)}) fusion(f32[6,896]{1,0:T(8,128)S(1)} %get-tuple-element.922, f32[6,896,2688]{2,1,0:T(8,128)} %get-tuple-element.923, pred[896,2688]{1,0:T(8,128)(4,1)S(1)} %broadcast_compare_fusion.10, f32[6,896]{1,0:T(8,128)S(1)} %neg.109, ...), kind=kLoop, calls=%fused_computation.359.clone.1 | loop fusion | flops 130050816 | bytes 204804096 | tf_op jit(solution)/shard_map/transpose(jvp())/while/body/eval_jaxpr/checkpoint/reduce_sum | solution.py:169
  2407.7 28.9 fusion.375
  2436.6 30.6 fusion.373
  2543.0 53.6 %convert_reduce_fusion.7 = (f32[6,896]{1,0:T(8,128)S(1)}, pred[6,896,2688]{2,1,0:T(32,128)(4,1)}, f32[6,896]{1,0:T(8,128)S(1)}, f32[6,896,2688]{2,1,0:T(8,128)}) fusion(f32[6,896]{1,0:T(8,128)S(1)} %get-tuple-element.922, f32[6,896,2688]{2,1,0:T(8,128)} %get-tuple-element.923, pred[896,2688]{1,0:T(8,128)(4,1)S(1)} %broadcast_compare_fusion.10, ...), kind=kOutput, calls=%fused_computation.49.clone.1 | convolution fusion | flops 1979733504 | bytes 135303168 | tf_op jit(solution)/shard_map/transpose(jvp())/while/body/eval_jaxpr/checkpoint/hqk,khd->qhd/dot_general | solution.py:65
  2596.5 67.6 %fusion.372 = (f32[6,896]{1,0:T(8,128)S(1)}, f32[6,896,2688]{2,1,0:T(8,128)}, bf16[6,896,2688]{2,1,0:T(8,128)(2,1)}) fusion(f32[6,896]{1,0:T(8,128)S(1)} %get-tuple-element.922, f32[6,896,2688]{2,1,0:T(8,128)} %get-tuple-element.923, pred[896,2688]{1,0:T(8,128)(4,1)S(1)} %broadcast_compare_fusion.10, f32[6,896]{1,0:T(8,128)S(1)} %neg.109, ...), kind=kLoop, calls=%fused_computation.359.clone.1 | loop fusion | flops 130050816 | bytes 204804096 | tf_op jit(solution)/shard_map/transpose(jvp())/while/body/eval_jaxpr/checkpoint/reduce_sum | solution.py:169
  2676.4 28.9 fusion.375
  2705.3 30.6 fusion.373
  2918.8 38.4 pad_add_fusion.1
  2957.3 163.6 %pad_add_fusion = f32[8564736]{0:T(1024)} fusion(f32[1179648]{0:T(1024)} %reshape.826, f32[768]{0:T(1024)S(1)} %copy-done.118, f32[768]{0:T(1024)S(1)} %copy-done.170, f32[768]{0:T(1024)S(1)} %copy-done.171, f32[1769472]{0:T(1024)} %reshape.825, f32[768]{0:T(1024)S(1)} %slice-done.7, f32[768]{0:T(1024)S(1)} %slice_reduce_fusion, f32[589824]{0:T(1024)S(1)} %reshape.817, ...), kind=kLoop, calls=%fused_computation.83 | loop fusion | flops 145600512 | bytes 68514816 | tf_op jit(solution)/shard_map/transpose(jvp())/add_any | solution.py:73
  3123.5 1296.2 %all-reduce.52.cloned.1.call-done = (f32[8564736]{0:T(1024)}, f32[2367488]{0:T(1024)}) async-done(((f32[8564736]{0:T(1024)}, f32[2367488]{0:T(1024)}), (f32[8564736]{0:T(1024)}, f32[2367488]{0:T(1024)})) %all-reduce.52.cloned.1.call-update) | async-done | bytes 43728912
  4427.7 104.4 %all-reduce.54.cloned.1.call-done = (f32[1070592]{0:T(1024)}, f32[295936]{0:T(1024)}) async-done(((f32[1070592]{0:T(1024)}, f32[295936]{0:T(1024)}), (f32[1070592]{0:T(1024)}, f32[295936]{0:T(1024)})) %all-reduce.54.cloned.1.call-update) | async-done | bytes 5466128
  4556.2 32.8 all-gather.12.cloned.1.call-done
  4623.4 44.1 multiply_reduce_fusion.1
  (716 shorter events, 1223.7 us)
Async XLA Ops:
  7.2 1112.4 %copy-start = (bf16[256,1536]{1,0:T(8,128)(2,1)S(1)}, bf16[256,1536]{1,0:T(8,128)(2,1)}, u32[]{:S(2)}) copy-start(bf16[256,1536]{1,0:T(8,128)(2,1)} %param.16) | copy-start | bytes 2359300
  7.2 86.4 %all-gather.8.cloned.1.call-start = ((), (), s32[]{:S(2)}) async-start(), calls=%async_computation | async-start | bytes 5326848 | tf_op jit(solution)/shard_map/all_gather | solution.py:242
  9.5 735.4 %all-gather.10.cloned.1.call-start = ((), (), s32[]{:S(2)}) async-start(), calls=%async_computation.1 | async-start | bytes 38541312 | tf_op jit(solution)/shard_map/all_gather | solution.py:241
  11.9 29.4 copy-start.173
  37.2 4382.5 %all-reduce.52.cloned.1.call-start = ((), (), s32[]{:S(2)}) async-start(), calls=%async_computation.4 | async-start | bytes 87457792
  117.4 1074.3 %copy-start.98 = (f32[384]{0:T(512)}, f32[384]{0:T(512)S(1)}, u32[]{:S(2)}) copy-start(f32[384]{0:T(512)S(1)} %get-tuple-element.683) | copy-start | bytes 4612
  1094.1 78.2 %copy-start.95 = (f32[768]{0:T(1024)}, f32[768]{0:T(1024)S(1)}, u32[]{:S(2)}) copy-start(f32[768]{0:T(1024)S(1)} %get-tuple-element.654) | copy-start | bytes 9220
  1223.9 229.7 %copy-start.81 = (s32[1,1,2688]{2,1,0:T(1,128)S(1)}, s32[1,1,2688]{2,1,0:T(1,128)}, u32[]{:S(2)}) copy-start(s32[1,1,2688]{2,1,0:T(1,128)} %broadcast_in_dim.375) | copy-start | bytes 32260
  1453.6 226.7 %copy-start.114 = (f32[384]{0:T(512)S(1)}, f32[384]{0:T(512)}, u32[]{:S(2)}) copy-start(f32[384]{0:T(512)} %get-tuple-element.680) | copy-start | bytes 4612
  1691.0 42.0 copy-start.72
  1691.1 42.0 copy-start.177
  1740.0 41.9 copy-start.9
  2060.4 67.6 %copy-start.5 = (f32[2688,6,64]{0,2,1:T(8,128)S(1)}, f32[2688,6,64]{0,2,1:T(8,128)}, u32[]{:S(2)}) copy-start(f32[2688,6,64]{0,2,1:T(8,128)} %get-tuple-element.999) | copy-start | bytes 12386308 | tf_op jit(solution)/shard_map/transpose(jvp())/while
  2140.2 28.9 copy-start.6
  2140.2 28.9 copy-start.23
  2327.9 67.6 %copy-start.5 = (f32[2688,6,64]{0,2,1:T(8,128)S(1)}, f32[2688,6,64]{0,2,1:T(8,128)}, u32[]{:S(2)}) copy-start(f32[2688,6,64]{0,2,1:T(8,128)} %get-tuple-element.999) | copy-start | bytes 12386308 | tf_op jit(solution)/shard_map/transpose(jvp())/while
  2407.7 28.9 copy-start.6
  2407.7 28.9 copy-start.23
  2596.5 67.6 %copy-start.5 = (f32[2688,6,64]{0,2,1:T(8,128)S(1)}, f32[2688,6,64]{0,2,1:T(8,128)}, u32[]{:S(2)}) copy-start(f32[2688,6,64]{0,2,1:T(8,128)} %get-tuple-element.999) | copy-start | bytes 12386308 | tf_op jit(solution)/shard_map/transpose(jvp())/while
  2918.7 38.5 slice-start.7
  2918.7 38.5 copy-start.115
  2918.7 38.5 copy-start.116
  2918.8 38.5 copy-start.117
  2918.8 38.5 copy-start.118
  2918.8 38.5 copy-start.136
  2918.8 38.5 copy-start.168
  2918.8 38.5 copy-start.169
  2918.8 38.5 copy-start.170
  2918.8 38.5 copy-start.171
  3121.0 1411.1 %all-reduce.54.cloned.1.call-start = ((), (), s32[]{:S(2)}) async-start(), calls=%async_computation.5 | async-start | bytes 10936320
  4426.4 125.5 %all-gather.14.cloned.1.call-start = ((), (), s32[]{:S(2)}) async-start(), calls=%async_computation.3 | async-start | bytes 1479680 | tf_op jit(solution)/shard_map/all_gather | solution.py:260
  4534.1 54.9 %all-gather.12.cloned.1.call-start = ((), (), s32[]{:S(2)}) async-start(), calls=%async_computation.2 | async-start | bytes 5352960 | tf_op jit(solution)/shard_map/all_gather | solution.py:259
  (175 other events, 1196.7 us)
Sparse Core Ops, SparseCore 0:
  10.8 82.7 all-gather.7
  95.7 649.0 all-gather.9
  3121.1 1298.5 all-reduce.51
  4426.5 105.5 all-reduce.53
  4534.2 17.6 all-gather.13
  4554.0 34.9 all-gather.11
where the time goes:
time: 4710 us; the launch traced here: 4700 us
  waiting for transfers between devices  2070 us (44%)
  other arithmetic  1130 us (24%)
  matrix products  956 us (20%)
  local copies, waits for them, and re-layouts  452 us (10%)
  blocking collectives  61.6 us (1%)
    unnamed x8, waiting for transfers between devices  1400 us
    all_gather x1, waiting for transfers between devices, body(): lax.all_gather(params_enc.astype(jnp.bfloat16), 'wide', axis=0, tiled=True)  616 us
    dot_general x27, matrix products, product_sum(): return jnp.einsum(form, left, right, preferred_element_type=jnp.float32)  540 us
    all_gather x1, other arithmetic, body(): lax.all_gather(params_enc.astype(jnp.bfloat16), 'wide', axis=0, tiled=True)  309 us
    dot_general x36, matrix products, product(): return jnp.dot(left, right, preferred_element_type=jnp.float32)  254 us
    reduce_sum x4, other arithmetic, one_block(): soft_weights = jnp.exp(scores - highest)  204 us
    add_any x2, other arithmetic, unpack(): pieces.append(vector[offset:offset + length].reshape(extent))  202 us
    sub x7, matrix products, one_block(): soft_weights = jnp.exp(scores - highest)  162 us
  transfers between devices with their start and end apart: 6, of which 6 were waited for; matrix products, arithmetic and copies ran while one was open for 3% of the time, Pallas kernels for 0%

commit v1 on v0

v1 whole, which is shorter than its diff:
```python
import functools
import math

import jax
import jax.numpy as jnp
from jax import lax
from jax.experimental import pallas as pl
from jax.experimental.pallas import tpu as pltpu
from jax.sharding import PartitionSpec as P

D = 768
HEADS = 12
FF = 3072
DD = 384
DHEADS = 6
DFF = 1536
PIX = 1536
STEP = 10
ROWS = 2592

learn_rate = 0.05
BETA_ONE = 0.9
BETA_TWO = 0.95
EPSILON = 1e-08
weight_decay = 0.05
clip_norm = 0.05

F = jnp.float32
B = jnp.bfloat16
AXES = ("narrow", "wide")
NT = (((1,), (1,)), ((), ()))
NN = (((1,), (0,)), ((), ()))
TN = (((0,), (0,)), ((), ()))
VMEM_LIMIT = 60 << 20


def mm(left, right, dims=NN):
    return lax.dot_general(left, right, dims, preferred_element_type=F)


def plain_round(value):
    return lax.optimization_barrier(value.astype(B)).astype(F)


def round_value(value):
    rounding = jax.custom_vjp(plain_round)
    rounding.defvjp(lambda given: (plain_round(given), None), lambda kept, grad: (grad,))
    return rounding(value)


def round_grad(value):
    passing = jax.custom_vjp(lambda given: given)
    passing.defvjp(lambda given: (given, None), lambda kept, grad: (plain_round(grad),))
    return passing(value)


def product(left, right):
    return jnp.dot(left, right, preferred_element_type=F)


def product_sum(form, left, right):
    return jnp.einsum(form, left, right, preferred_element_type=F)


def unpack(vector, extents):
    pieces = []
    offset = 0
    for extent in extents:
        length = math.prod(extent)
        pieces.append(vector[offset : offset + length].reshape(extent))
        offset = offset + length
    return pieces


ENC_SHAPES = [
    (PIX, D), (D,), (D,), (D,), (D, 3 * D), (D,), (D,), (D, D), (D,), (D,), (D,),
    (D, FF), (FF,), (FF, D), (D,), (D,), (D,), (D, DD),
]
DEC_SHAPES = [
    (DD,), (DD,), (DD,), (DD, 3 * DD), (DD,), (DD,), (DD, DD), (DD,), (DD,), (DD,),
    (DD, DFF), (DFF,), (DFF, DD), (DD,), (DD,), (DD,), (DD, PIX), (PIX,),
]


def layer_norm(stream, scale_vec, offset_vec):
    center = stream - jnp.mean(stream, axis=-1, keepdims=True)
    spread = jnp.mean(center * center, axis=-1, keepdims=True)
    return center * lax.rsqrt(spread + 1e-06) * scale_vec + offset_vec


def sinusoid(places, columns):
    half_width = columns // 2
    frequency = jnp.exp(jnp.arange(half_width, dtype=F) * (-math.log(10000.0) / half_width))
    angles = places[:, None] * frequency[None, :]
    return jnp.concatenate([jnp.sin(angles), jnp.cos(angles)], axis=1)


def layout(lengths, visible, row_count):
    positions = jnp.arange(row_count, dtype=jnp.int32)
    clip_ends = jnp.cumsum(lengths)
    starts = clip_ends - lengths
    segment = jnp.sum((positions[:, None] >= clip_ends[None, :]).astype(jnp.int32), axis=1)
    member = segment[:, None] == jnp.arange(3, dtype=jnp.int32)[None, :]
    clip_begin = jnp.sum(jnp.where(member, starts[None, :], 0), axis=1)
    clip_place = (positions - clip_begin).astype(F)
    pack_total = clip_ends[2]
    slot_live = (visible < pack_total).astype(F)
    shown_flag = jnp.zeros((row_count,), F).at[visible].add(slot_live)
    counted = jnp.where(positions < pack_total, 1.0 - shown_flag, 0.0)
    return (segment, clip_place, slot_live, shown_flag, counted)


def slot_layout(lengths, visible):
    clip_ends = jnp.cumsum(lengths)
    starts = clip_ends - lengths
    segment = jnp.sum((visible[:, None] >= clip_ends[None, :]).astype(jnp.int32), axis=1)
    member = segment[:, None] == jnp.arange(3, dtype=jnp.int32)[None, :]
    clip_begin = jnp.sum(jnp.where(member, starts[None, :], 0), axis=1)
    return segment, (visible - clip_begin).astype(F)


def encode(encoder, pixels, segment, places):
    tokens = product(pixels.astype(F), encoder[0]) + encoder[1] + places
    weights = encoder[2:15]
    rows, columns = tokens.shape
    normed = layer_norm(tokens, weights[0], weights[1])
    bias_row = jnp.concatenate([weights[3], jnp.zeros_like(weights[3]), weights[4]])
    packed = round_grad(product(round_value(normed), weights[2]) + bias_row)
    queries, key_rows, value_rows = (
        round_value(packed[:, i * columns : (i + 1) * columns]).reshape(rows, HEADS, columns // HEADS)
        for i in range(3)
    )
    scores = product_sum("qhd,khd->hqk", queries, key_rows) * (1.0 / math.sqrt(columns // HEADS))
    allowed = segment[None, :, None] == segment[None, None, :]
    scores = jnp.where(allowed, scores, -1e30)
    soft = jnp.exp(scores - jnp.max(scores, axis=-1, keepdims=True))
    soft = soft / jnp.sum(soft, axis=-1, keepdims=True)
    mixture = product_sum("hqk,khd->qhd", round_value(soft), value_rows).reshape(rows, columns)
    tokens = tokens + product(round_value(mixture), weights[5]) + weights[6]
    normed = layer_norm(tokens, weights[7], weights[8])
    hidden = jax.nn.gelu(product(round_value(normed), weights[9]) + weights[10], approximate=False)
    tokens = tokens + product(round_value(hidden), weights[11]) + weights[12]
    return product(round_value(layer_norm(tokens, encoder[15], encoder[16])), encoder[17])


def norm_rows(x):
    center = x - jnp.mean(x, axis=1, keepdims=True)
    inverse = lax.rsqrt(jnp.mean(center * center, axis=1, keepdims=True) + 1e-06)
    return center * inverse, inverse


def norm_back(grad, hat, inverse):
    return inverse * (
        grad
        - jnp.mean(grad, axis=1, keepdims=True)
        - hat * jnp.mean(grad * hat, axis=1, keepdims=True)
    )


def total(x):
    return jnp.sum(x, axis=0, keepdims=True)


def qkv_kernel(x_ref, w_ref, vec_ref, o_ref):
    hat, inverse = norm_rows(x_ref[...])
    normed = (hat * vec_ref[0:1, :DD] + vec_ref[1:2, :DD]).astype(B)
    o_ref[...] = (mm(normed, w_ref[...]) + vec_ref[2:3, :]).astype(B)


def qkv_forward(x, w, vec, bm=432):
    full = lambda a: pl.BlockSpec(a.shape, lambda i: (0, 0))
    return pl.pallas_call(
        qkv_kernel,
        grid=(ROWS // bm,),
        in_specs=[pl.BlockSpec((bm, DD), lambda i: (i, 0)), full(w), full(vec)],
        out_specs=pl.BlockSpec((bm, 3 * DD), lambda i: (i, 0)),
        out_shape=jax.ShapeDtypeStruct((ROWS, 3 * DD), B),
        compiler_params=pltpu.CompilerParams(vmem_limit_bytes=VMEM_LIMIT),
        name="dec_qkv",
    )(x, w, vec)


def lanes_low(rows):
    return lax.broadcasted_iota(jnp.int32, (rows, 128), 1) < 64


def attend_kernel(q_ref, k_ref, v_ref, qf_ref, kf_ref, o_ref, lse_ref, k0, k1):
    rows, bq = k_ref.shape[0], q_ref.shape[0]

    @pl.when(pl.program_id(1) == 0)
    def _():
        low = lanes_low(rows)
        keys, marks = k_ref[...], kf_ref[...]
        k0[...] = jnp.where(low, keys, marks)
        k1[...] = jnp.where(low, marks, keys)

    low = lanes_low(bq)
    q, qf = q_ref[...] * jnp.asarray(0.125, B), qf_ref[...]
    outs, logs = [], []
    for h in range(2):
        s = mm(jnp.where(low, q, qf) if h == 0 else jnp.where(low, qf, q), (k0, k1)[h][...], NT)
        m = jnp.max(s, axis=1, keepdims=True)
        e = jnp.exp(s - m)
        l = jnp.sum(e, axis=1, keepdims=True)
        outs.append(mm((e * (1.0 / l)).astype(B), v_ref[...]))
        logs.append(m + jnp.log(l))
    o_ref[...] = jnp.where(low, outs[0], outs[1]).astype(B)
    lse_ref[0] = jnp.where(low, logs[0], logs[1])


def attend_forward(qkv, qf, kf, bq=432):
    return pl.pallas_call(
        attend_kernel,
        grid=(3, ROWS // bq),
        in_specs=[
            pl.BlockSpec((bq, 128), lambda h, i: (i, h)),
            pl.BlockSpec((ROWS, 128), lambda h, i: (0, 3 + h)),
            pl.BlockSpec((ROWS, 128), lambda h, i: (0, 6 + h)),
            pl.BlockSpec((bq, 128), lambda h, i: (i, 0)),
            pl.BlockSpec((ROWS, 128), lambda h, i: (0, 0)),
        ],
        out_specs=[
            pl.BlockSpec((bq, 128), lambda h, i: (i, h)),
            pl.BlockSpec((1, bq, 128), lambda h, i: (h, i, 0)),
        ],
        out_shape=[
            jax.ShapeDtypeStruct((ROWS, DD), B),
            jax.ShapeDtypeStruct((3, ROWS, 128), F),
        ],
        scratch_shapes=[pltpu.VMEM((ROWS, 128), B)] * 2,
        compiler_params=pltpu.CompilerParams(vmem_limit_bytes=VMEM_LIMIT),
        name="dec_attend",
    )(qkv, qkv, qkv, qf, kf)


def attend_back_kernel(
    kc, q_ref, k_ref, v_ref, qf_ref, kf_ref, da_ref, st_ref, dq_ref, dk_ref, dv_ref,
    k0, k1, z0, z1, dk_sum, dv_sum,
):
    rows, bq = k_ref.shape[0], q_ref.shape[0]
    step = pl.program_id(1)

    @pl.when(step == 0)
    def _():
        low = lanes_low(rows)
        keys, marks = k_ref[...], kf_ref[...]
        zero = jnp.zeros_like(keys)
        k0[...] = jnp.where(low, keys, marks)
        k1[...] = jnp.where(low, marks, keys)
        z0[...] = jnp.where(low, keys, zero)
        z1[...] = jnp.where(low, zero, keys)
        dk_sum[...] = jnp.zeros_like(dk_sum)
        dv_sum[...] = jnp.zeros_like(dv_sum)

    low = lanes_low(bq)
    q, qf, da = q_ref[...] * jnp.asarray(0.125, B), qf_ref[...], da_ref[...]
    zero = jnp.zeros_like(q)
    qs = (jnp.where(low, q, qf), jnp.where(low, qf, q))
    qz = (jnp.where(low, q, zero), jnp.where(low, zero, q))
    dz = (jnp.where(low, da, zero), jnp.where(low, zero, da))
    stats = st_ref[0]
    dq = jnp.zeros((bq, 128), F)
    for c in range(rows // kc):
        part = slice(c * kc, (c + 1) * kc)
        v = v_ref[part, :]
        for h in range(2):
            s = mm((k0, k1)[h][part, :], qs[h], NT)
            p = jnp.exp(s - stats[h : h + 1, :])
            dv_sum[part, :] += mm(p.astype(B), dz[h])
            dp = mm(v, dz[h], NT)
            ds = (p * (dp - stats[2 + h : 3 + h, :])).astype(B)
            dk_sum[part, :] += mm(ds, qz[h])
            dq += mm(ds, (z0, z1)[h][part, :], TN)
    dq_ref[...] = (dq * 0.125).astype(B)

    @pl.when(step == pl.num_programs(1) - 1)
    def _():
        dk_ref[...] = dk_sum[...].astype(B)
        dv_ref[...] = dv_sum[...].astype(B)


def attend_back(qkv, qf, kf, da, stats, bq=432, kc=864):
    nq = ROWS // bq
    return pl.pallas_call(
        functools.partial(attend_back_kernel, kc),
        grid=(3, nq),
        in_specs=[
            pl.BlockSpec((bq, 128), lambda h, i: (i, h)),
            pl.BlockSpec((ROWS, 128), lambda h, i: (0, 3 + h)),
            pl.BlockSpec((ROWS, 128), lambda h, i: (0, 6 + h)),
            pl.BlockSpec((bq, 128), lambda h, i: (i, 0)),
            pl.BlockSpec((ROWS, 128), lambda h, i: (0, 0)),
            pl.BlockSpec((bq, 128), lambda h, i: (i, h)),
            pl.BlockSpec((1, 8, bq), lambda h, i: (h * nq + i, 0, 0)),
        ],
        out_specs=[
            pl.BlockSpec((bq, 128), lambda h, i: (i, h)),
            pl.BlockSpec((ROWS, 128), lambda h, i: (0, h)),
            pl.BlockSpec((ROWS, 128), lambda h, i: (0, h)),
        ],
        out_shape=[jax.ShapeDtypeStruct((ROWS, DD), B)] * 3,
        scratch_shapes=[pltpu.VMEM((ROWS, 128), B)] * 4 + [pltpu.VMEM((ROWS, 128), F)] * 2,
        compiler_params=pltpu.CompilerParams(vmem_limit_bytes=VMEM_LIMIT),
        name="dec_attend_back",
    )(qkv, qkv, qkv, qf, kf, da, stats)


def mlp_kernel(
    x_ref, a_ref, t_ref, row_ref, wo_ref, wu_ref, wd_ref, wh_ref, vec_ref,
    da_ref, dx_ref, dd_ref, go_ref, gu_ref, gd_ref, gh_ref, gv_ref,
):
    @pl.when(pl.program_id(0) == 0)
    def _():
        for ref in (go_ref, gu_ref, gd_ref, gh_ref, gv_ref):
            ref[...] = jnp.zeros_like(ref)

    a = a_ref[...]
    x1 = x_ref[...] + mm(a, wo_ref[...]) + vec_ref[0:1, :DD]
    hat2, inv2 = norm_rows(x1)
    n2 = (hat2 * vec_ref[1:2, :DD] + vec_ref[2:3, :DD]).astype(B)
    h = mm(n2, wu_ref[...]) + vec_ref[3:4, :]
    cdf = 0.5 * (1.0 + lax.erf(h * (1.0 / math.sqrt(2.0))))
    u = (h * cdf).astype(B)
    slope = cdf + h * jnp.exp(-0.5 * h * h) * (1.0 / math.sqrt(2.0 * math.pi))
    x2 = x1 + mm(u, wd_ref[...]) + vec_ref[4:5, :DD]
    hatf, invf = norm_rows(x2)
    nf = (hatf * vec_ref[5:6, :DD] + vec_ref[6:7, :DD]).astype(B)
    pred = mm(nf, wh_ref[...]) + vec_ref[7:8, :]
    goal, unused = norm_rows(t_ref[...].astype(F))
    err = pred - goal
    gv_ref[8:9, :] += total(err * err * row_ref[:, 0:1])
    dpred = err * row_ref[:, 1:2]
    gv_ref[7:8, :] += total(dpred)
    dpred = dpred.astype(B)
    gh_ref[...] += mm(nf, dpred, TN)
    dnf = mm(dpred, wh_ref[...], NT)
    gv_ref[5:6, :DD] += total(dnf * hatf)
    gv_ref[6:7, :DD] += total(dnf)
    dx2 = norm_back(dnf * vec_ref[5:6, :DD], hatf, invf)
    gv_ref[4:5, :DD] += total(dx2)
    dx2b = dx2.astype(B)
    gd_ref[...] += mm(u, dx2b, TN)
    dh = mm(dx2b, wd_ref[...], NT) * slope
    gv_ref[3:4, :] += total(dh)
    dh = dh.astype(B)
    gu_ref[...] += mm(n2, dh, TN)
    dn2 = mm(dh, wu_ref[...], NT)
    gv_ref[1:2, :DD] += total(dn2 * hat2)
    gv_ref[2:3, :DD] += total(dn2)
    dx1 = dx2 + norm_back(dn2 * vec_ref[1:2, :DD], hat2, inv2)
    gv_ref[0:1, :DD] += total(dx1)
    dx_ref[...] = dx1
    dx1 = dx1.astype(B)
    go_ref[...] += mm(a, dx1, TN)
    da = mm(dx1, wo_ref[...], NT).astype(B)
    da_ref[...] = da
    head_of = lax.broadcasted_iota(jnp.int32, (DD, 128), 0) // 64
    pick = (head_of == lax.broadcasted_iota(jnp.int32, (DD, 128), 1)).astype(F)
    dd_ref[...] = lax.dot_general(
        da.astype(F) * a.astype(F), pick, NN, precision=lax.Precision.HIGHEST, preferred_element_type=F
    )


def mlp_both(x, a, target, rows, wo, wu, wd, wh, vec, bm=432):
    full = lambda shape: pl.BlockSpec(shape, lambda i: (0, 0))
    part = lambda width: pl.BlockSpec((bm, width), lambda i: (i, 0))
    sums = [wo.shape, wu.shape, wd.shape, wh.shape, vec.shape]
    return pl.pallas_call(
        mlp_kernel,
        grid=(ROWS // bm,),
        in_specs=[part(DD), part(DD), part(PIX), part(128)]
        + [full(w.shape) for w in (wo, wu, wd, wh, vec)],
        out_specs=[part(DD), part(DD), part(128)] + [full(s) for s in sums],
        out_shape=[
            jax.ShapeDtypeStruct((ROWS, DD), B),
            jax.ShapeDtypeStruct((ROWS, DD), F),
            jax.ShapeDtypeStruct((ROWS, 128), F),
        ]
        + [jax.ShapeDtypeStruct(s, F) for s in sums],
        compiler_params=pltpu.CompilerParams(vmem_limit_bytes=VMEM_LIMIT),
        name="dec_mlp",
    )(x, a, target, rows, wo, wu, wd, wh, vec)


def qkv_back_kernel(x_ref, dx_ref, dq_ref, dk_ref, dv_ref, row_ref, w_ref, vec_ref, o_ref, g_ref, gv_ref):
    @pl.when(pl.program_id(0) == 0)
    def _():
        for ref in (g_ref, gv_ref):
            ref[...] = jnp.zeros_like(ref)

    hat, inverse = norm_rows(x_ref[...])
    normed = (hat * vec_ref[0:1, :DD] + vec_ref[1:2, :DD]).astype(B)
    dn = jnp.zeros(hat.shape, F)
    for i, ref in enumerate((dq_ref, dk_ref, dv_ref)):
        part = slice(i * DD, (i + 1) * DD)
        dp = ref[...]
        g_ref[:, part] += mm(normed, dp, TN)
        dn += mm(dp, w_ref[:, part], NT)
        if i != 1:
            gv_ref[2:3, part] += total(dp.astype(F))
    gv_ref[0:1, :DD] += total(dn * hat)
    gv_ref[1:2, :DD] += total(dn)
    dx = dx_ref[...] + norm_back(dn * vec_ref[0:1, :DD], hat, inverse)
    o_ref[...] = dx
    gv_ref[3:4, :DD] += total(dx * row_ref[:, 2:3])


def qkv_back(x, dx, dq, dk, dv, rows, w, vec, bm=432):
    full = lambda shape: pl.BlockSpec(shape, lambda i: (0, 0))
    part = lambda width: pl.BlockSpec((bm, width), lambda i: (i, 0))
    return pl.pallas_call(
        qkv_back_kernel,
        grid=(ROWS // bm,),
        in_specs=[part(DD)] * 5 + [part(128), full(w.shape), full(vec.shape)],
        out_specs=[part(DD), full(w.shape), full(vec.shape)],
        out_shape=[
            jax.ShapeDtypeStruct((ROWS, DD), F),
            jax.ShapeDtypeStruct(w.shape, F),
            jax.ShapeDtypeStruct(vec.shape, F),
        ],
        compiler_params=pltpu.CompilerParams(vmem_limit_bytes=VMEM_LIMIT),
        name="dec_qkv_back",
    )(x, dx, dq, dk, dv, rows, w, vec)


def stack_rows(pieces, width, count=8):
    rows = [jnp.pad(p.astype(F), (0, width - p.shape[0])) for p in pieces]
    rows += [jnp.zeros((width,), F)] * (count - len(rows))
    return jnp.stack(rows)


class Links:
    def __init__(self, mesh):
        self.narrow, self.wide = mesh.shape["narrow"], mesh.shape["wide"]
        self.wide_bits = self.wide.bit_length() - 1
        self.narrow_bits = self.narrow.bit_length() - 1

    def bits(self):
        return [("wide", b) for b in reversed(range(self.wide_bits))] + [
            ("narrow", b) for b in reversed(range(self.narrow_bits))
        ]

    def mine(self, bit):
        return (lax.axis_index(bit[0]) >> bit[1]) & 1

    def swap(self, value, bit):
        mask = 1 << bit[1] if bit[0] == "wide" else self.wide << bit[1]
        pairs = [(i, i ^ mask) for i in range(self.narrow * self.wide)]
        return lax.ppermute(value, AXES, pairs)

    def add_all(self, value, bits):
        for bit in bits:
            value = value + self.swap(value, bit)
        return value

    def scatter_sum(self, value, axes, order):
        axes = list(axes)
        for bit in order:
            place = axes.index(bit)
            mine = self.mine(bit)
            away = lax.dynamic_index_in_dim(value, 1 - mine, place, keepdims=False)
            kept = lax.dynamic_index_in_dim(value, mine, place, keepdims=False)
            value = kept + self.swap(away, bit)
            axes.pop(place)
        return value

    def gather(self, value, axes, order):
        have = []
        for bit in order:
            other = self.swap(value, bit)
            low = self.mine(bit) == 0
            after = [b for b in axes if b in have or b == bit]
            place = after.index(bit)
            value = jnp.stack([jnp.where(low, value, other), jnp.where(low, other, value)], axis=place)
            have.append(bit)
        return value


def piece_rows(length, links):
    rows = -(-length // (128 * links.wide * links.narrow))
    return -(-rows // 32) * 32


def gather_params(shard, links):
    rows = piece_rows(shard.shape[0] * links.wide, links)
    flat = jnp.pad(shard.astype(B), (0, links.narrow * rows * 128 - shard.shape[0]))
    piece = lax.dynamic_index_in_dim(
        flat.reshape(links.narrow, rows, 128), lax.axis_index("narrow"), 0, keepdims=False
    )
    bits = links.bits()
    x, upper = ("wide", 0), [("wide", b) for b in reversed(range(1, links.wide_bits))]
    y, core = ("narrow", 1), ("narrow", 0)
    half = rows // 2
    one = links.gather(piece[:half], bits, upper + [x, y, core])
    two = links.gather(piece[half:], bits, upper + [y, x, core])
    both = jnp.concatenate([one, two], axis=-2).reshape(links.wide, links.narrow * rows * 128)
    return both[:, : shard.shape[0]].reshape(-1)


def scatter_grads(flat, links):
    rows = piece_rows(flat.shape[0], links)
    shard = flat.shape[0] // links.wide
    value = jnp.pad(flat.reshape(links.wide, shard), ((0, 0), (0, links.narrow * rows * 128 - shard)))
    value = value.reshape((2,) * (links.wide_bits + links.narrow_bits) + (rows, 128))
    bits = links.bits()
    x, upper = ("wide", 0), [("wide", b) for b in reversed(range(1, links.wide_bits))]
    y, core = ("narrow", 1), ("narrow", 0)
    half = rows // 2
    one = links.scatter_sum(value[..., :half, :], bits, [core, x, y] + upper)
    two = links.scatter_sum(value[..., half:, :], bits, [core, y, x] + upper)
    return jnp.concatenate([one, two])


def join_shard(piece, shard, links):
    axes = [("narrow", b) for b in reversed(range(links.narrow_bits))]
    whole = links.gather(piece, axes, [("narrow", 1), ("narrow", 0)])
    return whole.reshape(-1)[:shard]


def adamw_update(master, gradient, moment_one, moment_two, clip_scale):
    gradient = gradient * clip_scale
    moment_one = BETA_ONE * moment_one + (1.0 - BETA_ONE) * gradient
    moment_two = BETA_TWO * moment_two + (1.0 - BETA_TWO) * gradient * gradient
    first_hat = moment_one / (1.0 - BETA_ONE**STEP)
    second_hat = moment_two / (1.0 - BETA_TWO**STEP)
    updated = master - learn_rate * (
        first_hat / (jnp.sqrt(second_hat) + EPSILON) + weight_decay * master
    )
    return (moment_one, moment_two, updated)


def body(
    links, vis_pixels, target, clip_lens, vis_index, params_enc, m_enc, v_enc, params_dec, m_dec, v_dec
):
    lengths = clip_lens[0]
    visible = vis_index[0]
    segment, clip_place, slot_live, shown_flag, counted = layout(lengths, visible, target.shape[0])
    masked_count = links.add_all(jnp.sum(counted), links.bits())
    cotangent = 1.0 / masked_count
    segment, clip_place, shown_flag, counted = (
        v[:ROWS] for v in (segment, clip_place, shown_flag, counted)
    )
    rows = jnp.stack([counted, counted * (cotangent * (2.0 / PIX)), 1.0 - shown_flag], axis=1)
    rows = jnp.pad(rows, ((0, 0), (0, 125)))
    lane = jnp.arange(128, dtype=jnp.int32)[None, :] % 64
    mark = lane == segment[:, None]
    q_marks = mark.astype(B)
    k_marks = jnp.where(mark | (lane > 3), 0.0, -1e30).astype(B)

    enc_full = gather_params(params_enc, links)
    dec_full = gather_params(params_dec, links)
    encoder = [w.astype(F) for w in unpack(enc_full, ENC_SHAPES)]
    dec = unpack(dec_full, DEC_SHAPES)
    slot_segment, slot_place = slot_layout(lengths, visible)
    latent, pull = jax.vjp(
        lambda weights: encode(weights, vis_pixels, slot_segment, sinusoid(slot_place, D)), encoder
    )

    place_rows = jnp.where(visible < ROWS, visible, ROWS)
    placed = jnp.zeros((ROWS, DD), F).at[place_rows].add(latent * slot_live[:, None], mode="drop")
    x0 = placed + (1.0 - shown_flag)[:, None] * dec[0].astype(F)[None, :] + sinusoid(clip_place, DD)
    bias = jnp.concatenate([dec[4], jnp.zeros_like(dec[4]), dec[5]])
    vec_one = stack_rows([dec[1], dec[2], bias], 3 * DD)
    vec_two = stack_rows([dec[7], dec[8], dec[9], dec[11], dec[13], dec[14], dec[15], dec[17]], DFF, 16)
    qkv = qkv_forward(x0, dec[3], vec_one)
    a, lse = attend_forward(qkv, q_marks, k_marks)
    da, dx1, dd, g_out, g_up, g_down, g_head, g_two = mlp_both(
        x0, a, target, rows, dec[6], dec[10], dec[12], dec[16], vec_two
    )
    loss_sum = links.add_all(jnp.sum(g_two[8]) / PIX, links.bits())
    blocks = ROWS // 432
    lse = jnp.stack([lse[:, :, 0], lse[:, :, 64]], axis=1)
    dd = dd[:, :DHEADS].T.reshape(3, 2, ROWS)
    stats = jnp.concatenate([lse, dd, jnp.zeros((3, 4, ROWS), F)], axis=1)
    stats = stats.reshape(3, 8, blocks, 432).transpose(0, 2, 1, 3).reshape(3 * blocks, 8, 432)
    dq, dk, dv = attend_back(qkv, q_marks, k_marks, da, stats)
    dx0, g_qkv, g_one = qkv_back(x0, dx1, dq, dk, dv, rows, dec[3], vec_one)
    grad_dec = jnp.concatenate(
        [
            g_one[3, :DD], g_one[0, :DD], g_one[1, :DD], g_qkv.reshape(-1),
            g_one[2, :DD], g_one[2, 2 * DD :], g_out.reshape(-1), g_two[0, :DD],
            g_two[1, :DD], g_two[2, :DD], g_up.reshape(-1), g_two[3],
            g_down.reshape(-1), g_two[4, :DD], g_two[5, :DD], g_two[6, :DD],
            g_head.reshape(-1), g_two[7],
        ]
    )
    grad_dec = jnp.pad(grad_dec, (0, dec_full.shape[0] - grad_dec.shape[0]))
    piece_dec = scatter_grads(grad_dec, links)

    d_latent = dx0[jnp.minimum(visible, ROWS - 1)] * slot_live[:, None]
    grad_enc = jnp.concatenate([g.reshape(-1) for g in pull(d_latent)[0]])
    grad_enc = jnp.pad(grad_enc, (0, enc_full.shape[0] - grad_enc.shape[0]))
    piece_enc = scatter_grads(grad_enc, links)

    squares = jnp.sum(piece_enc * piece_enc) + jnp.sum(piece_dec * piece_dec)
    grad_norm = jnp.sqrt(links.add_all(squares, links.bits()))
    clip_scale = jnp.minimum(1.0, clip_norm / (grad_norm + 1e-06))
    grad_enc = join_shard(piece_enc, params_enc.shape[0], links)
    grad_dec = join_shard(piece_dec, params_dec.shape[0], links)
    enc_one, enc_two, enc_new = adamw_update(params_enc, grad_enc, m_enc, v_enc, clip_scale)
    dec_one, dec_two, dec_new = adamw_update(params_dec, grad_dec, m_dec, v_dec, clip_scale)
    return (loss_sum, masked_count, grad_norm, enc_one, enc_two, enc_new, dec_one, dec_two, dec_new)


def solution(mesh):
    placed = (P(AXES, None),) * 4 + (P("wide"),) * 6
    return jax.shard_map(
        functools.partial(body, Links(mesh)),
        mesh=mesh,
        in_specs=placed,
        out_specs=(P(), P(), P()) + (P("wide"),) * 6,
        check_vma=False,
    )
```

time: 4710 us -> 1720 us (0.37)
  waiting for transfers between devices: 2070 us -> 357 us
  other arithmetic: 1130 us -> 152 us
  matrix products: 956 us -> 69 us
  Pallas kernels: 0 us -> 324 us
  local copies, waits for them, and re-layouts: 452 us -> 704 us
  starting transfers between devices: 0.25 us -> 81.5 us
  blocking collectives: 61.6 us -> 0 us
    unnamed x8 -> x0, waiting for transfers between devices: 1400 us -> none
    dot_general x63 -> x23, matrix products: 794 us -> 69 us  [the longest x17 64.2 us: product(): return jnp.dot(left, right, preferred_element_type=F)]
    all_gather x4 -> x0, waiting for transfers between devices: 670 us -> none  [the longest x1 616 us: body(): lax.all_gather(params_enc.astype(jnp.bfloat16), 'wide', axis=0, tiled=True)]
    ppermute x0 -> x59, waiting for transfers between devices: none -> 357 us  [swap(): return lax.ppermute(value, AXES, pairs)]
    pallas_call x0 -> x5, Pallas kernels: none -> 324 us  [the longest x1 135 us: attend_back(): pl.pallas_call(functools.partial(attend_back_kernel, kc), grid=(3, nq), i...]
    all_gather x1 -> x0, other arithmetic: 309 us -> none  [body(): lax.all_gather(params_enc.astype(jnp.bfloat16), 'wide', axis=0, tiled=True)]
    reduce_sum x19 -> x9, other arithmetic: 295 us -> 9.41 us  [the longest x2 3.79 us: encode(): soft = jnp.exp(scores - jnp.max(scores, axis=-1, keepdims=True))]
    add_any x2 -> x0, other arithmetic: 202 us -> none  [unpack(): pieces.append(vector[offset:offset + length].reshape(extent))]
  transfers between devices with their start and end apart: 6 -> 59, of which waited for: 6 -> 35; matrix products, arithmetic and copies ran while one was open for 3% -> 16% of each run, Pallas kernels for 0% -> 0%
where the time goes in v1:
time: 1720 us; the launch traced here: 1710 us
  local copies, waits for them, and re-layouts  704 us (41%)
  waiting for transfers between devices  357 us (21%)
  Pallas kernels  324 us (19%)
  other arithmetic  152 us (9%)
  starting transfers between devices  81.5 us (5%)
  matrix products  69 us (4%)
  between operations  17.8 us (1%)
    ppermute x59, waiting for transfers between devices, swap(): return lax.ppermute(value, AXES, pairs)  357 us
    unnamed x317, local copies, waits for them, and re-layouts  260 us
    pallas_call x1, Pallas kernels, attend_back(): pl.pallas_call(functools.partial(attend_back_kernel, kc), grid=(3, nq), i...  135 us
    slice x8, local copies, waits for them, and re-layouts, unpack(): pieces.append(vector[offset:offset + length].reshape(extent))  123 us
    pallas_call x1, Pallas kernels, attend_forward(): pl.pallas_call(attend_kernel, grid=(3, ROWS // bq), in_specs=[pl.BlockSpe...  97.2 us
    ppermute x59, starting transfers between devices, swap(): return lax.ppermute(value, AXES, pairs)  81.5 us
    pallas_call x1, Pallas kernels, mlp_both(): pl.pallas_call(mlp_kernel, grid=(ROWS // bm,), in_specs=[part(DD), part(D...  66.1 us
    dot_general x17, matrix products, product(): return jnp.dot(left, right, preferred_element_type=F)  64.2 us
  transfers between devices with their start and end apart: 59, of which 35 were waited for; matrix products, arithmetic and copies ran while one was open for 16% of the time, Pallas kernels for 0%

profile of v1, /device:TPU:0, one launch (start us, length us, event | category | flops | bytes accessed | tf_op | source)
XLA Modules:
  0.0 1705.3 jit_solution(14051551340544639178)
XLA Ops:
  29.5 11.1 multiply_sine_fusion
  98.9 16.9 collective-permute-done.12
  141.4 26.2 %collective-permute-done.13 = bf16[2,2,2,1056,128]{4,3,2,1,0:T(8,128)(2,1)} collective-permute-done((bf16[2,2,2,1056,128]{4,3,2,1,0:T(8,128)(2,1)S(1)}, bf16[2,2,2,1056,128]{4,3,2,1,0:T(8,128)(2,1)}, u32[]{:S(2)}, u32[]{:S(2)}) %collective-permute-start.13) | collective-permute-done | bytes 2162720 | tf_op jit(solution)/shard_map/ppermute | solution.py:449
  217.8 19.2 %reshape.504 = bf16[8,1081344]{1,0:T(8,128)(2,1)} reshape(bf16[2,2,2,2,2,2112,128]{6,5,4,3,2,1,0:T(8,128)(2,1)} %maximum_maximum_fusion) | data formatting | bytes 34603008 | tf_op jit(solution)/shard_map/reshape | solution.py:496
  237.0 12.4 slice.334
  249.4 37.8 %reshape.505 = bf16[8564736]{0:T(1024)(128)(2,1)} reshape(bf16[8,1070592]{1,0:T(8,128)(2,1)} %slice.334) | data formatting | bytes 34258944 | tf_op jit(solution)/shard_map/reshape | solution.py:497
  287.2 38.3 %slice.262 = bf16[11152,768]{1,0:T(8,128)(2,1)} reshape(bf16[8,1070592]{1,0:T(8,128)(2,1)} %slice.334) | data formatting | bytes 34258944 | tf_op jit(solution)/shard_map/slice | solution.py:70
  330.6 37.5 %slice.277 = bf16[2788,3072]{1,0:T(8,128)(2,1)} reshape(bf16[8,1070592]{1,0:T(8,128)(2,1)} %slice.334) | data formatting | bytes 34258944 | tf_op jit(solution)/shard_map/slice | solution.py:70
  369.4 37.8 %slice.284 = bf16[22304,384]{1,0:T(8,128)(2,1)} reshape(bf16[8,1070592]{1,0:T(8,128)(2,1)} %slice.334) | data formatting | bytes 34258944 | tf_op jit(solution)/shard_map/slice | solution.py:70
  431.3 11.9 multiply_convert_fusion
  466.7 97.2 %dec_attend.1 = (bf16[2592,384]{1,0:T(8,128)(2,1)}, f32[3,2592,128]{2,1,0:T(8,128)}) custom-call(bf16[2592,1152]{1,0:T(8,128)(2,1)} %dec_qkv.1.q_ref.k_ref.v_ref, bf16[2592,1152]{1,0:T(8,128)(2,1)} %dec_qkv.1.q_ref.k_ref.v_ref, bf16[2592,1152]{1,0:T(8,128)(2,1)} %dec_qkv.1.q_ref.k_ref.v_ref, bf16[2592,128]{1,0:T(8,128)(2,1)} %compare_convert_fusion.qf_ref, ...), custom_call_target="tpu_custom_call" | custom-call | tf_op jit(solution)/shard_map/dec_attend/pallas_call | solution.py:212
  563.9 66.1 %dec_mlp.1 = (bf16[2592,384]{1,0:T(8,128)(2,1)}, f32[2592,384]{1,0:T(8,128)}, f32[2592,128]{1,0:T(8,128)}, f32[384,384]{1,0:T(8,128)}, f32[384,1536]{1,0:T(8,128...) custom-call(f32[2592,384]{1,0:T(8,128)} %scatter_fusion, ...), custom_call_target="tpu_custom_call" | custom-call | tf_op jit(solution)/shard_map/dec_mlp/pallas_call | solution.py:368
  647.1 135.0 %dec_attend_back.1 = (bf16[2592,384]{1,0:T(8,128)(2,1)}, bf16[2592,384]{1,0:T(8,128)(2,1)}, bf16[2592,384]{1,0:T(8,128)(2,1)}) custom-call(bf16[2592,1152]{1,0:T(8,128)(2,1)} %dec_qkv.1.q_ref.k_ref.v_ref, bf16[2592,1152]{1,0:T(8,128)(2,1)} %dec_qkv.1.q_ref.k_ref.v_ref, bf16[2592,1152]{1,0:T(8,128)(2,1)} %dec_qkv.1.q_ref.k_ref.v_ref, ...), custom_call_target="tpu_custom_call" | custom-call | tf_op jit(solution)/shard_map/dec_attend_back/pallas_call | solution.py:284
  782.2 15.8 dec_qkv_back.1
  913.8 61.1 %dynamic-update-slice.22 = f32[8563968]{0:T(1024)} dynamic-update-slice(f32[8563968]{0:T(1024)} %constant_dynamic-update-slice_fusion.10, f32[1769472]{0:T(1024)} %reshape.520, s32[]{} %constant.383) | dynamic-update-slice | bytes 14155780
  990.9 20.3 %dynamic-update-slice.25 = f32[8563968]{0:T(1024)} dynamic-update-slice(f32[8563968]{0:T(1024)} %slice_dynamic-update-slice_fusion, f32[589824]{0:T(1024)S(1)} %copy-done.28, s32[]{} %constant.386) | dynamic-update-slice | bytes 4718596
  1043.5 26.1 %pad.85 = f32[8564736]{0:T(1024)} pad(f32[8563968]{0:T(1024)} %dynamic-update-slice.35, f32[]{:T(128)} %constant.243.clone.1), padding=0_768 | pad | bytes 68514816 | tf_op jit(solution)/shard_map/jit(_pad)/pad | solution.py:592
  1069.6 33.3 %reshape.526 = f32[8,1070592]{1,0:T(8,128)} reshape(f32[8564736]{0:T(1024)} %pad.85) | data formatting | bytes 68517888 | tf_op jit(solution)/shard_map/reshape | solution.py:503
  1102.8 12.7 pad_bitcast_fusion
  1115.6 18.5 %copy.227 = f32[1,8,8448,128]{3,2,1,0:T(8,128)} copy(f32[1,8,8448,128]{3,1,2,0:T(8,128)S(1)} %pad_bitcast_fusion) | data formatting | bytes 69206016
  1134.1 18.3 %fusion.94 = (f32[2,2,2,2,2,1056,128]{6,5,4,3,2,1,0:T(8,128)}, f32[2,2,2,2,2,1056,128]{6,5,4,3,2,1,0:T(8,128)S(1)}) fusion(f32[2,2,2,2,2,2112,128]{6,5,4,3,2,1,0:T(8,128)} %bitcast.315), kind=kLoop, calls=%fused_computation.376 | loop fusion | bytes 69206016 | tf_op jit(solution)/shard_map/slice | solution.py:509
  1152.4 13.6 dynamic-slice_bitcast_fusion.1
  1174.7 16.3 dynamic-update-slice.3
  1202.5 21.2 %dynamic-update-slice.12 = f32[2366592]{0:T(1024)} dynamic-update-slice(f32[2366592]{0:T(1024)} %constant_dynamic-update-slice_fusion.17, f32[589824]{0:T(1024)} %reshape.531, s32[]{} %constant.373) | dynamic-update-slice | bytes 4718596
  1227.6 20.1 %dynamic-update-slice.16 = f32[2366592]{0:T(1024)} dynamic-update-slice(f32[2366592]{0:T(1024)} %constant_dynamic-update-slice_fusion.14, f32[589824]{0:T(1024)S(1)} %copy-done.25, s32[]{} %constant.377) | dynamic-update-slice | bytes 4718596
  1331.7 96.7 %collective-permute-done.41 = f32[2,2,2,304,128]{4,3,2,1,0:T(8,128)} collective-permute-done((f32[2,2,2,304,128]{4,3,2,1,0:T(8,128)}, f32[2,2,2,304,128]{4,3,2,1,0:T(8,128)}, u32[]{:S(2)}, u32[]{:S(2)}) %collective-permute-start.41) | collective-permute-done | bytes 1245216 | tf_op jit(solution)/shard_map/ppermute | solution.py:449
  1431.9 13.4 collective-permute-done.46
  1470.6 12.6 collective-permute-done.43
  1492.2 19.7 %collective-permute-done.32 = f32[2,2,1056,128]{3,2,1,0:T(8,128)S(1)} collective-permute-done((f32[2,2,1056,128]{3,2,1,0:T(8,128)S(1)}, f32[2,2,1056,128]{3,2,1,0:T(8,128)S(1)}, u32[]{:S(2)}, u32[]{:S(2)}) %collective-permute-start.32) | collective-permute-done | bytes 2162720 | tf_op jit(solution)/shard_map/ppermute | solution.py:449
  1519.7 64.8 %collective-permute-done.33 = f32[2,1056,128]{2,1,0:T(8,128)S(1)} collective-permute-done((f32[2,1056,128]{2,1,0:T(8,128)S(1)}, f32[2,1056,128]{2,1,0:T(8,128)S(1)}, u32[]{:S(2)}, u32[]{:S(2)}) %collective-permute-start.33) | collective-permute-done | bytes 1081376 | tf_op jit(solution)/shard_map/ppermute | solution.py:449
  1584.8 21.9 %collective-permute-done.38 = f32[2,1056,128]{2,1,0:T(8,128)S(1)} collective-permute-done((f32[2,1056,128]{2,1,0:T(8,128)S(1)}, f32[2,1056,128]{2,1,0:T(8,128)S(1)}, u32[]{:S(2)}, u32[]{:S(2)}) %collective-permute-start.38) | collective-permute-done | bytes 1081376 | tf_op jit(solution)/shard_map/ppermute | solution.py:449
  1618.3 11.4 collective-permute-done.39
  (693 shorter events, 622.2 us)
Async XLA Ops:
  2.1 56.7 %collective-permute-start = (bf16[304,128]{1,0:T(8,128)(2,1)S(1)}, bf16[304,128]{1,0:T(8,128)(2,1)}, u32[]{:S(2)}, u32[]{:S(2)}) collective-permute-start(bf16[304,128]{1,0:T(8,128)(2,1)S(1)} %get-tuple-element.157), channel_id=1, source_target_pairs={{0,4},{1,5},{2,6},{3,7},{4,0},{5,1},{6,2},{7,3},{8,12},{9,13},{10,... | collective-permute-start | bytes 233480 | tf_op jit(solution)/shard_map/ppermute | solution.py:449
  6.3 55.2 %collective-permute-start.5 = (bf16[304,128]{1,0:T(8,128)(2,1)S(1)}, bf16[304,128]{1,0:T(8,128)(2,1)}, u32[]{:S(2)}, u32[]{:S(2)}) collective-permute-start(bf16[304,128]{1,0:T(8,128)(2,1)S(1)} %get-tuple-element.158), channel_id=1, source_target_pairs={{0,4},{1,5},{2,6},{3,7},{4,0},{5,1},{6,2},{7,3},{8,12},{9,13},{10,... | collective-permute-start | bytes 233480 | tf_op jit(solution)/shard_map/ppermute | solution.py:449
  10.3 60.6 %collective-permute-start.10 = (bf16[1056,128]{1,0:T(8,128)(2,1)}, bf16[1056,128]{1,0:T(8,128)(2,1)S(1)}, u32[]{:S(2)}, u32[]{:S(2)}) collective-permute-start(bf16[1056,128]{1,0:T(8,128)(2,1)} %get-tuple-element.133), channel_id=1, source_target_pairs={{0,4},{1,5},{2,6},{3,7},{4,0},{5,1},{6,2},{7,3},{8,12},{9,13},{10,... | collective-permute-start | bytes 811016 | tf_op jit(solution)/shard_map/ppermute | solution.py:449
  13.2 60.5 %collective-permute-start.15 = (bf16[1056,128]{1,0:T(8,128)(2,1)S(1)}, bf16[1056,128]{1,0:T(8,128)(2,1)S(1)}, u32[]{:S(2)}, u32[]{:S(2)}) collective-permute-start(bf16[1056,128]{1,0:T(8,128)(2,1)S(1)} %get-tuple-element.134), channel_id=1, source_target_pairs={{0,4},{1,5},{2,6},{3,7},{4,0},{5,1},{6,2},{7,3},{8,12},{9,13},{10,... | collective-permute-start | bytes 811016 | tf_op jit(solution)/shard_map/ppermute | solution.py:449
  73.8 23.2 %collective-permute-start.16 = (bf16[2,1056,128]{2,1,0:T(8,128)(2,1)S(1)}, bf16[2,1056,128]{2,1,0:T(8,128)(2,1)S(1)}, u32[]{:S(2)}, u32[]{:S(2)}) collective-permute-start(bf16[2,1056,128]{2,1,0:T(8,128)(2,1)S(1)} %pad_maximum_fusion.18), channel_id=1, source_target_pairs={{0,2},{1,3},{2,0},{3,1},{4,6},{5,7},{6,4},{7,5},{8,10},{9,11},{10,... | collective-permute-start | bytes 1622024 | tf_op jit(solution)/shard_map/ppermute | solution.py:449
  87.5 28.4 %collective-permute-start.12 = (bf16[2,2,1056,128]{3,2,1,0:T(8,128)(2,1)S(1)}, bf16[2,2,1056,128]{3,2,1,0:T(8,128)(2,1)S(1)}, u32[]{:S(2)}, u32[]{:S(2)}) collective-permute-start(bf16[2,2,1056,128]{3,2,1,0:T(8,128)(2,1)S(1)} %pad_maximum_fusion.11), channel_id=1, source_target_pairs={{0,1},{1,0},{2,3},{3,2},{4,5},{5,4},{6,7},{7,6},{8,9},{9,8},{10,11... | collective-permute-start | bytes 3244040 | tf_op jit(solution)/shard_map/ppermute | solution.py:449
  97.2 26.9 %collective-permute-start.17 = (bf16[2,2,1056,128]{3,2,0,1:T(8,128)(2,1)S(1)}, bf16[2,2,1056,128]{3,2,0,1:T(8,128)(2,1)S(1)}, u32[]{:S(2)}, u32[]{:S(2)}) collective-permute-start(bf16[2,2,1056,128]{3,2,0,1:T(8,128)(2,1)S(1)} %pad_maximum_fusion.12), channel_id=1, source_target_pairs={{0,16},{1,17},{2,18},{3,19},{4,20},{5,21},{6,22},{7,23},{8,24},{9,... | collective-permute-start | bytes 3244040 | tf_op jit(solution)/shard_map/ppermute | solution.py:449
  98.0 29.5 %collective-permute-start.4 = (bf16[2,2,2,2,304,128]{5,4,3,2,1,0:T(8,128)(2,1)S(1)}, bf16[2,2,2,2,304,128]{5,4,3,2,1,0:T(8,128)(2,1)S(1)}, u32[]{:S(2)}, u32[]{:S(2)}) collective-permute-start(bf16[2,2,2,2,304,128]{5,4,3,2,1,0:T(8,128)(2,1)S(1)} %pad_maximum_fusion.8), channel_id=1, source_target_pairs={{0,8},{1,9},{2,10},{3,11},{4,12},{5,13},{6,14},{7,15},{8,0},{9,1},... | collective-permute-start | bytes 3735560 | tf_op jit(solution)/shard_map/ppermute | solution.py:449
  98.4 29.3 %collective-permute-start.9 = (bf16[2,2,2,2,304,128]{5,4,3,2,1,0:T(8,128)(2,1)S(1)}, bf16[2,2,2,2,304,128]{5,4,3,2,1,0:T(8,128)(2,1)S(1)}, u32[]{:S(2)}, u32[]{:S(2)}) collective-permute-start(bf16[2,2,2,2,304,128]{5,4,3,2,1,0:T(8,128)(2,1)S(1)} %copy.222), channel_id=1, source_target_pairs={{0,8},{1,9},{2,10},{3,11},{4,12},{5,13},{6,14},{7,15},{8,0},{9,1},... | collective-permute-start | bytes 3735560 | tf_op jit(solution)/shard_map/ppermute | solution.py:449
  116.2 51.4 %collective-permute-start.13 = (bf16[2,2,2,1056,128]{4,3,2,1,0:T(8,128)(2,1)S(1)}, bf16[2,2,2,1056,128]{4,3,2,1,0:T(8,128)(2,1)}, u32[]{:S(2)}, u32[]{:S(2)}) collective-permute-start(bf16[2,2,2,1056,128]{4,3,2,1,0:T(8,128)(2,1)S(1)} %pad_maximum_fusion.5), channel_id=1, source_target_pairs={{0,16},{1,17},{2,18},{3,19},{4,20},{5,21},{6,22},{7,23},{8,24},{9,... | collective-permute-start | bytes 6488072 | tf_op jit(solution)/shard_map/ppermute | solution.py:449
  125.9 46.7 %collective-permute-start.18 = (bf16[2,2,2,1056,128]{4,3,0,1,2:T(8,128)(2,1)}, bf16[2,2,2,1056,128]{4,3,0,1,2:T(8,128)(2,1)}, u32[]{:S(2)}, u32[]{:S(2)}) collective-permute-start(bf16[2,2,2,1056,128]{4,3,0,1,2:T(8,128)(2,1)} %pad_maximum_fusion.6), channel_id=1, source_target_pairs={{0,1},{1,0},{2,3},{3,2},{4,5},{5,4},{6,7},{7,6},{8,9},{9,8},{10,11... | collective-permute-start | bytes 6488072 | tf_op jit(solution)/shard_map/ppermute | solution.py:449
  172.6 31.1 %collective-permute-start.14 = (bf16[2,2,2,2,1056,128]{5,4,3,2,1,0:T(8,128)(2,1)}, bf16[2,2,2,2,1056,128]{5,4,3,2,1,0:T(8,128)(2,1)}, u32[]{:S(2)}, u32[]{:S(2)}) collective-permute-start(bf16[2,2,2,2,1056,128]{5,4,3,2,1,0:T(8,128)(2,1)} %pad_maximum_fusion.1), channel_id=1, source_target_pairs={{0,8},{1,9},{2,10},{3,11},{4,12},{5,13},{6,14},{7,15},{8,0},{9,1},... | collective-permute-start | bytes 12976136 | tf_op jit(solution)/shard_map/ppermute | solution.py:449
  179.2 27.3 %collective-permute-start.19 = (bf16[2,2,2,2,1056,128]{5,4,3,2,1,0:T(8,128)(2,1)}, bf16[2,2,2,2,1056,128]{5,4,3,2,1,0:T(8,128)(2,1)}, u32[]{:S(2)}, u32[]{:S(2)}) collective-permute-start(bf16[2,2,2,2,1056,128]{5,4,3,2,1,0:T(8,128)(2,1)} %copy.223), channel_id=1, source_target_pairs={{0,8},{1,9},{2,10},{3,11},{4,12},{5,13},{6,14},{7,15},{8,0},{9,1},... | collective-permute-start | bytes 12976136 | tf_op jit(solution)/shard_map/ppermute | solution.py:449
  1166.0 124.8 %collective-permute-start.30 = (f32[2,2,2,2,1056,128]{5,4,3,2,1,0:T(8,128)}, f32[2,2,2,2,1056,128]{5,4,3,2,1,0:T(8,128)}, u32[]{:S(2)}, u32[]{:S(2)}) collective-permute-start(f32[2,2,2,2,1056,128]{5,4,3,2,1,0:T(8,128)} %dynamic-slice_bitcast_fusion.1), channel_id=1, source_target_pairs={{0,8},{1,9},{2,10},{3,11},{4,12},{5,13},{6,14},{7,15},{8,0},{9,1},... | collective-permute-start | bytes 25952264 | tf_op jit(solution)/shard_map/ppermute | solution.py:449
  1170.4 136.8 %collective-permute-start.35 = (f32[2,2,2,2,1056,128]{5,4,3,2,1,0:T(8,128)}, f32[2,2,2,2,1056,128]{5,4,3,2,1,0:T(8,128)}, u32[]{:S(2)}, u32[]{:S(2)}) collective-permute-start(f32[2,2,2,2,1056,128]{5,4,3,2,1,0:T(8,128)} %dynamic-slice_bitcast_fusion), channel_id=1, source_target_pairs={{0,8},{1,9},{2,10},{3,11},{4,12},{5,13},{6,14},{7,15},{8,0},{9,1},... | collective-permute-start | bytes 25952264 | tf_op jit(solution)/shard_map/ppermute | solution.py:449
  1288.7 33.9 %collective-permute-start.40 = (f32[2,2,2,2,304,128]{5,4,3,2,1,0:T(8,128)}, f32[2,2,2,2,304,128]{5,4,3,2,1,0:T(8,128)}, u32[]{:S(2)}, u32[]{:S(2)}) collective-permute-start(f32[2,2,2,2,304,128]{5,4,3,2,1,0:T(8,128)} %dynamic-slice_bitcast_fusion.5), channel_id=1, source_target_pairs={{0,8},{1,9},{2,10},{3,11},{4,12},{5,13},{6,14},{7,15},{8,0},{9,1},... | collective-permute-start | bytes 7471112 | tf_op jit(solution)/shard_map/ppermute | solution.py:449
  1290.8 36.5 %collective-permute-start.45 = (f32[2,2,2,2,304,128]{5,4,3,2,1,0:T(8,128)}, f32[2,2,2,2,304,128]{5,4,3,2,1,0:T(8,128)}, u32[]{:S(2)}, u32[]{:S(2)}) collective-permute-start(f32[2,2,2,2,304,128]{5,4,3,2,1,0:T(8,128)} %dynamic-slice_bitcast_fusion.4), channel_id=1, source_target_pairs={{0,8},{1,9},{2,10},{3,11},{4,12},{5,13},{6,14},{7,15},{8,0},{9,1},... | collective-permute-start | bytes 7471112 | tf_op jit(solution)/shard_map/ppermute | solution.py:449
  1305.7 153.8 %collective-permute-start.31 = (f32[2,2,2,1056,128]{4,3,2,1,0:T(8,128)}, f32[2,2,2,1056,128]{4,3,2,1,0:T(8,128)}, u32[]{:S(2)}, u32[]{:S(2)}) collective-permute-start(f32[2,2,2,1056,128]{4,3,2,1,0:T(8,128)} %dynamic-slice_bitcast_fusion.3), channel_id=1, source_target_pairs={{0,1},{1,0},{2,3},{3,2},{4,5},{5,4},{6,7},{7,6},{8,9},{9,8},{10,11... | collective-permute-start | bytes 12976136 | tf_op jit(solution)/shard_map/ppermute | solution.py:449
  1322.0 142.4 %collective-permute-start.36 = (f32[2,2,2,1056,128]{4,3,2,1,0:T(8,128)}, f32[2,2,2,1056,128]{4,3,2,1,0:T(8,128)}, u32[]{:S(2)}, u32[]{:S(2)}) collective-permute-start(f32[2,2,2,1056,128]{4,3,2,1,0:T(8,128)} %dynamic-slice_bitcast_fusion.2), channel_id=1, source_target_pairs={{0,16},{1,17},{2,18},{3,19},{4,20},{5,21},{6,22},{7,23},{8,24},{9,... | collective-permute-start | bytes 12976136 | tf_op jit(solution)/shard_map/ppermute | solution.py:449
  1326.7 101.7 %collective-permute-start.41 = (f32[2,2,2,304,128]{4,3,2,1,0:T(8,128)}, f32[2,2,2,304,128]{4,3,2,1,0:T(8,128)}, u32[]{:S(2)}, u32[]{:S(2)}) collective-permute-start(f32[2,2,2,304,128]{4,3,2,1,0:T(8,128)} %dynamic-slice_bitcast_fusion.9), channel_id=1, source_target_pairs={{0,1},{1,0},{2,3},{3,2},{4,5},{5,4},{6,7},{7,6},{8,9},{9,8},{10,11... | collective-permute-start | bytes 3735560 | tf_op jit(solution)/shard_map/ppermute | solution.py:449
  1330.5 114.8 %collective-permute-start.46 = (f32[2,2,2,304,128]{4,3,2,1,0:T(8,128)}, f32[2,2,2,304,128]{4,3,2,1,0:T(8,128)}, u32[]{:S(2)}, u32[]{:S(2)}) collective-permute-start(f32[2,2,2,304,128]{4,3,2,1,0:T(8,128)} %dynamic-slice_bitcast_fusion.8), channel_id=1, source_target_pairs={{0,16},{1,17},{2,18},{3,19},{4,20},{5,21},{6,22},{7,23},{8,24},{9,... | collective-permute-start | bytes 3735560 | tf_op jit(solution)/shard_map/ppermute | solution.py:449
  1431.3 26.6 %collective-permute-start.42 = (f32[2,2,304,128]{3,2,1,0:T(8,128)S(1)}, f32[2,2,304,128]{3,2,1,0:T(8,128)}, u32[]{:S(2)}, u32[]{:S(2)}) collective-permute-start(f32[2,2,304,128]{3,2,1,0:T(8,128)S(1)} %dynamic-slice_bitcast_fusion.13), channel_id=1, source_target_pairs={{0,16},{1,17},{2,18},{3,19},{4,20},{5,21},{6,22},{7,23},{8,24},{9,... | collective-permute-start | bytes 1867784 | tf_op jit(solution)/shard_map/ppermute | solution.py:449
  1459.1 24.1 %collective-permute-start.43 = (f32[2,304,128]{2,1,0:T(8,128)S(1)}, f32[2,304,128]{2,1,0:T(8,128)S(1)}, u32[]{:S(2)}, u32[]{:S(2)}) collective-permute-start(f32[2,304,128]{2,1,0:T(8,128)S(1)} %dynamic-slice_bitcast_fusion.17), channel_id=1, source_target_pairs={{0,4},{1,5},{2,6},{3,7},{4,0},{5,1},{6,2},{7,3},{8,12},{9,13},{10,... | collective-permute-start | bytes 933896 | tf_op jit(solution)/shard_map/ppermute | solution.py:449
  1463.8 48.0 %collective-permute-start.32 = (f32[2,2,1056,128]{3,2,1,0:T(8,128)S(1)}, f32[2,2,1056,128]{3,2,1,0:T(8,128)S(1)}, u32[]{:S(2)}, u32[]{:S(2)}) collective-permute-start(f32[2,2,1056,128]{3,2,1,0:T(8,128)S(1)} %dynamic-slice_bitcast_fusion.7), channel_id=1, source_target_pairs={{0,16},{1,17},{2,18},{3,19},{4,20},{5,21},{6,22},{7,23},{8,24},{9,... | collective-permute-start | bytes 6488072 | tf_op jit(solution)/shard_map/ppermute | solution.py:449
  1468.1 48.4 %collective-permute-start.37 = (f32[2,2,1056,128]{3,2,1,0:T(8,128)S(1)}, f32[2,2,1056,128]{3,2,1,0:T(8,128)S(1)}, u32[]{:S(2)}, u32[]{:S(2)}) collective-permute-start(f32[2,2,1056,128]{3,2,1,0:T(8,128)S(1)} %dynamic-slice_bitcast_fusion.6), channel_id=1, source_target_pairs={{0,1},{1,0},{2,3},{3,2},{4,5},{5,4},{6,7},{7,6},{8,9},{9,8},{10,11... | collective-permute-start | bytes 6488072 | tf_op jit(solution)/shard_map/ppermute | solution.py:449
  1488.9 29.2 %collective-permute-start.49 = (f32[304,128]{1,0:T(8,128)S(1)}, f32[304,128]{1,0:T(8,128)S(1)}, u32[]{:S(2)}, u32[]{:S(2)}) collective-permute-start(f32[304,128]{1,0:T(8,128)S(1)} %dynamic-slice_bitcast_fusion.20), channel_id=1, source_target_pairs={{0,2},{1,3},{2,0},{3,1},{4,6},{5,7},{6,4},{7,5},{8,10},{9,11},{10,... | collective-permute-start | bytes 466952 | tf_op jit(solution)/shard_map/ppermute | solution.py:449
  1512.2 72.4 %collective-permute-start.33 = (f32[2,1056,128]{2,1,0:T(8,128)S(1)}, f32[2,1056,128]{2,1,0:T(8,128)S(1)}, u32[]{:S(2)}, u32[]{:S(2)}) collective-permute-start(f32[2,1056,128]{2,1,0:T(8,128)S(1)} %dynamic-slice_bitcast_fusion.11), channel_id=1, source_target_pairs={{0,4},{1,5},{2,6},{3,7},{4,0},{5,1},{6,2},{7,3},{8,12},{9,13},{10,... | collective-permute-start | bytes 3244040 | tf_op jit(solution)/shard_map/ppermute | solution.py:449
  1516.8 89.9 %collective-permute-start.38 = (f32[2,1056,128]{2,1,0:T(8,128)S(1)}, f32[2,1056,128]{2,1,0:T(8,128)S(1)}, u32[]{:S(2)}, u32[]{:S(2)}) collective-permute-start(f32[2,1056,128]{2,1,0:T(8,128)S(1)} %dynamic-slice_bitcast_fusion.10), channel_id=1, source_target_pairs={{0,4},{1,5},{2,6},{3,7},{4,0},{5,1},{6,2},{7,3},{8,12},{9,13},{10,... | collective-permute-start | bytes 3244040 | tf_op jit(solution)/shard_map/ppermute | solution.py:449
  1518.2 89.3 %collective-permute-start.57 = (f32[608,128]{1,0:T(8,128)S(1)}, f32[608,128]{1,0:T(8,128)S(1)}, u32[]{:S(2)}, u32[]{:S(2)}) collective-permute-start(f32[608,128]{1,0:T(8,128)S(1)} %pad_maximum_fusion.21), channel_id=1, source_target_pairs={{0,16},{1,17},{2,18},{3,19},{4,20},{5,21},{6,22},{7,23},{8,24},{9,... | collective-permute-start | bytes 933896 | tf_op jit(solution)/shard_map/ppermute | solution.py:449
  1584.7 33.5 %collective-permute-start.34 = (f32[1056,128]{1,0:T(8,128)S(1)}, f32[1056,128]{1,0:T(8,128)S(1)}, u32[]{:S(2)}, u32[]{:S(2)}) collective-permute-start(f32[1056,128]{1,0:T(8,128)S(1)} %dynamic-slice_bitcast_fusion.15), channel_id=1, source_target_pairs={{0,2},{1,3},{2,0},{3,1},{4,6},{5,7},{6,4},{7,5},{8,10},{9,11},{10,... | collective-permute-start | bytes 1622024 | tf_op jit(solution)/shard_map/ppermute | solution.py:449
  1630.9 31.1 %collective-permute-start.55 = (f32[2112,128]{1,0:T(8,128)}, f32[2112,128]{1,0:T(8,128)}, u32[]{:S(2)}, u32[]{:S(2)}) collective-permute-start(f32[2112,128]{1,0:T(8,128)} %pad_maximum_fusion.13), channel_id=1, source_target_pairs={{0,16},{1,17},{2,18},{3,19},{4,20},{5,21},{6,22},{7,23},{8,24},{9,... | collective-permute-start | bytes 3244040 | tf_op jit(solution)/shard_map/ppermute | solution.py:449
  1631.5 28.0 %collective-permute-start.58 = (f32[2,608,128]{2,1,0:T(8,128)S(1)}, f32[2,608,128]{2,1,0:T(8,128)}, u32[]{:S(2)}, u32[]{:S(2)}) collective-permute-start(f32[2,608,128]{2,1,0:T(8,128)S(1)} %pad_maximum_fusion.16), channel_id=1, source_target_pairs={{0,8},{1,9},{2,10},{3,11},{4,12},{5,13},{6,14},{7,15},{8,0},{9,1},... | collective-permute-start | bytes 1867784 | tf_op jit(solution)/shard_map/ppermute | solution.py:449
  (165 other events, 2346.8 us)

commit v2 on v1

--- a/solution.py
+++ b/solution.py
@@ -60,16 +60,6 @@
 
 def product_sum(form, left, right):
     return jnp.einsum(form, left, right, preferred_element_type=F)
-
-
-def unpack(vector, extents):
-    pieces = []
-    offset = 0
-    for extent in extents:
-        length = math.prod(extent)
-        pieces.append(vector[offset : offset + length].reshape(extent))
-        offset = offset + length
-    return pieces
 
 
 ENC_SHAPES = [
@@ -429,6 +419,202 @@
     return jnp.stack(rows)
 
 
+def table(shapes):
+    out, row = [], 0
+    for s in shapes:
+        m, c = (s[0], s[1] // 128) if len(s) == 2 else (1, s[0] // 128)
+        out.append((row, m, c))
+        row += m * c
+    return out
+
+def job_rows(m, c, most=2304):
+    return max(n for n in range(16, m + 1, 16) if m % n == 0 and n * c % 16 == 0 and n * c <= most)
+
+def unpack_kernel(pieces, width, flat, *refs):
+    mats = [p for p in pieces if p[1] > 1]
+    outs, vec_ref = refs[: len(mats)], refs[len(mats)]
+    buf, lin, in_sem, out_sem = refs[len(mats) + 1 : len(mats) + 5]
+    stages = refs[len(mats) + 5 :]
+    vbuf = buf
+    vec_ref[...] = jnp.zeros_like(vec_ref)
+    v = 0
+    for row, m, c in pieces:
+        if m > 1:
+            continue
+        start = row // 16 * 16
+        size = -(-(row - start + c) // 16) * 16
+        copy = pltpu.make_async_copy(flat.at[pl.ds(start, size)], buf.at[0, pl.ds(0, size)], in_sem.at[0])
+        copy.start()
+        copy.wait()
+        lin[pl.ds(0, size), :] = buf[0, pl.ds(0, size), :].astype(F)
+        for j in range(c):
+            vec_ref[v : v + 1, j * 128 : (j + 1) * 128] = lin[pl.ds(row - start + j, 1), :]
+        v += 1
+    for k, (row, m, c) in enumerate(mats):
+        n = job_rows(m, c)
+        size = n * c
+        start = row // 16 * 16
+        delta = row - start
+        reach = -(-(delta + size) // 16) * 16
+        jobs = m // n
+        stage, out = stages[k], outs[k]
+
+        def load(j, slot):
+            at = pl.multiple_of(start + j * size, 16)
+            return pltpu.make_async_copy(flat.at[pl.ds(at, reach)], buf.at[slot, pl.ds(0, reach)], in_sem.at[slot])
+
+        def store(j, slot):
+            return pltpu.make_async_copy(stage.at[slot], out.at[pl.ds(pl.multiple_of(j * n, 16), n)], out_sem.at[slot])
+
+        load(0, 0).start()
+
+        def job(j, carry):
+            slot = lax.rem(j, 2)
+
+            @pl.when(j + 1 < jobs)
+            def _():
+                load(j + 1, 1 - slot).start()
+
+            load(j, slot).wait()
+            lin[pl.ds(0, reach), :] = buf[slot, pl.ds(0, reach), :].astype(F)
+
+            @pl.when(j >= 2)
+            def _():
+                store(j - 2, slot).wait()
+
+            for i in range(c):
+                stage[slot, :, i * 128 : (i + 1) * 128] = lin[pl.ds(delta + i, n, stride=c), :].astype(B)
+            store(j, slot).start()
+            return carry
+
+        lax.fori_loop(0, jobs, job, 0)
+        for j in range(max(jobs - 2, 0), jobs):
+            store(j, j % 2).wait()
+
+def unpack_flat(flat, shapes, name):
+    pieces = table(shapes)
+    mats = [s for s in shapes if len(s) == 2]
+    vectors = [s for s in shapes if len(s) == 1]
+    width = max(s[0] for s in vectors)
+    count = -(-len(vectors) // 8) * 8
+    hbm = pl.BlockSpec(memory_space=pl.ANY)
+    stages = [pltpu.VMEM((2, job_rows(s[0], s[1] // 128), s[1]), B) for s in mats]
+    return pl.pallas_call(
+        functools.partial(unpack_kernel, pieces, width),
+        in_specs=[hbm],
+        out_specs=[hbm] * len(mats) + [pl.BlockSpec(memory_space=pltpu.VMEM)],
+        out_shape=[jax.ShapeDtypeStruct(s, B) for s in mats] + [jax.ShapeDtypeStruct((count, width), F)],
+        scratch_shapes=[
+            pltpu.VMEM((2, 2336, 128), B), pltpu.VMEM((2336, 128), F),
+            pltpu.SemaphoreType.DMA((2,)), pltpu.SemaphoreType.DMA((2,)),
+        ] + stages,
+        compiler_params=pltpu.CompilerParams(vmem_limit_bytes=VMEM_LIMIT),
+        name=name,
+    )(flat)
+
+def pack_kernel(pieces, shard, padded, wide, core_ref, *refs):
+    mats = [p for p in pieces if p[1] > 1]
+    ins, vec_ref = refs[: len(mats)], refs[len(mats)]
+    kept, away, top_ref = refs[len(mats) + 1 : len(mats) + 4]
+    lin, turn, in_sem, out_sem = refs[len(mats) + 4 : len(mats) + 8]
+    stages = refs[len(mats) + 8 :]
+    end = pieces[-1][0] + pieces[-1][1] * pieces[-1][2]
+    lin[pl.ds(end, lin.shape[0] - end), :] = jnp.zeros((lin.shape[0] - end, 128), F)
+    top_ref[...] = jnp.zeros_like(top_ref)
+    top = jnp.max(jnp.abs(vec_ref[...]), axis=0, keepdims=True)
+    for j in range(vec_ref.shape[1] // 128):
+        top_ref[0:1, :] = jnp.maximum(top_ref[0:1, :], top[:, j * 128 : (j + 1) * 128])
+    v = 0
+    for row, m, c in pieces:
+        if m == 1:
+            for j in range(c):
+                lin[pl.ds(row + j, 1), :] = vec_ref[v : v + 1, j * 128 : (j + 1) * 128]
+            v += 1
+    for k, (row, m, c) in enumerate(mats):
+        n = job_rows(m, c)
+        size = n * c
+        jobs = m // n
+        stage, source = stages[k], ins[k]
+
+        def load(j, slot):
+            return pltpu.make_async_copy(source.at[pl.ds(pl.multiple_of(j * n, 8), n)], stage.at[slot], in_sem.at[slot])
+
+        load(0, 0).start()
+
+        def job(j, carry):
+            slot = lax.rem(j, 2)
+
+            @pl.when(j + 1 < jobs)
+            def _():
+                load(j + 1, 1 - slot).start()
+
+            load(j, slot).wait()
+            most = top_ref[...]
+            for i in range(c):
+                value = stage[slot, :, i * 128 : (i + 1) * 128]
+                most = jnp.maximum(most, jnp.max(jnp.abs(value).reshape(-1, 8, 128), axis=0))
+                lin[pl.ds(row + i + j * size, n, stride=c), :] = value
+            top_ref[...] = most
+            return carry
+
+        lax.fori_loop(0, jobs, job, 0)
+
+    half = padded // 2
+    core = core_ref[0]
+
+    def sends(source, s, low, high):
+        return [
+            pltpu.make_async_copy(source.at[pl.ds(0, half)], low.at[s], out_sem.at[s % 2, 0]),
+            pltpu.make_async_copy(source.at[pl.ds(half, half)], high.at[s], out_sem.at[s % 2, 1]),
+        ]
+
+    def source_of(s):
+        at = s * shard
+        return lin.at[pl.ds(at, padded)] if at % 8 == 0 else turn.at[s % 2]
+
+    def run(s, act):
+        @pl.when(core == 0)
+        def _():
+            for copy in sends(source_of(s), s, kept, away):
+                act(copy)
+
+        @pl.when(core == 1)
+        def _():
+            for copy in sends(source_of(s), s, away, kept):
+                act(copy)
+
+    for s in range(wide):
+        if s >= 2:
+            run(s - 2, lambda copy: copy.wait())
+        if s * shard % 8:
+            turn[s % 2] = lin[pl.ds(s * shard, padded), :]
+        run(s, lambda copy: copy.start())
+    for s in range(max(wide - 2, 0), wide):
+        run(s, lambda copy: copy.wait())
+
+def pack_grads(mats, vectors, shapes, total_rows, core, wide, padded, name):
+    pieces = table(shapes)
+    shard = total_rows // wide
+    hbm = pl.BlockSpec(memory_space=pl.ANY)
+    vmem = pl.BlockSpec(memory_space=pltpu.VMEM)
+    length = -(-((wide - 1) * shard + padded) // 8) * 8
+    stages = [pltpu.VMEM((2, job_rows(m.shape[0], m.shape[1] // 128), m.shape[1]), F) for m in mats]
+    out = jax.ShapeDtypeStruct((wide, padded // 2, 128), F)
+    kept, away, top = pl.pallas_call(
+        functools.partial(pack_kernel, pieces, shard, padded, wide),
+        in_specs=[pl.BlockSpec(memory_space=pltpu.SMEM)] + [hbm] * len(mats) + [vmem],
+        out_specs=[hbm, hbm, vmem],
+        out_shape=[out, out, jax.ShapeDtypeStruct((8, 128), F)],
+        scratch_shapes=[
+            pltpu.VMEM((length, 128), F), pltpu.VMEM((2, padded, 128), F),
+            pltpu.SemaphoreType.DMA((2,)), pltpu.SemaphoreType.DMA((2, 2)),
+        ] + stages,
+        compiler_params=pltpu.CompilerParams(vmem_limit_bytes=VMEM_LIMIT),
+        name=name,
+    )(core, *mats, vectors)
+    return kept, away, jnp.max(top)
+
+
 class Links:
     def __init__(self, mesh):
         self.narrow, self.wide = mesh.shape["narrow"], mesh.shape["wide"]
@@ -448,21 +634,31 @@
         pairs = [(i, i ^ mask) for i in range(self.narrow * self.wide)]
         return lax.ppermute(value, AXES, pairs)
 
-    def add_all(self, value, bits):
-        for bit in bits:
+    def add_all(self, value):
+        for bit in self.bits():
             value = value + self.swap(value, bit)
         return value
 
-    def scatter_sum(self, value, axes, order):
+    def max_all(self, value):
+        for bit in self.bits():
+            value = jnp.maximum(value, self.swap(value, bit))
+        return value
+
+    def scatter_sum(self, kept, other, axes, order, scale):
         axes = list(axes)
         for bit in order:
             place = axes.index(bit)
             mine = self.mine(bit)
-            away = lax.dynamic_index_in_dim(value, 1 - mine, place, keepdims=False)
-            kept = lax.dynamic_index_in_dim(value, mine, place, keepdims=False)
-            value = kept + self.swap(away, bit)
+            take = lambda value, index: lax.dynamic_index_in_dim(value, index, place, keepdims=False)
+            away = ((take(kept, 1 - mine) + take(other, 1 - mine)) * scale).astype(jnp.float16)
+            kept = take(kept, mine) + take(other, mine)
+            other = self.swap(away, bit).astype(F) * (1.0 / scale)
             axes.pop(place)
-        return value
+        return kept + other
+
+    def scale(self, top):
+        count = self.narrow * self.wide
+        return 32768.0 / (count * jnp.maximum(self.max_all(top), 1e-30))
 
     def gather(self, value, axes, order):
         have = []
@@ -493,28 +689,33 @@
     half = rows // 2
     one = links.gather(piece[:half], bits, upper + [x, y, core])
     two = links.gather(piece[half:], bits, upper + [y, x, core])
-    both = jnp.concatenate([one, two], axis=-2).reshape(links.wide, links.narrow * rows * 128)
-    return both[:, : shard.shape[0]].reshape(-1)
-
-
-def scatter_grads(flat, links):
-    rows = piece_rows(flat.shape[0], links)
-    shard = flat.shape[0] // links.wide
-    value = jnp.pad(flat.reshape(links.wide, shard), ((0, 0), (0, links.narrow * rows * 128 - shard)))
-    value = value.reshape((2,) * (links.wide_bits + links.narrow_bits) + (rows, 128))
-    bits = links.bits()
+    both = jnp.concatenate([one, two], axis=-2).reshape(links.wide, links.narrow * rows, 128)
+    return both[:, : shard.shape[0] // 128].reshape(-1, 128)
+
+
+def scatter_grads(kept, away, scale, links):
+    rows = kept.shape[1] // 2
+    y, core = ("narrow", 1), ("narrow", 0)
     x, upper = ("wide", 0), [("wide", b) for b in reversed(range(1, links.wide_bits))]
-    y, core = ("narrow", 1), ("narrow", 0)
+    axes = links.bits()[: links.wide_bits] + [y]
+    shape = (2,) * len(axes) + (rows, 128)
+    kept, other = kept.reshape(shape), links.swap(away, core).reshape(shape)
     half = rows // 2
-    one = links.scatter_sum(value[..., :half, :], bits, [core, x, y] + upper)
-    two = links.scatter_sum(value[..., half:, :], bits, [core, y, x] + upper)
+    one = links.scatter_sum(kept[..., :half, :], other[..., :half, :], axes, [x, y] + upper, scale)
+    two = links.scatter_sum(kept[..., half:, :], other[..., half:, :], axes, [y, x] + upper, scale)
     return jnp.concatenate([one, two])
 
 
+def piece_squares(piece, shard_rows, links):
+    rows = piece.shape[0]
+    part = links.mine(("narrow", 0)) * 2 + links.mine(("narrow", 1))
+    inside = part * rows + jnp.arange(rows, dtype=jnp.int32)[:, None] < shard_rows
+    return jnp.sum(jnp.where(inside, piece * piece, 0.0))
+
+
 def join_shard(piece, shard, links):
-    axes = [("narrow", b) for b in reversed(range(links.narrow_bits))]
-    whole = links.gather(piece, axes, [("narrow", 1), ("narrow", 0)])
-    return whole.reshape(-1)[:shard]
+    axes = [("narrow", 0), ("narrow", 1)]
+    return links.gather(piece, axes, [("narrow", 1), ("narrow", 0)]).reshape(-1)[:shard]
 
 
 def adamw_update(master, gradient, moment_one, moment_two, clip_scale):
@@ -535,7 +736,7 @@
     lengths = clip_lens[0]
     visible = vis_index[0]
     segment, clip_place, slot_live, shown_flag, counted = layout(lengths, visible, target.shape[0])
-    masked_count = links.add_all(jnp.sum(counted), links.bits())
+    masked_count = links.add_all(jnp.sum(counted))
     cotangent = 1.0 / masked_count
     segment, clip_place, shown_flag, counted = (
         v[:ROWS] for v in (segment, clip_place, shown_flag, counted)
@@ -547,10 +748,12 @@
     q_marks = mark.astype(B)
     k_marks = jnp.where(mark | (lane > 3), 0.0, -1e30).astype(B)
 
-    enc_full = gather_params(params_enc, links)
-    dec_full = gather_params(params_dec, links)
-    encoder = [w.astype(F) for w in unpack(enc_full, ENC_SHAPES)]
-    dec = unpack(dec_full, DEC_SHAPES)
+    *enc_mats, enc_vec = unpack_flat(gather_params(params_enc, links), ENC_SHAPES, "unpack_enc")
+    *dec_mats, dec_vec = unpack_flat(gather_params(params_dec, links), DEC_SHAPES, "unpack_dec")
+    w_qkv, w_out, w_up, w_down, w_head = dec_mats
+    encoder, mats, vecs = [], list(enc_mats), [enc_vec[i] for i in range(12)]
+    for extent in ENC_SHAPES:
+        encoder.append(mats.pop(0).astype(F) if len(extent) == 2 else vecs.pop(0)[: extent[0]])
     slot_segment, slot_place = slot_layout(lengths, visible)
     latent, pull = jax.vjp(
         lambda weights: encode(weights, vis_pixels, slot_segment, sinusoid(slot_place, D)), encoder
@@ -558,42 +761,48 @@
 
     place_rows = jnp.where(visible < ROWS, visible, ROWS)
     placed = jnp.zeros((ROWS, DD), F).at[place_rows].add(latent * slot_live[:, None], mode="drop")
-    x0 = placed + (1.0 - shown_flag)[:, None] * dec[0].astype(F)[None, :] + sinusoid(clip_place, DD)
-    bias = jnp.concatenate([dec[4], jnp.zeros_like(dec[4]), dec[5]])
-    vec_one = stack_rows([dec[1], dec[2], bias], 3 * DD)
-    vec_two = stack_rows([dec[7], dec[8], dec[9], dec[11], dec[13], dec[14], dec[15], dec[17]], DFF, 16)
-    qkv = qkv_forward(x0, dec[3], vec_one)
+    x0 = placed + (1.0 - shown_flag)[:, None] * dec_vec[0:1, :DD] + sinusoid(clip_place, DD)
+    bias = jnp.concatenate([dec_vec[3, :DD], jnp.zeros((DD,), F), dec_vec[4, :DD]])
+    vec_one = stack_rows([dec_vec[1, :DD], dec_vec[2, :DD], bias], 3 * DD)
+    vec_two = jnp.concatenate([dec_vec[5:13], jnp.zeros((8, DFF), F)])
+    qkv = qkv_forward(x0, w_qkv, vec_one)
     a, lse = attend_forward(qkv, q_marks, k_marks)
     da, dx1, dd, g_out, g_up, g_down, g_head, g_two = mlp_both(
-        x0, a, target, rows, dec[6], dec[10], dec[12], dec[16], vec_two
-    )
-    loss_sum = links.add_all(jnp.sum(g_two[8]) / PIX, links.bits())
+        x0, a, target, rows, w_out, w_up, w_down, w_head, vec_two
+    )
+    loss_sum = links.add_all(jnp.sum(g_two[8]) / PIX)
     blocks = ROWS // 432
     lse = jnp.stack([lse[:, :, 0], lse[:, :, 64]], axis=1)
     dd = dd[:, :DHEADS].T.reshape(3, 2, ROWS)
     stats = jnp.concatenate([lse, dd, jnp.zeros((3, 4, ROWS), F)], axis=1)
     stats = stats.reshape(3, 8, blocks, 432).transpose(0, 2, 1, 3).reshape(3 * blocks, 8, 432)
     dq, dk, dv = attend_back(qkv, q_marks, k_marks, da, stats)
-    dx0, g_qkv, g_one = qkv_back(x0, dx1, dq, dk, dv, rows, dec[3], vec_one)
-    grad_dec = jnp.concatenate(
-        [
-            g_one[3, :DD], g_one[0, :DD], g_one[1, :DD], g_qkv.reshape(-1),
-            g_one[2, :DD], g_one[2, 2 * DD :], g_out.reshape(-1), g_two[0, :DD],
-            g_two[1, :DD], g_two[2, :DD], g_up.reshape(-1), g_two[3],
-            g_down.reshape(-1), g_two[4, :DD], g_two[5, :DD], g_two[6, :DD],
-            g_head.reshape(-1), g_two[7],
-        ]
-    )
-    grad_dec = jnp.pad(grad_dec, (0, dec_full.shape[0] - grad_dec.shape[0]))
-    piece_dec = scatter_grads(grad_dec, links)
+    dx0, g_qkv, g_one = qkv_back(x0, dx1, dq, dk, dv, rows, w_qkv, vec_one)
+    core = (lax.axis_index("narrow") & 1).astype(jnp.int32).reshape(1)
+    one_vec = jnp.stack(
+        [g_one[3, :DD], g_one[0, :DD], g_one[1, :DD], g_one[2, :DD], g_one[2, 2 * DD :]]
+    )
+    dec_grads = jnp.concatenate([jnp.pad(one_vec, ((0, 0), (0, DFF - DD))), g_two[:8], jnp.zeros((3, DFF), F)])
+    dec_rows, enc_rows = (v.shape[0] * links.wide // 128 for v in (params_dec, params_enc))
+    dec_kept, dec_away, dec_top = pack_grads(
+        [g_qkv, g_out, g_up, g_down, g_head], dec_grads, DEC_SHAPES, dec_rows, core, links.wide,
+        links.narrow * piece_rows(dec_rows * 128, links), "pack_dec",
+    )
+    dec_scale = links.scale(dec_top)
+    piece_dec = scatter_grads(dec_kept, dec_away, dec_scale, links)
 
     d_latent = dx0[jnp.minimum(visible, ROWS - 1)] * slot_live[:, None]
-    grad_enc = jnp.concatenate([g.reshape(-1) for g in pull(d_latent)[0]])
-    grad_enc = jnp.pad(grad_enc, (0, enc_full.shape[0] - grad_enc.shape[0]))
-    piece_enc = scatter_grads(grad_enc, links)
-
-    squares = jnp.sum(piece_enc * piece_enc) + jnp.sum(piece_dec * piece_dec)
-    grad_norm = jnp.sqrt(links.add_all(squares, links.bits()))
+    grads = pull(d_latent)[0]
+    enc_grads = stack_rows([g for g in grads if g.ndim == 1], FF, 16)
+    enc_kept, enc_away, enc_top = pack_grads(
+        [g for g in grads if g.ndim == 2], enc_grads, ENC_SHAPES, enc_rows, core, links.wide,
+        links.narrow * piece_rows(enc_rows * 128, links), "pack_enc",
+    )
+    piece_enc = scatter_grads(enc_kept, enc_away, links.scale(enc_top), links)
+
+    squares = piece_squares(piece_enc, enc_rows // links.wide, links)
+    squares = squares + piece_squares(piece_dec, dec_rows // links.wide, links)
+    grad_norm = jnp.sqrt(links.add_all(squares))
     clip_scale = jnp.minimum(1.0, clip_norm / (grad_norm + 1e-06))
     grad_enc = join_shard(piece_enc, params_enc.shape[0], links)
     grad_dec = join_shard(piece_dec, params_dec.shape[0], links)

time: 1720 us -> 1170 us (0.68)
  local copies, waits for them, and re-layouts: 704 us -> 135 us
  Pallas kernels: 324 us -> 432 us
  waiting for transfers between devices: 357 us -> 273 us
  other arithmetic: 152 us -> 132 us
    unnamed x317 -> x228, local copies, waits for them, and re-layouts: 260 us -> 10.9 us
    reshape x21 -> x1, local copies, waits for them, and re-layouts: 166 us -> 20.3 us  [gather_params(): return both[:, :shard.shape[0] // 128].reshape(-1, 128)]
    slice x13, local copies, waits for them, and re-layouts: 160 us -> 50.1 us  [the longest x2 17.3 us: scatter_grads(): other[..., :half, :]]
    pallas_call x0 -> x4, Pallas kernels: none -> 108 us  [the longest x2 58.2 us: unpack_flat(): pl.pallas_call(functools.partial(unpack_kernel, pieces, width), in_specs=...]
    ppermute x59 -> x67, waiting for transfers between devices: 357 us -> 273 us  [swap(): return lax.ppermute(value, AXES, pairs)]
    squeeze x20 -> x0, local copies, waits for them, and re-layouts: 36.8 us -> none  [scatter_sum(): away = lax.dynamic_index_in_dim(value, 1 - mine, place, keepdims=False)]
    pad x2 -> x13, local copies, waits for them, and re-layouts: 34.7 us -> 0.05 us  [stack_rows(): rows = [jnp.pad(p.astype(F), (0, width - p.shape[0])) for p in pieces]]
    add x20 -> x16, other arithmetic: 37.8 us -> 16.4 us  [the longest x12 16.1 us: scatter_sum(): kept = take(kept, mine) + take(other, mine)]
  transfers between devices with their start and end apart: 59 -> 67, of which waited for: 35 -> 42; matrix products, arithmetic and copies ran while one was open for 16% -> 12% of each run, Pallas kernels for 0% -> 3%
where the time goes in v2:
time: 1170 us; the launch traced here: 1150 us
  Pallas kernels  432 us (37%)
  waiting for transfers between devices  273 us (23%)
  local copies, waits for them, and re-layouts  135 us (12%)
  other arithmetic  132 us (11%)
  starting transfers between devices  92.7 us (8%)
  matrix products  62.1 us (5%)
  between operations  26.4 us (2%)
    ppermute x67, waiting for transfers between devices, swap(): return lax.ppermute(value, AXES, pairs)  273 us
    pallas_call x1, Pallas kernels, attend_back(): pl.pallas_call(functools.partial(attend_back_kernel, kc), grid=(3, nq), i...  135 us
    pallas_call x1, Pallas kernels, attend_forward(): pl.pallas_call(attend_kernel, grid=(3, ROWS // bq), in_specs=[pl.BlockSpe...  97.2 us
    ppermute x67, starting transfers between devices, swap(): return lax.ppermute(value, AXES, pairs)  92.7 us
    pallas_call x1, Pallas kernels, mlp_both(): pl.pallas_call(mlp_kernel, grid=(ROWS // bm,), in_specs=[part(DD), part(D...  66 us
    pallas_call x2, Pallas kernels, unpack_flat(): pl.pallas_call(functools.partial(unpack_kernel, pieces, width), in_specs=...  58.2 us
    dot_general x17, matrix products, product(): return jnp.dot(left, right, preferred_element_type=F)  57.5 us
    pallas_call x2, Pallas kernels, pack_grads(): pl.pallas_call(functools.partial(pack_kernel, pieces, shard, padded, wide...  50.1 us
  transfers between devices with their start and end apart: 67, of which 42 were waited for; matrix products, arithmetic and copies ran while one was open for 12% of the time, Pallas kernels for 3%

profile of v2, /device:TPU:0, one launch (start us, length us, event | category | flops | bytes accessed | tf_op | source)
XLA Modules:
  0.0 1153.1 jit_solution(401136088733033105)
XLA Ops:
  27.3 11.1 multiply_sine_fusion
  40.8 9.4 collective-permute-done.1
  57.4 13.0 %collective-permute-done.11 = bf16[2,1056,128]{2,1,0:T(8,128)(2,1)S(1)} collective-permute-done((bf16[2,1056,128]{2,1,0:T(8,128)(2,1)S(1)}, bf16[2,1056,128]{2,1,0:T(8,128)(2,1)S(1)}, u32[]{:S(2)}, u32[]{:S(2)}) %collective-permute-start.11) | collective-permute-done | bytes 540704 | tf_op jit(solution)/shard_map/ppermute | solution.py:635
  72.8 7.9 collective-permute-done.16
  81.5 12.5 %collective-permute-done.12 = bf16[2,2,1056,128]{3,2,1,0:T(8,128)(2,1)S(1)} collective-permute-done((bf16[2,2,1056,128]{3,2,1,0:T(8,128)(2,1)S(1)}, bf16[2,2,1056,128]{3,2,1,0:T(8,128)(2,1)S(1)}, u32[]{:S(2)}, u32[]{:S(2)}) %collective-permute-start.12) | collective-permute-done | bytes 1081376 | tf_op jit(solution)/shard_map/ppermute | solution.py:635
  96.6 15.2 %collective-permute-done.17 = bf16[2,2,1056,128]{3,2,0,1:T(8,128)(2,1)S(1)} collective-permute-done((bf16[2,2,1056,128]{3,2,0,1:T(8,128)(2,1)S(1)}, bf16[2,2,1056,128]{3,2,0,1:T(8,128)(2,1)S(1)}, u32[]{:S(2)}, u32[]{:S(2)}) %collective-permute-start.17) | collective-permute-done | bytes 1081376 | tf_op jit(solution)/shard_map/ppermute | solution.py:635
  115.7 39.3 %collective-permute-done.13 = bf16[2,2,2,1056,128]{4,3,2,1,0:T(8,128)(2,1)S(1)} collective-permute-done((bf16[2,2,2,1056,128]{4,3,2,1,0:T(8,128)(2,1)S(1)}, bf16[2,2,2,1056,128]{4,3,2,1,0:T(8,128)(2,1)S(1)}, u32[]{:S(2)}, u32[]{:S(2)}) %collective-permute-start.13) | collective-permute-done | bytes 2162720 | tf_op jit(solution)/shard_map/ppermute | solution.py:635
  194.0 20.4 %unpack_dec.1 = (bf16[384,1152]{1,0:T(8,128)(2,1)}, bf16[384,384]{1,0:T(8,128)(2,1)}, bf16[384,1536]{1,0:T(8,128)(2,1)}, bf16[1536,384]{1,0:T(8,128)(2,1)}, bf16...) custom-call(bf16[18496,128]{1,0:T(8,128)(2,1)} %bitcast.415), custom_call_target="tpu_custom_call" | custom-call | tf_op jit(solution)/shard_map/unpack_dec/pallas_call | solution.py:502
  237.7 20.3 %reshape.536.flat = bf16[66912,128]{1,0:T(8,128)(2,1)} reshape(bf16[8,8364,128]{2,1,0:T(8,128)(2,1)} %slice.269) | data formatting | bytes 34258944 | tf_op jit(solution)/shard_map/reshape | solution.py:693
  258.1 37.8 %unpack_enc.1 = (bf16[1536,768]{1,0:T(8,128)(2,1)}, bf16[768,2304]{1,0:T(8,128)(2,1)}, bf16[768,768]{1,0:T(8,128)(2,1)}, bf16[768,3072]{1,0:T(8,128)(2,1)}, bf16...) custom-call(bf16[66912,128]{1,0:T(8,128)(2,1)} %reshape.536.flat), custom_call_target="tpu_custom_call" | custom-call | tf_op jit(solution)/shard_map/unpack_enc/pallas_call | solution.py:502
  314.6 11.8 %multiply_convert_fusion.1 = (bf16[256,3072]{1,0:T(8,128)(2,1)S(1)}, f32[256,3072]{1,0:T(8,128)}, f32[256,3072]{1,0:T(8,128)}) fusion(f32[3072]{0:T(1024)S(1)} %bitcast.461, bf16[256,768]{0,1:T(8,128)(2,1)S(1)} %add_convert_fusion.2, bf16[768,3072]{1,0:T(8,128)(2,1)} %get-tuple-element.49), kind=kOutput, calls=%fused_computation.42 | convolution fusion | flops 1259864064 | bytes 12988416 | tf_op jit(solution)/shard_map/jvp()/dot_general | solution.py:58
  338.1 9.3 dec_qkv.1.q_ref.k_ref.v_ref
  347.4 97.2 %dec_attend.1 = (bf16[2592,384]{1,0:T(8,128)(2,1)}, f32[3,2592,128]{2,1,0:T(8,128)}) custom-call(bf16[2592,1152]{1,0:T(8,128)(2,1)} %dec_qkv.1.q_ref.k_ref.v_ref, bf16[2592,1152]{1,0:T(8,128)(2,1)} %dec_qkv.1.q_ref.k_ref.v_ref, bf16[2592,1152]{1,0:T(8,128)(2,1)} %dec_qkv.1.q_ref.k_ref.v_ref, bf16[2592,128]{1,0:T(8,128)(2,1)} %compare_convert_fusion.qf_ref, ...), custom_call_target="tpu_custom_call" | custom-call | tf_op jit(solution)/shard_map/dec_attend/pallas_call | solution.py:202
  444.6 7.2 slice_reduce_fusion.1
  454.9 66.0 %dec_mlp.1 = (bf16[2592,384]{1,0:T(8,128)(2,1)}, f32[2592,384]{1,0:T(8,128)}, f32[2592,128]{1,0:T(8,128)}, f32[384,384]{1,0:T(8,128)}, f32[384,1536]{1,0:T(8,128...) custom-call(f32[2592,384]{1,0:T(8,128)} %scatter_fusion, ...), custom_call_target="tpu_custom_call" | custom-call | tf_op jit(solution)/shard_map/dec_mlp/pallas_call | solution.py:358
  529.9 135.4 %dec_attend_back.1 = (bf16[2592,384]{1,0:T(8,128)(2,1)}, bf16[2592,384]{1,0:T(8,128)(2,1)}, bf16[2592,384]{1,0:T(8,128)(2,1)}) custom-call(bf16[2592,1152]{1,0:T(8,128)(2,1)} %dec_qkv.1.q_ref.k_ref.v_ref, bf16[2592,1152]{1,0:T(8,128)(2,1)} %dec_qkv.1.q_ref.k_ref.v_ref, bf16[2592,1152]{1,0:T(8,128)(2,1)} %dec_qkv.1.q_ref.k_ref.v_ref, ...), custom_call_target="tpu_custom_call" | custom-call | tf_op jit(solution)/shard_map/dec_attend_back/pallas_call | solution.py:274
  665.3 15.6 %dec_qkv_back.1 = (f32[2592,384]{1,0:T(8,128)}, f32[384,1152]{1,0:T(8,128)}, f32[8,1152]{1,0:T(8,128)}) custom-call(f32[2592,384]{1,0:T(8,128)} %scatter_fusion, f32[2592,384]{1,0:T(8,128)} %get-tuple-element.59.dx_ref, bf16[2592,384]{1,0:T(8,128)(2,1)} %get-tuple-element.63.dq_ref, bf16[2592,384]{1,0:T(8,128)(2,1)} %get-tuple-element.64.dk_ref, ...), custom_call_target="tpu_custom_call" | custom-call | tf_op jit(solution)/shard_map/dec_qkv_back/pallas_call | solution.py:401
  697.2 7.2 fusion.116
  748.3 36.0 %pack_enc.1 = (f32[8,4224,128]{2,1,0:T(8,128)}, f32[8,4224,128]{2,1,0:T(8,128)}, f32[8,128]{1,0:T(8,128)}) custom-call(s32[1]{0:T(128)} %bitcast.73.core_ref, f32[1536,768]{1,0:T(8,128)} %convolution_bitcast_fusion.refs_0_, f32[768,2304]{1,0:T(8,128)} %fusion.120.refs_1_, f32[768,768]{1,0:T(8,128)} %fusion.121.refs_2_, f32[768,3072]{1,0:T(8,128)} %fusion.122.refs_3_, ...), custom_call_target="tpu_custom_call" | custom-call | tf_op jit(solution)/shard_map/pack_enc/pallas_call | solution.py:603
  786.9 14.0 %pack_dec.1 = (f32[8,1216,128]{2,1,0:T(8,128)}, f32[8,1216,128]{2,1,0:T(8,128)}, f32[8,128]{1,0:T(8,128)}) custom-call(s32[1]{0:T(128)} %bitcast.73.core_ref, f32[384,1152]{1,0:T(8,128)} %get-tuple-element.70.refs_0_, f32[384,384]{1,0:T(8,128)} %get-tuple-element.71.refs_1_, f32[384,1536]{1,0:T(8,128)} %get-tuple-element.72.refs_2_, ...), custom_call_target="tpu_custom_call" | custom-call | tf_op jit(solution)/shard_map/pack_dec/pallas_call | solution.py:603
  830.3 12.6 %fusion.104 = (f32[2,2,2,2,1056,128]{5,4,3,2,1,0:T(8,128)}, f32[2,2,2,2,1056,128]{5,4,3,2,1,0:T(8,128)}) fusion(f32[2,2,2,2,2112,128]{5,4,3,2,1,0:T(8,128)} %bitcast.416), kind=kLoop, calls=%fused_computation.372 | loop fusion | bytes 34603008 | tf_op jit(solution)/shard_map/slice | solution.py:704
  869.5 13.3 %collective-permute-done.54 = f16[2,2,2,304,128]{4,3,2,1,0:T(8,128)(2,1)S(1)} collective-permute-done((f16[2,2,2,304,128]{4,3,2,1,0:T(8,128)(2,1)S(1)}, f16[2,2,2,304,128]{4,3,2,1,0:T(8,128)(2,1)S(1)}, u32[]{:S(2)}, u32[]{:S(2)}) %collective-permute-start.54) | collective-permute-done | bytes 622624 | tf_op jit(solution)/shard_map/ppermute | solution.py:635
  893.9 9.0 collective-permute-done.52
  905.4 13.1 %fusion.105 = (f32[2,2,2,2,1056,128]{5,4,3,2,1,0:T(8,128)}, f32[2,2,2,2,1056,128]{5,4,3,2,1,0:T(8,128)}) fusion(f32[2,2,2,2,2112,128]{5,4,3,2,1,0:T(8,128)} %bitcast.101), kind=kLoop, calls=%fused_computation.373 | loop fusion | bytes 34603008 | tf_op jit(solution)/shard_map/slice | solution.py:704
  919.8 9.7 constant_dynamic-slice_fusion.6
  941.6 7.6 dynamic-slice_add_fusion
  954.7 28.5 %collective-permute-done.36 = f16[2,2,2,1056,128]{4,3,1,0,2:T(8,128)(2,1)} collective-permute-done((f16[2,2,2,1056,128]{4,3,1,0,2:T(8,128)(2,1)}, f16[2,2,2,1056,128]{4,3,1,0,2:T(8,128)(2,1)}, u32[]{:S(2)}, u32[]{:S(2)}) %collective-permute-start.36) | collective-permute-done | bytes 2162720 | tf_op jit(solution)/shard_map/ppermute | solution.py:635
  986.3 13.1 %collective-permute-done.40 = f16[2,2,2,1056,128]{4,3,2,1,0:T(8,128)(2,1)S(1)} collective-permute-done((f16[2,2,2,1056,128]{4,3,2,1,0:T(8,128)(2,1)}, f16[2,2,2,1056,128]{4,3,2,1,0:T(8,128)(2,1)S(1)}, u32[]{:S(2)}, u32[]{:S(2)}) %collective-permute-start.40) | collective-permute-done | bytes 2162720 | tf_op jit(solution)/shard_map/ppermute | solution.py:635
  1001.8 17.0 %collective-permute-done.37 = f16[2,2,1056,128]{3,2,1,0:T(8,128)(2,1)S(1)} collective-permute-done((f16[2,2,1056,128]{3,2,1,0:T(8,128)(2,1)S(1)}, f16[2,2,1056,128]{3,2,1,0:T(8,128)(2,1)S(1)}, u32[]{:S(2)}, u32[]{:S(2)}) %collective-permute-start.37) | collective-permute-done | bytes 1081376 | tf_op jit(solution)/shard_map/ppermute | solution.py:635
  1022.7 32.2 %collective-permute-done.38 = f16[2,1056,128]{2,1,0:T(8,128)(2,1)S(1)} collective-permute-done((f16[2,1056,128]{2,1,0:T(8,128)(2,1)S(1)}, f16[2,1056,128]{2,1,0:T(8,128)(2,1)S(1)}, u32[]{:S(2)}, u32[]{:S(2)}) %collective-permute-start.38) | collective-permute-done | bytes 540704 | tf_op jit(solution)/shard_map/ppermute | solution.py:635
  1055.2 10.5 collective-permute-done.42
  1096.0 7.5 collective-permute-start.28
  (601 shorter events, 366.1 us)
Async XLA Ops:
  8.3 158.8 %collective-permute-start.20 = (f32[]{:T(128)}, f32[]{:T(128)}, u32[]{:S(2)}, u32[]{:S(2)}) collective-permute-start(f32[]{:T(128)} %get-tuple-element.119), channel_id=1, source_target_pairs={{0,4},{1,5},{2,6},{3,7},{4,0},{5,1},{6,2},{7,3},{8,12},{9,13},{10,... | collective-permute-start | bytes 20 | tf_op jit(solution)/shard_map/ppermute | solution.py:635
  13.7 24.8 %collective-permute-start = (bf16[304,128]{1,0:T(8,128)(2,1)S(1)}, bf16[304,128]{1,0:T(8,128)(2,1)S(1)}, u32[]{:S(2)}, u32[]{:S(2)}) collective-permute-start(bf16[304,128]{1,0:T(8,128)(2,1)S(1)} %get-tuple-element.202), channel_id=1, source_target_pairs={{0,4},{1,5},{2,6},{3,7},{4,0},{5,1},{6,2},{7,3},{8,12},{9,13},{10,... | collective-permute-start | bytes 233480 | tf_op jit(solution)/shard_map/ppermute | solution.py:635
  13.8 26.4 %collective-permute-start.5 = (bf16[304,128]{1,0:T(8,128)(2,1)S(1)}, bf16[304,128]{1,0:T(8,128)(2,1)S(1)}, u32[]{:S(2)}, u32[]{:S(2)}) collective-permute-start(bf16[304,128]{1,0:T(8,128)(2,1)S(1)} %get-tuple-element.203), channel_id=1, source_target_pairs={{0,4},{1,5},{2,6},{3,7},{4,0},{5,1},{6,2},{7,3},{8,12},{9,13},{10,... | collective-permute-start | bytes 233480 | tf_op jit(solution)/shard_map/ppermute | solution.py:635
  20.0 35.0 %collective-permute-start.10 = (bf16[1056,128]{1,0:T(8,128)(2,1)S(1)}, bf16[1056,128]{1,0:T(8,128)(2,1)S(1)}, u32[]{:S(2)}, u32[]{:S(2)}) collective-permute-start(bf16[1056,128]{1,0:T(8,128)(2,1)S(1)} %get-tuple-element.174), channel_id=1, source_target_pairs={{0,4},{1,5},{2,6},{3,7},{4,0},{5,1},{6,2},{7,3},{8,12},{9,13},{10,... | collective-permute-start | bytes 811016 | tf_op jit(solution)/shard_map/ppermute | solution.py:635
  20.2 35.0 %collective-permute-start.15 = (bf16[1056,128]{1,0:T(8,128)(2,1)S(1)}, bf16[1056,128]{1,0:T(8,128)(2,1)S(1)}, u32[]{:S(2)}, u32[]{:S(2)}) collective-permute-start(bf16[1056,128]{1,0:T(8,128)(2,1)S(1)} %get-tuple-element.175), channel_id=1, source_target_pairs={{0,4},{1,5},{2,6},{3,7},{4,0},{5,1},{6,2},{7,3},{8,12},{9,13},{10,... | collective-permute-start | bytes 811016 | tf_op jit(solution)/shard_map/ppermute | solution.py:635
  50.2 21.9 %collective-permute-start.2 = (bf16[2,2,304,128]{3,2,1,0:T(8,128)(2,1)S(1)}, bf16[2,2,304,128]{3,2,1,0:T(8,128)(2,1)S(1)}, u32[]{:S(2)}, u32[]{:S(2)}) collective-permute-start(bf16[2,2,304,128]{3,2,1,0:T(8,128)(2,1)S(1)} %pad_maximum_fusion.19), channel_id=1, source_target_pairs={{0,1},{1,0},{2,3},{3,2},{4,5},{5,4},{6,7},{7,6},{8,9},{9,8},{10,11... | collective-permute-start | bytes 933896 | tf_op jit(solution)/shard_map/ppermute | solution.py:635
  53.4 41.5 %collective-permute-start.7 = (bf16[2,2,304,128]{3,2,0,1:T(8,128)(2,1)S(1)}, bf16[2,2,304,128]{3,2,0,1:T(8,128)(2,1)S(1)}, u32[]{:S(2)}, u32[]{:S(2)}) collective-permute-start(bf16[2,2,304,128]{3,2,0,1:T(8,128)(2,1)S(1)} %pad_maximum_fusion.20), channel_id=1, source_target_pairs={{0,16},{1,17},{2,18},{3,19},{4,20},{5,21},{6,22},{7,23},{8,24},{9,... | collective-permute-start | bytes 933896 | tf_op jit(solution)/shard_map/ppermute | solution.py:635
  55.3 25.4 %collective-permute-start.16 = (bf16[2,1056,128]{2,1,0:T(8,128)(2,1)S(1)}, bf16[2,1056,128]{2,1,0:T(8,128)(2,1)S(1)}, u32[]{:S(2)}, u32[]{:S(2)}) collective-permute-start(bf16[2,1056,128]{2,1,0:T(8,128)(2,1)S(1)} %pad_maximum_fusion.18), channel_id=1, source_target_pairs={{0,2},{1,3},{2,0},{3,1},{4,6},{5,7},{6,4},{7,5},{8,10},{9,11},{10,... | collective-permute-start | bytes 1622024 | tf_op jit(solution)/shard_map/ppermute | solution.py:635
  70.6 23.4 %collective-permute-start.12 = (bf16[2,2,1056,128]{3,2,1,0:T(8,128)(2,1)S(1)}, bf16[2,2,1056,128]{3,2,1,0:T(8,128)(2,1)S(1)}, u32[]{:S(2)}, u32[]{:S(2)}) collective-permute-start(bf16[2,2,1056,128]{3,2,1,0:T(8,128)(2,1)S(1)} %pad_maximum_fusion.11), channel_id=1, source_target_pairs={{0,1},{1,0},{2,3},{3,2},{4,5},{5,4},{6,7},{7,6},{8,9},{9,8},{10,11... | collective-permute-start | bytes 3244040 | tf_op jit(solution)/shard_map/ppermute | solution.py:635
  72.2 41.6 %collective-permute-start.3 = (bf16[2,2,2,304,128]{4,3,2,1,0:T(8,128)(2,1)S(1)}, bf16[2,2,2,304,128]{4,3,2,1,0:T(8,128)(2,1)S(1)}, u32[]{:S(2)}, u32[]{:S(2)}) collective-permute-start(bf16[2,2,2,304,128]{4,3,2,1,0:T(8,128)(2,1)S(1)} %pad_maximum_fusion.14), channel_id=1, source_target_pairs={{0,16},{1,17},{2,18},{3,19},{4,20},{5,21},{6,22},{7,23},{8,24},{9,... | collective-permute-start | bytes 1867784 | tf_op jit(solution)/shard_map/ppermute | solution.py:635
  80.9 30.9 %collective-permute-start.17 = (bf16[2,2,1056,128]{3,2,0,1:T(8,128)(2,1)S(1)}, bf16[2,2,1056,128]{3,2,0,1:T(8,128)(2,1)S(1)}, u32[]{:S(2)}, u32[]{:S(2)}) collective-permute-start(bf16[2,2,1056,128]{3,2,0,1:T(8,128)(2,1)S(1)} %pad_maximum_fusion.12), channel_id=1, source_target_pairs={{0,16},{1,17},{2,18},{3,19},{4,20},{5,21},{6,22},{7,23},{8,24},{9,... | collective-permute-start | bytes 3244040 | tf_op jit(solution)/shard_map/ppermute | solution.py:635
  94.3 60.7 %collective-permute-start.13 = (bf16[2,2,2,1056,128]{4,3,2,1,0:T(8,128)(2,1)S(1)}, bf16[2,2,2,1056,128]{4,3,2,1,0:T(8,128)(2,1)S(1)}, u32[]{:S(2)}, u32[]{:S(2)}) collective-permute-start(bf16[2,2,2,1056,128]{4,3,2,1,0:T(8,128)(2,1)S(1)} %pad_maximum_fusion.5), channel_id=1, source_target_pairs={{0,16},{1,17},{2,18},{3,19},{4,20},{5,21},{6,22},{7,23},{8,24},{9,... | collective-permute-start | bytes 6488072 | tf_op jit(solution)/shard_map/ppermute | solution.py:635
  112.1 46.1 %collective-permute-start.18 = (bf16[2,2,2,1056,128]{4,3,0,1,2:T(8,128)(2,1)S(1)}, bf16[2,2,2,1056,128]{4,3,0,1,2:T(8,128)(2,1)S(1)}, u32[]{:S(2)}, u32[]{:S(2)}) collective-permute-start(bf16[2,2,2,1056,128]{4,3,0,1,2:T(8,128)(2,1)S(1)} %pad_maximum_fusion.6), channel_id=1, source_target_pairs={{0,1},{1,0},{2,3},{3,2},{4,5},{5,4},{6,7},{7,6},{8,9},{9,8},{10,11... | collective-permute-start | bytes 6488072 | tf_op jit(solution)/shard_map/ppermute | solution.py:635
  115.2 72.4 %collective-permute-start.4 = (bf16[2,2,2,2,304,128]{5,4,3,2,1,0:T(8,128)(2,1)}, bf16[2,2,2,2,304,128]{5,4,3,2,1,0:T(8,128)(2,1)}, u32[]{:S(2)}, u32[]{:S(2)}) collective-permute-start(bf16[2,2,2,2,304,128]{5,4,3,2,1,0:T(8,128)(2,1)} %pad_maximum_fusion.8), channel_id=1, source_target_pairs={{0,8},{1,9},{2,10},{3,11},{4,12},{5,13},{6,14},{7,15},{8,0},{9,1},... | collective-permute-start | bytes 3735560 | tf_op jit(solution)/shard_map/ppermute | solution.py:635
  115.2 74.0 %collective-permute-start.9 = (bf16[2,2,2,2,304,128]{5,4,3,2,1,0:T(8,128)(2,1)}, bf16[2,2,2,2,304,128]{5,4,3,2,1,0:T(8,128)(2,1)}, u32[]{:S(2)}, u32[]{:S(2)}) collective-permute-start(bf16[2,2,2,2,304,128]{5,4,3,2,1,0:T(8,128)(2,1)} %copy.206), channel_id=1, source_target_pairs={{0,8},{1,9},{2,10},{3,11},{4,12},{5,13},{6,14},{7,15},{8,0},{9,1},... | collective-permute-start | bytes 3735560 | tf_op jit(solution)/shard_map/ppermute | solution.py:635
  158.2 64.5 %collective-permute-start.14 = (bf16[2,2,2,2,1056,128]{5,4,3,2,1,0:T(8,128)(2,1)}, bf16[2,2,2,2,1056,128]{5,4,3,2,1,0:T(8,128)(2,1)}, u32[]{:S(2)}, u32[]{:S(2)}) collective-permute-start(bf16[2,2,2,2,1056,128]{5,4,3,2,1,0:T(8,128)(2,1)} %pad_maximum_fusion.1), channel_id=1, source_target_pairs={{0,8},{1,9},{2,10},{3,11},{4,12},{5,13},{6,14},{7,15},{8,0},{9,1},... | collective-permute-start | bytes 12976136 | tf_op jit(solution)/shard_map/ppermute | solution.py:635
  162.9 62.5 %collective-permute-start.19 = (bf16[2,2,2,2,1056,128]{5,4,3,2,1,0:T(8,128)(2,1)}, bf16[2,2,2,2,1056,128]{5,4,3,2,1,0:T(8,128)(2,1)}, u32[]{:S(2)}, u32[]{:S(2)}) collective-permute-start(bf16[2,2,2,2,1056,128]{5,4,3,2,1,0:T(8,128)(2,1)} %copy.207), channel_id=1, source_target_pairs={{0,8},{1,9},{2,10},{3,11},{4,12},{5,13},{6,14},{7,15},{8,0},{9,1},... | collective-permute-start | bytes 12976136 | tf_op jit(solution)/shard_map/ppermute | solution.py:635
  784.3 121.0 %collective-permute-start.30 = (f32[8,4224,128]{2,1,0:T(8,128)}, f32[8,4224,128]{2,1,0:T(8,128)}, u32[]{:S(2)}, u32[]{:S(2)}) collective-permute-start(f32[8,4224,128]{2,1,0:T(8,128)} %get-tuple-element.68), channel_id=1, source_target_pairs={{0,8},{1,9},{2,10},{3,11},{4,12},{5,13},{6,14},{7,15},{8,0},{9,1},... | collective-permute-start | bytes 51904520 | tf_op jit(solution)/shard_map/ppermute | solution.py:635
  801.0 22.5 %collective-permute-start.44 = (f32[8,1216,128]{2,1,0:T(8,128)}, f32[8,1216,128]{2,1,0:T(8,128)}, u32[]{:S(2)}, u32[]{:S(2)}) collective-permute-start(f32[8,1216,128]{2,1,0:T(8,128)} %get-tuple-element.77), channel_id=1, source_target_pairs={{0,8},{1,9},{2,10},{3,11},{4,12},{5,13},{6,14},{7,15},{8,0},{9,1},... | collective-permute-start | bytes 14942216 | tf_op jit(solution)/shard_map/ppermute | solution.py:635
  829.7 36.8 %collective-permute-start.50 = (f16[2,2,2,304,128]{4,3,1,0,2:T(8,128)(2,1)S(1)}, f16[2,2,2,304,128]{4,3,1,0,2:T(8,128)(2,1)}, u32[]{:S(2)}, u32[]{:S(2)}) collective-permute-start(f16[2,2,2,304,128]{4,3,1,0,2:T(8,128)(2,1)S(1)} %fusion.48), channel_id=1, source_target_pairs={{0,1},{1,0},{2,3},{3,2},{4,5},{5,4},{6,7},{7,6},{8,9},{9,8},{10,11... | collective-permute-start | bytes 1867784 | tf_op jit(solution)/shard_map/ppermute | solution.py:635
  867.8 20.9 %collective-permute-start.51 = (f16[2,2,304,128]{3,2,1,0:T(8,128)(2,1)S(1)}, f16[2,2,304,128]{3,2,1,0:T(8,128)(2,1)S(1)}, u32[]{:S(2)}, u32[]{:S(2)}) collective-permute-start(f16[2,2,304,128]{3,2,1,0:T(8,128)(2,1)S(1)} %get-tuple-element.159), channel_id=1, source_target_pairs={{0,16},{1,17},{2,18},{3,19},{4,20},{5,21},{6,22},{7,23},{8,24},{9,... | collective-permute-start | bytes 933896 | tf_op jit(solution)/shard_map/ppermute | solution.py:635
  903.0 33.6 %collective-permute-start.53 = (f16[304,128]{1,0:T(8,128)(2,1)S(1)}, f16[304,128]{1,0:T(8,128)(2,1)S(1)}, u32[]{:S(2)}, u32[]{:S(2)}) collective-permute-start(f16[304,128]{1,0:T(8,128)(2,1)S(1)} %fusion.81), channel_id=1, source_target_pairs={{0,2},{1,3},{2,0},{3,1},{4,6},{5,7},{6,4},{7,5},{8,10},{9,11},{10,... | collective-permute-start | bytes 233480 | tf_op jit(solution)/shard_map/ppermute | solution.py:635
  935.0 48.2 %collective-permute-start.36 = (f16[2,2,2,1056,128]{4,3,1,0,2:T(8,128)(2,1)}, f16[2,2,2,1056,128]{4,3,1,0,2:T(8,128)(2,1)}, u32[]{:S(2)}, u32[]{:S(2)}) collective-permute-start(f16[2,2,2,1056,128]{4,3,1,0,2:T(8,128)(2,1)} %fusion.13), channel_id=1, source_target_pairs={{0,1},{1,0},{2,3},{3,2},{4,5},{5,4},{6,7},{7,6},{8,9},{9,8},{10,11... | collective-permute-start | bytes 6488072 | tf_op jit(solution)/shard_map/ppermute | solution.py:635
  941.0 60.0 %collective-permute-start.65 = (f32[608,128]{1,0:T(8,128)S(1)}, f32[608,128]{1,0:T(8,128)S(1)}, u32[]{:S(2)}, u32[]{:S(2)}) collective-permute-start(f32[608,128]{1,0:T(8,128)S(1)} %pad_maximum_fusion.21), channel_id=1, source_target_pairs={{0,16},{1,17},{2,18},{3,19},{4,20},{5,21},{6,22},{7,23},{8,24},{9,... | collective-permute-start | bytes 933896 | tf_op jit(solution)/shard_map/ppermute | solution.py:635
  949.2 50.2 %collective-permute-start.40 = (f16[2,2,2,1056,128]{4,3,2,1,0:T(8,128)(2,1)}, f16[2,2,2,1056,128]{4,3,2,1,0:T(8,128)(2,1)S(1)}, u32[]{:S(2)}, u32[]{:S(2)}) collective-permute-start(f16[2,2,2,1056,128]{4,3,2,1,0:T(8,128)(2,1)} %get-tuple-element.128), channel_id=1, source_target_pairs={{0,16},{1,17},{2,18},{3,19},{4,20},{5,21},{6,22},{7,23},{8,24},{9,... | collective-permute-start | bytes 6488072 | tf_op jit(solution)/shard_map/ppermute | solution.py:635
  985.7 33.1 %collective-permute-start.37 = (f16[2,2,1056,128]{3,2,1,0:T(8,128)(2,1)S(1)}, f16[2,2,1056,128]{3,2,1,0:T(8,128)(2,1)S(1)}, u32[]{:S(2)}, u32[]{:S(2)}) collective-permute-start(f16[2,2,1056,128]{3,2,1,0:T(8,128)(2,1)S(1)} %get-tuple-element.130), channel_id=1, source_target_pairs={{0,16},{1,17},{2,18},{3,19},{4,20},{5,21},{6,22},{7,23},{8,24},{9,... | collective-permute-start | bytes 3244040 | tf_op jit(solution)/shard_map/ppermute | solution.py:635
  1000.5 20.7 %collective-permute-start.41 = (f16[2,2,1056,128]{3,2,1,0:T(8,128)(2,1)S(1)}, f16[2,2,1056,128]{3,2,1,0:T(8,128)(2,1)S(1)}, u32[]{:S(2)}, u32[]{:S(2)}) collective-permute-start(f16[2,2,1056,128]{3,2,1,0:T(8,128)(2,1)S(1)} %get-tuple-element.136), channel_id=1, source_target_pairs={{0,1},{1,0},{2,3},{3,2},{4,5},{5,4},{6,7},{7,6},{8,9},{9,8},{10,11... | collective-permute-start | bytes 3244040 | tf_op jit(solution)/shard_map/ppermute | solution.py:635
  1019.3 35.6 %collective-permute-start.38 = (f16[2,1056,128]{2,1,0:T(8,128)(2,1)S(1)}, f16[2,1056,128]{2,1,0:T(8,128)(2,1)S(1)}, u32[]{:S(2)}, u32[]{:S(2)}) collective-permute-start(f16[2,1056,128]{2,1,0:T(8,128)(2,1)S(1)} %get-tuple-element.150), channel_id=1, source_target_pairs={{0,4},{1,5},{2,6},{3,7},{4,0},{5,1},{6,2},{7,3},{8,12},{9,13},{10,... | collective-permute-start | bytes 1622024 | tf_op jit(solution)/shard_map/ppermute | solution.py:635
  1021.5 44.1 %collective-permute-start.42 = (f16[2,1056,128]{2,1,0:T(8,128)(2,1)S(1)}, f16[2,1056,128]{2,1,0:T(8,128)(2,1)S(1)}, u32[]{:S(2)}, u32[]{:S(2)}) collective-permute-start(f16[2,1056,128]{2,1,0:T(8,128)(2,1)S(1)} %get-tuple-element.152), channel_id=1, source_target_pairs={{0,4},{1,5},{2,6},{3,7},{4,0},{5,1},{6,2},{7,3},{8,12},{9,13},{10,... | collective-permute-start | bytes 1622024 | tf_op jit(solution)/shard_map/ppermute | solution.py:635
  1078.3 31.1 %collective-permute-start.63 = (f32[2112,128]{1,0:T(8,128)}, f32[2112,128]{1,0:T(8,128)}, u32[]{:S(2)}, u32[]{:S(2)}) collective-permute-start(f32[2112,128]{1,0:T(8,128)} %pad_maximum_fusion.13), channel_id=1, source_target_pairs={{0,16},{1,17},{2,18},{3,19},{4,20},{5,21},{6,22},{7,23},{8,24},{9,... | collective-permute-start | bytes 3244040 | tf_op jit(solution)/shard_map/ppermute | solution.py:635
  1079.9 27.2 %collective-permute-start.66 = (f32[2,608,128]{2,1,0:T(8,128)S(1)}, f32[2,608,128]{2,1,0:T(8,128)}, u32[]{:S(2)}, u32[]{:S(2)}) collective-permute-start(f32[2,608,128]{2,1,0:T(8,128)S(1)} %pad_maximum_fusion.16), channel_id=1, source_target_pairs={{0,8},{1,9},{2,10},{3,11},{4,12},{5,13},{6,14},{7,15},{8,0},{9,1},... | collective-permute-start | bytes 1867784 | tf_op jit(solution)/shard_map/ppermute | solution.py:635
  1117.6 21.7 %collective-permute-start.64 = (f32[2,2112,128]{2,1,0:T(8,128)}, f32[2,2112,128]{2,1,0:T(8,128)}, u32[]{:S(2)}, u32[]{:S(2)}) collective-permute-start(f32[2,2112,128]{2,1,0:T(8,128)} %pad_maximum_fusion.7), channel_id=1, source_target_pairs={{0,8},{1,9},{2,10},{3,11},{4,12},{5,13},{6,14},{7,15},{8,0},{9,1},... | collective-permute-start | bytes 6488072 | tf_op jit(solution)/shard_map/ppermute | solution.py:635
  (149 other events, 1570.0 us)

commit v3 on v1

v3 whole, which is shorter than its diff:
```python
import functools
import math

import jax
import jax.numpy as jnp
from jax import lax
from jax.experimental import pallas as pl
from jax.experimental.pallas import tpu as pltpu
from jax.sharding import PartitionSpec as P

D = 768
HEADS = 12
FF = 3072
DD = 384
DHEADS = 6
DFF = 1536
PIX = 1536
STEP = 10
ROWS = 2592

learn_rate = 0.05
BETA_ONE = 0.9
BETA_TWO = 0.95
EPSILON = 1e-08
weight_decay = 0.05
clip_norm = 0.05

F = jnp.float32
B = jnp.bfloat16
AXES = ("narrow", "wide")
NT = (((1,), (1,)), ((), ()))
NN = (((1,), (0,)), ((), ()))
TN = (((0,), (0,)), ((), ()))
VMEM_LIMIT = 60 << 20


def mm(left, right, dims=NN):
    return lax.dot_general(left, right, dims, preferred_element_type=F)


ENC_SHAPES = [
    (PIX, D), (D,), (D,), (D,), (D, 3 * D), (D,), (D,), (D, D), (D,), (D,), (D,),
    (D, FF), (FF,), (FF, D), (D,), (D,), (D,), (D, DD),
]
DEC_SHAPES = [
    (DD,), (DD,), (DD,), (DD, 3 * DD), (DD,), (DD,), (DD, DD), (DD,), (DD,), (DD,),
    (DD, DFF), (DFF,), (DFF, DD), (DD,), (DD,), (DD,), (DD, PIX), (PIX,),
]


def sinusoid(places, columns):
    half_width = columns // 2
    frequency = jnp.exp(jnp.arange(half_width, dtype=F) * (-math.log(10000.0) / half_width))
    angles = places[:, None] * frequency[None, :]
    return jnp.concatenate([jnp.sin(angles), jnp.cos(angles)], axis=1)


def layout(lengths, visible, row_count):
    positions = jnp.arange(row_count, dtype=jnp.int32)
    clip_ends = jnp.cumsum(lengths)
    starts = clip_ends - lengths
    segment = jnp.sum((positions[:, None] >= clip_ends[None, :]).astype(jnp.int32), axis=1)
    member = segment[:, None] == jnp.arange(3, dtype=jnp.int32)[None, :]
    clip_begin = jnp.sum(jnp.where(member, starts[None, :], 0), axis=1)
    clip_place = (positions - clip_begin).astype(F)
    pack_total = clip_ends[2]
    slot_live = (visible < pack_total).astype(F)
    shown_flag = jnp.zeros((row_count,), F).at[visible].add(slot_live)
    counted = jnp.where(positions < pack_total, 1.0 - shown_flag, 0.0)
    return (segment, clip_place, slot_live, shown_flag, counted)


def slot_layout(lengths, visible):
    clip_ends = jnp.cumsum(lengths)
    starts = clip_ends - lengths
    segment = jnp.sum((visible[:, None] >= clip_ends[None, :]).astype(jnp.int32), axis=1)
    member = segment[:, None] == jnp.arange(3, dtype=jnp.int32)[None, :]
    clip_begin = jnp.sum(jnp.where(member, starts[None, :], 0), axis=1)
    return segment, (visible - clip_begin).astype(F)


def norm_rows(x):
    center = x - jnp.mean(x, axis=1, keepdims=True)
    inverse = lax.rsqrt(jnp.mean(center * center, axis=1, keepdims=True) + 1e-06)
    return center * inverse, inverse


def norm_back(grad, hat, inverse):
    return inverse * (
        grad
        - jnp.mean(grad, axis=1, keepdims=True)
        - hat * jnp.mean(grad * hat, axis=1, keepdims=True)
    )


def total(x):
    return jnp.sum(x, axis=0, keepdims=True)


def low_lanes(rows):
    return lax.broadcasted_iota(jnp.int32, (rows, 128), 1) < 64


def low_rows(columns):
    return lax.broadcasted_iota(jnp.int32, (128, columns), 0) < 64


def halves(low, value, other):
    return jnp.where(low, value, other), jnp.where(low, other, value)


def softmax_keys(s):
    m = jnp.max(s, axis=0, keepdims=True)
    e = jnp.exp(s - m)
    l = jnp.sum(e, axis=0, keepdims=True)
    return e * (1.0 / l), m + jnp.log(l)


def qkv_kernel(vis_ref, live_ref, latent_ref, place_ref, row_ref, w_ref, vec_ref, mask_ref, x_ref, o_ref):
    x_ref[...] = place_ref[...] + row_ref[:, 2:3] * mask_ref[0:1, :DD]

    def add_slot(i, carry):
        at = pl.ds(jnp.minimum(vis_ref[i], ROWS - 1), 1)
        x_ref[at, :] += latent_ref[pl.ds(i, 1), :] * live_ref[i]
        return carry

    lax.fori_loop(0, latent_ref.shape[0], add_slot, 0, unroll=8)
    bm = 432

    def block(i, carry):
        part = pl.ds(pl.multiple_of(i * bm, 16), bm)
        hat, inverse = norm_rows(x_ref[part, :])
        normed = (hat * vec_ref[0:1, :DD] + vec_ref[1:2, :DD]).astype(B)
        o_ref[part, :] = (mm(normed, w_ref[...]) + vec_ref[2:3, :]).astype(B)
        return carry

    lax.fori_loop(0, ROWS // bm, block, 0)


def qkv_forward(visible, live, latent, places, rows, w, vec, mask):
    smem, vmem = pl.BlockSpec(memory_space=pltpu.SMEM), pl.BlockSpec(memory_space=pltpu.VMEM)
    return pl.pallas_call(
        qkv_kernel,
        in_specs=[smem] * 2 + [vmem] * 6,
        out_specs=[vmem] * 2,
        out_shape=[jax.ShapeDtypeStruct((ROWS, DD), F), jax.ShapeDtypeStruct((ROWS, 3 * DD), B)],
        compiler_params=pltpu.CompilerParams(vmem_limit_bytes=VMEM_LIMIT),
        cost_estimate=pl.CostEstimate(flops=10 * 10**9, bytes_accessed=16 << 20, transcendentals=0),
        name="dec_qkv",
    )(visible, live, latent, places, rows, w, vec, mask)


def attend_kernel(q_ref, k_ref, v_ref, qf_ref, kf_ref, o_ref, lse_ref, k0, k1):
    rows, bq = k_ref.shape[0], q_ref.shape[0]

    @pl.when(pl.program_id(1) == 0)
    def _():
        k0[...], k1[...] = halves(low_lanes(rows), k_ref[...], kf_ref[...])

    qs = halves(low_lanes(bq), q_ref[...] * jnp.asarray(0.125, B), qf_ref[...])
    scores = [mm(keys[...], q, NT) for keys, q in zip((k0, k1), qs)]
    outs, logs = [], []
    for s in scores:
        p, log = softmax_keys(s)
        outs.append(mm(v_ref[...], p.astype(B), TN))
        logs.append(log)
    o_ref[...] = jnp.where(low_rows(bq), outs[0], outs[1]).T.astype(B)
    lse_ref[0] = jnp.concatenate(logs + [jnp.zeros((6, bq), F)], axis=0)


def attend_forward(qkv, qf, kf, bq=864):
    nq = ROWS // bq
    return pl.pallas_call(
        attend_kernel,
        grid=(3, nq),
        in_specs=[
            pl.BlockSpec((bq, 128), lambda h, i: (i, h)),
            pl.BlockSpec((ROWS, 128), lambda h, i: (0, 3 + h)),
            pl.BlockSpec((ROWS, 128), lambda h, i: (0, 6 + h)),
            pl.BlockSpec((bq, 128), lambda h, i: (i, 0)),
            pl.BlockSpec((ROWS, 128), lambda h, i: (0, 0)),
        ],
        out_specs=[
            pl.BlockSpec((bq, 128), lambda h, i: (i, h)),
            pl.BlockSpec((1, 8, bq), lambda h, i: (h * nq + i, 0, 0)),
        ],
        out_shape=[
            jax.ShapeDtypeStruct((ROWS, DD), B),
            jax.ShapeDtypeStruct((3 * nq, 8, bq), F),
        ],
        scratch_shapes=[pltpu.VMEM((ROWS, 128), B)] * 2,
        compiler_params=pltpu.CompilerParams(vmem_limit_bytes=VMEM_LIMIT),
        cost_estimate=pl.CostEstimate(flops=60 * 10**9, bytes_accessed=16 << 20, transcendentals=0),
        name="dec_attend",
    )(qkv, qkv, qkv, qf, kf)


def attend_back_kernel(
    h, kc, q_ref, k_ref, v_ref, qf_ref, kf_ref, da_ref, lse_ref, dd_ref, dq_ref, dk_ref, dv_ref,
    k0, k1, z0, z1, dk_sum, dv_sum,
):
    rows, bq = k_ref.shape[0], q_ref.shape[0]
    step = pl.program_id(0)

    @pl.when(step == 0)
    def _():
        low, keys = low_lanes(rows), k_ref[...]
        k0[...], k1[...] = halves(low, keys, kf_ref[...])
        z0[...], z1[...] = halves(low, keys, jnp.zeros_like(keys))
        dk_sum[...] = jnp.zeros_like(dk_sum)
        dv_sum[...] = jnp.zeros_like(dv_sum)

    low = low_lanes(bq)
    q, da = q_ref[...] * jnp.asarray(0.125, B), da_ref[...]
    zero = jnp.zeros_like(q)
    qs = halves(low, q, qf_ref[...])
    dz = halves(low, da, zero)
    q_both, d_both = jnp.concatenate(halves(low, q, zero), axis=0), jnp.concatenate(dz, axis=0)
    mean = jnp.concatenate([dd_ref[i] for i in range(dd_ref.shape[0])], axis=1)
    dq = jnp.zeros((128, bq), F)
    for c in range(rows // kc):
        part = slice(c * kc, (c + 1) * kc)
        scores = [mm(keys[part, :], q, NT) for keys, q in zip((k0, k1), qs)]
        dps = [mm(v_ref[part, :], d, NT) for d in dz]
        ps, dss = [], []
        for i in range(2):
            p = jnp.exp(scores[i] - lse_ref[0, i : i + 1, :])
            ps.append(p.astype(B))
            dss.append((p * (dps[i] - mean[2 * h + i : 2 * h + i + 1, :])).astype(B))
        dv_sum[part, :] += mm(jnp.concatenate(ps, axis=1), d_both)
        dk_sum[part, :] += mm(jnp.concatenate(dss, axis=1), q_both)
        for z, ds in zip((z0, z1), dss):
            dq += mm(z[part, :], ds, TN)
    dq_ref[...] = (dq.T * 0.125).astype(B)

    @pl.when(step == pl.num_programs(0) - 1)
    def _():
        dk_ref[...] = dk_sum[...].astype(B)
        dv_ref[...] = dv_sum[...].astype(B)


def attend_back(qkv, qf, kf, da, lse, dd, h, bq=864, kc=864):
    nq = ROWS // bq
    many = bq // dd.shape[2]
    return pl.pallas_call(
        functools.partial(attend_back_kernel, h, kc),
        grid=(nq,),
        in_specs=[
            pl.BlockSpec((bq, 128), lambda i: (i, h)),
            pl.BlockSpec((ROWS, 128), lambda i: (0, 3 + h)),
            pl.BlockSpec((ROWS, 128), lambda i: (0, 6 + h)),
            pl.BlockSpec((bq, 128), lambda i: (i, 0)),
            pl.BlockSpec((ROWS, 128), lambda i: (0, 0)),
            pl.BlockSpec((bq, 128), lambda i: (i, h)),
            pl.BlockSpec((1, 8, bq), lambda i: (h * nq + i, 0, 0)),
            pl.BlockSpec((many, 8, bq // many), lambda i: (i, 0, 0)),
        ],
        out_specs=[
            pl.BlockSpec((bq, 128), lambda i: (i, 0)),
            pl.BlockSpec((ROWS, 128), lambda i: (0, 0)),
            pl.BlockSpec((ROWS, 128), lambda i: (0, 0)),
        ],
        out_shape=[jax.ShapeDtypeStruct((ROWS, 128), B)] * 3,
        scratch_shapes=[pltpu.VMEM((ROWS, 128), B)] * 4 + [pltpu.VMEM((ROWS, 128), F)] * 2,
        compiler_params=pltpu.CompilerParams(vmem_limit_bytes=VMEM_LIMIT),
        cost_estimate=pl.CostEstimate(flops=40 * 10**9, bytes_accessed=8 << 20, transcendentals=0),
        name="dec_attend_back",
    )(qkv, qkv, qkv, qf, kf, da, lse, dd)


def mlp_kernel(
    x_ref, a_ref, t_ref, row_ref, wo_ref, wu_ref, wd_ref, wh_ref, vec_ref,
    da_ref, dx_ref, dd_ref, go_ref, gu_ref, gd_ref, gh_ref, gv_ref,
):
    @pl.when(pl.program_id(0) == 0)
    def _():
        for ref in (go_ref, gu_ref, gd_ref, gh_ref, gv_ref):
            ref[...] = jnp.zeros_like(ref)

    a = a_ref[...]
    x1 = x_ref[...] + mm(a, wo_ref[...]) + vec_ref[0:1, :DD]
    hat2, inv2 = norm_rows(x1)
    n2 = (hat2 * vec_ref[1:2, :DD] + vec_ref[2:3, :DD]).astype(B)
    h = mm(n2, wu_ref[...]) + vec_ref[3:4, :]
    cdf = 0.5 * (1.0 + lax.erf(h * (1.0 / math.sqrt(2.0))))
    u = (h * cdf).astype(B)
    slope = cdf + h * jnp.exp(-0.5 * h * h) * (1.0 / math.sqrt(2.0 * math.pi))
    x2 = x1 + mm(u, wd_ref[...]) + vec_ref[4:5, :DD]
    hatf, invf = norm_rows(x2)
    nf = (hatf * vec_ref[5:6, :DD] + vec_ref[6:7, :DD]).astype(B)
    pred = mm(nf, wh_ref[...]) + vec_ref[7:8, :]
    goal, unused = norm_rows(t_ref[...].astype(F))
    err = pred - goal
    gv_ref[8:9, :] += total(err * err * row_ref[:, 0:1])
    dpred = err * row_ref[:, 1:2]
    gv_ref[7:8, :] += total(dpred)
    dpred = dpred.astype(B)
    gh_ref[...] += mm(nf, dpred, TN)
    dnf = mm(dpred, wh_ref[...], NT)
    gv_ref[5:6, :DD] += total(dnf * hatf)
    gv_ref[6:7, :DD] += total(dnf)
    dx2 = norm_back(dnf * vec_ref[5:6, :DD], hatf, invf)
    gv_ref[4:5, :DD] += total(dx2)
    dx2b = dx2.astype(B)
    gd_ref[...] += mm(u, dx2b, TN)
    dh = mm(dx2b, wd_ref[...], NT) * slope
    gv_ref[3:4, :] += total(dh)
    dh = dh.astype(B)
    gu_ref[...] += mm(n2, dh, TN)
    dn2 = mm(dh, wu_ref[...], NT)
    gv_ref[1:2, :DD] += total(dn2 * hat2)
    gv_ref[2:3, :DD] += total(dn2)
    dx1 = dx2 + norm_back(dn2 * vec_ref[1:2, :DD], hat2, inv2)
    gv_ref[0:1, :DD] += total(dx1)
    dx_ref[...] = dx1
    dx1 = dx1.astype(B)
    go_ref[...] += mm(a, dx1, TN)
    da = mm(dx1, wo_ref[...], NT).astype(B)
    da_ref[...] = da
    head_of = lax.broadcasted_iota(jnp.int32, (8, DD), 1) // 64
    pick = (head_of == lax.broadcasted_iota(jnp.int32, (8, DD), 0)).astype(F)
    dd_ref[0] = lax.dot_general(
        pick, da.astype(F) * a.astype(F), NT, precision=lax.Precision.HIGHEST, preferred_element_type=F
    )


def mlp_both(x, a, target, rows, wo, wu, wd, wh, vec, bm=432):
    full = lambda shape: pl.BlockSpec(shape, lambda i: (0, 0))
    part = lambda width: pl.BlockSpec((bm, width), lambda i: (i, 0))
    sums = [wo.shape, wu.shape, wd.shape, wh.shape, vec.shape]
    return pl.pallas_call(
        mlp_kernel,
        grid=(ROWS // bm,),
        in_specs=[part(DD), part(DD), part(PIX), part(128)]
        + [full(w.shape) for w in (wo, wu, wd, wh, vec)],
        out_specs=[part(DD), part(DD), pl.BlockSpec((1, 8, bm), lambda i: (i, 0, 0))] + [full(s) for s in sums],
        out_shape=[
            jax.ShapeDtypeStruct((ROWS, DD), B),
            jax.ShapeDtypeStruct((ROWS, DD), F),
            jax.ShapeDtypeStruct((ROWS // bm, 8, bm), F),
        ]
        + [jax.ShapeDtypeStruct(s, F) for s in sums],
        compiler_params=pltpu.CompilerParams(vmem_limit_bytes=VMEM_LIMIT),
        name="dec_mlp",
    )(x, a, target, rows, wo, wu, wd, wh, vec)


def qkv_back_kernel(x_ref, dx_ref, *refs):
    parts, (row_ref, w_ref, vec_ref, o_ref, g_ref, gv_ref) = refs[:9], refs[9:]

    @pl.when(pl.program_id(0) == 0)
    def _():
        for ref in (g_ref, gv_ref):
            ref[...] = jnp.zeros_like(ref)

    hat, inverse = norm_rows(x_ref[...])
    normed = (hat * vec_ref[0:1, :DD] + vec_ref[1:2, :DD]).astype(B)
    dp = jnp.concatenate([parts[3 * h + i][...] for i in range(3) for h in range(3)], axis=1)
    g_ref[...] += mm(normed, dp, TN)
    dn = mm(dp, w_ref[...], NT)
    gv_ref[2:3, :] += total(dp.astype(F))
    gv_ref[0:1, :DD] += total(dn * hat)
    gv_ref[1:2, :DD] += total(dn)
    dx = dx_ref[...] + norm_back(dn * vec_ref[0:1, :DD], hat, inverse)
    o_ref[...] = dx
    gv_ref[3:4, :DD] += total(dx * row_ref[:, 2:3])


def qkv_back(x, dx, dqkv, rows, w, vec, bm=432):
    full = lambda shape: pl.BlockSpec(shape, lambda i: (0, 0))
    part = lambda width: pl.BlockSpec((bm, width), lambda i: (i, 0))
    return pl.pallas_call(
        qkv_back_kernel,
        grid=(ROWS // bm,),
        in_specs=[part(DD)] * 2 + [part(128)] * 10 + [full(w.shape), full(vec.shape)],
        out_specs=[part(DD), full(w.shape), full(vec.shape)],
        out_shape=[
            jax.ShapeDtypeStruct((ROWS, DD), F),
            jax.ShapeDtypeStruct(w.shape, F),
            jax.ShapeDtypeStruct(vec.shape, F),
        ],
        compiler_params=pltpu.CompilerParams(vmem_limit_bytes=VMEM_LIMIT),
        cost_estimate=pl.CostEstimate(flops=15 * 10**9, bytes_accessed=8 << 20, transcendentals=0),
        name="dec_qkv_back",
    )(x, dx, *[part for head in dqkv for part in head], rows, w, vec)


def stack_rows(pieces, width, count=8):
    rows = [jnp.pad(p.astype(F), (0, width - p.shape[0])) for p in pieces]
    rows += [jnp.zeros((width,), F)] * (count - len(rows))
    return jnp.stack(rows)


def gelu_parts(h):
    cdf = 0.5 * (1.0 + lax.erf(h * (1.0 / math.sqrt(2.0))))
    return cdf, cdf + h * jnp.exp(-0.5 * h * h) * (1.0 / math.sqrt(2.0 * math.pi))


def enc_pair(qkv_ref, marks, j):
    q, k, v = (qkv_ref[:, i * D + j * 128 : i * D + (j + 1) * 128] for i in range(3))
    q = q * jnp.asarray(0.125, B)
    low = low_lanes(q.shape[0])
    return q, k, v, halves(low, q, marks[0]), halves(low, k, marks[1])


def enc_forward_kernel(
    pix_ref, place_ref, qm_ref, km_ref, vec_ref, we_hbm, wq_hbm, wo_hbm, wu_hbm, wd_hbm, wp_hbm,
    latent_ref, e0_ref, qkv_ref, a_ref, x1_ref, h_ref, x2_ref,
    we, wq, wo, wu, wd, wp, sems,
):
    loads = [
        pltpu.make_async_copy(source, target, sems.at[i])
        for i, (source, target) in enumerate(
            zip((we_hbm, wq_hbm, wo_hbm, wu_hbm, wd_hbm, wp_hbm), (we, wq, wo, wu, wd, wp))
        )
    ]
    for load in loads:
        load.start()
    loads[0].wait()
    e0 = mm(pix_ref[...], we[...]) + vec_ref[0:1, :D] + place_ref[...]
    e0_ref[...] = e0
    hat, unused = norm_rows(e0)
    n1 = (hat * vec_ref[1:2, :D] + vec_ref[2:3, :D]).astype(B)
    loads[1].wait()
    for i, bias in enumerate((vec_ref[3:4, :D], 0.0, vec_ref[4:5, :D])):
        part = slice(i * D, (i + 1) * D)
        qkv_ref[:, part] = (mm(n1, wq[:, part]) + bias).astype(B)
    marks = (qm_ref[...], km_ref[...])
    for j in range(HEADS // 2):
        unused, unused, v, qs, ks = enc_pair(qkv_ref, marks, j)
        scores = [mm(ks[i], qs[i], NT) for i in range(2)]
        outs = [mm(v, softmax_keys(s)[0].astype(B), TN) for s in scores]
        a_ref[:, j * 128 : (j + 1) * 128] = jnp.where(low_rows(v.shape[0]), outs[0], outs[1]).T.astype(B)
    loads[2].wait()
    x1 = e0 + mm(a_ref[...], wo[...]) + vec_ref[5:6, :D]
    x1_ref[...] = x1
    hat, unused = norm_rows(x1)
    n2 = (hat * vec_ref[6:7, :D] + vec_ref[7:8, :D]).astype(B)
    loads[3].wait()
    loads[4].wait()
    x2 = x1 + vec_ref[9:10, :D]
    for i in range(4):
        part = slice(i * D, (i + 1) * D)
        h = mm(n2, wu[:, part]) + vec_ref[8:9, part]
        h_ref[:, part] = h
        x2 += mm((h * gelu_parts(h)[0]).astype(B), wd[part, :])
    x2_ref[...] = x2
    hat, unused = norm_rows(x2)
    loads[5].wait()
    latent_ref[...] = mm((hat * vec_ref[10:11, :D] + vec_ref[11:12, :D]).astype(B), wp[...])


def enc_forward(pixels, places, q_marks, k_marks, vec, mats):
    rows = pixels.shape[0]
    hbm, vmem = pl.BlockSpec(memory_space=pl.ANY), pl.BlockSpec(memory_space=pltpu.VMEM)
    outs = [(DD, F), (D, F), (3 * D, B), (D, B), (D, F), (FF, F), (D, F)]
    return pl.pallas_call(
        enc_forward_kernel,
        in_specs=[vmem] * 5 + [hbm] * 6,
        out_specs=[vmem] * 7,
        out_shape=[jax.ShapeDtypeStruct((rows, width), kind) for width, kind in outs],
        scratch_shapes=[pltpu.VMEM(m.shape, B) for m in mats] + [pltpu.SemaphoreType.DMA((6,))],
        compiler_params=pltpu.CompilerParams(vmem_limit_bytes=VMEM_LIMIT),
        cost_estimate=pl.CostEstimate(flops=15 * 10**9, bytes_accessed=20 << 20, transcendentals=0),
        name="enc_forward",
    )(pixels, places, q_marks, k_marks, vec, *mats)


def put_product(lin, top, row, left, right):
    m, c = left.shape[0], right.shape[1] // 128
    step = min(m, 768)
    most = top[...]
    for r in range(0, m, step):
        for first in range(0, c, 2):
            last = min(first + 2, c)
            value = mm(left[r : r + step, :], right[:, first * 128 : last * 128])
            for i in range(first, last):
                piece = value[:, (i - first) * 128 : (i - first + 1) * 128]
                lin[pl.ds(row + r * c + i, step, stride=c), :] = piece
                most = jnp.maximum(most, jnp.max(jnp.abs(piece).reshape(-1, 8, 128), axis=0))
    top[...] = most


def put_vector(lin, top, row, value):
    for i in range(value.shape[1] // 128):
        piece = value[:, i * 128 : (i + 1) * 128]
        lin[pl.ds(row + i, 1), :] = piece
        top[0:1, :] = jnp.maximum(top[0:1, :], jnp.abs(piece))


def turned(value):
    return value.astype(F).T.astype(B)


def flush_start(lin, base, segments, core, kept, away, sem):
    for c in range(2):

        @pl.when(core == c)
        def _():
            for source, count, s, h, k, y, to in segments:
                target = (kept if h == c else away)[k]
                pltpu.make_async_copy(
                    lin.at[pl.ds(source - base, count)], target.at[s, y, pl.ds(to, count)], sem
                ).start()


def flush_wait(lin, segments, sem):
    count = sum(segment[1] for segment in segments)
    pltpu.make_async_copy(lin.at[pl.ds(0, count)], lin.at[pl.ds(0, count)], sem).wait()


def enc_back_one_kernel(
    base, rows_of, cuts, core_ref, vis_ref, live_ref, dx0_ref, x1_ref, h_ref, x2_ref, vec_ref, wu_hbm, wd_hbm, wp_hbm,
    dx1_ref, top_ref, *refs,
):
    chunks = (len(refs) - 7) // 2
    kept, away = refs[:chunks], refs[chunks : 2 * chunks]
    lin, wu, wd, wp, dl_ref, dh_ref, sems = refs[-7:]
    loads = [
        pltpu.make_async_copy(source, target, sems.at[i])
        for i, (source, target) in enumerate(zip((wp_hbm, wd_hbm, wu_hbm), (wp, wd, wu)))
    ]
    for load in loads:
        load.start()
    top_ref[...] = jnp.zeros_like(top_ref)
    upb, down, db, fg, fb, proj, end, last = (r - base for r in rows_of[1:])

    def take_slot(i, carry):
        at = pl.ds(jnp.minimum(vis_ref[i], ROWS - 1), 1)
        dl_ref[pl.ds(i, 1), :] = dx0_ref[at, :] * live_ref[i]
        return carry

    lax.fori_loop(0, dl_ref.shape[0], take_slot, 0, unroll=8)
    dl = dl_ref[...].astype(B)
    hatf, invf = norm_rows(x2_ref[...])
    put_product(lin, top_ref, proj, turned(hatf * vec_ref[10:11, :D] + vec_ref[11:12, :D]), dl)
    lin[pl.ds(end, lin.shape[0] - end), :] = jnp.zeros((lin.shape[0] - end, 128), F)
    loads[0].wait()
    dnf = mm(dl, wp[...], NT)
    put_vector(lin, top_ref, fg, total(dnf * hatf))
    put_vector(lin, top_ref, fb, total(dnf))
    dx2 = norm_back(dnf * vec_ref[10:11, :D], hatf, invf)
    put_vector(lin, top_ref, db, total(dx2))
    dx2b = dx2.astype(B)
    loads[1].wait()
    for i in range(4):
        part = slice(i * D, (i + 1) * D)
        h = h_ref[:, part]
        kept_share, slope = gelu_parts(h)
        put_product(lin, top_ref, down + i * D * (D // 128), turned(h * kept_share), dx2b)
        dh = mm(dx2b, wd[part, :], NT) * slope
        put_vector(lin, top_ref, upb + i * (D // 128), total(dh))
        dh_ref[:, part] = dh.astype(B)
    flush_start(lin, base, cuts[0], core_ref[0], kept, away, sems.at[3])
    loads[2].wait()
    hat2, inv2 = norm_rows(x1_ref[...])
    put_product(lin, top_ref, 0, turned(hat2 * vec_ref[6:7, :D] + vec_ref[7:8, :D]), dh_ref[...])
    flush_start(lin, base, cuts[1], core_ref[0], kept, away, sems.at[4])
    dn2 = mm(dh_ref[...], wu[...], NT)
    dx1_ref[0:1, :] = jnp.zeros((1, D), F)
    dx1 = dx2 + norm_back(dn2 * vec_ref[6:7, :D], hat2, inv2)
    count = dx1.shape[0]
    dx1_ref[0:count, :] = dx1
    dx1_ref[count : count + 1, :] = total(dn2 * hat2)
    dx1_ref[count + 1 : count + 2, :] = total(dn2)
    flush_wait(lin, cuts[0], sems.at[3])
    flush_wait(lin, cuts[1], sems.at[4])


def enc_back_two_kernel(
    rows_of, early_of, base_early, cuts, core_ref, dx1_ref, pix_ref, e0_ref, qkv_ref, a_ref, qm_ref, km_ref, vec_ref,
    g_qkv_ref, g_one_ref, wq_hbm, wo_hbm, top_in, *refs,
):
    chunks = (len(refs) - 6) // 4
    top_ref = refs[2 * chunks]
    kept, away = refs[2 * chunks + 1 : 3 * chunks + 1], refs[3 * chunks + 1 : 4 * chunks + 1]
    lin, wq, wo, dp_ref, sems = refs[-5:]
    loads = [
        pltpu.make_async_copy(source, target, sems.at[i])
        for i, (source, target) in enumerate(zip((wo_hbm, wq_hbm), (wo, wq)))
    ]
    for load in loads:
        load.start()
    top_ref[...] = top_in[...]
    embed, eb, g1, b1, qkv, qbias, vbias, out, ob, g2, b2 = rows_of
    count = pix_ref.shape[0]
    dx1 = dx1_ref[0:count, :]
    put_vector(lin, top_ref, g2, dx1_ref[count : count + 1, :])
    put_vector(lin, top_ref, b2, dx1_ref[count + 1 : count + 2, :])
    put_vector(lin, top_ref, ob, total(dx1))
    dx1b = dx1.astype(B)
    put_product(lin, top_ref, out, turned(a_ref[...]), dx1b)
    loads[0].wait()
    da = mm(dx1b, wo[...], NT).astype(B)
    marks = (qm_ref[...], km_ref[...])
    for j in range(HEADS // 2):
        q, k, v, qs, ks = enc_pair(qkv_ref, marks, j)
        low, zero = low_lanes(count), jnp.zeros_like(q)
        dz = halves(low, da[:, j * 128 : (j + 1) * 128], zero)
        scores = [mm(ks[i], qs[i], NT) for i in range(2)]
        dps = [mm(v, d, NT) for d in dz]
        ps, dss, dq = [], [], jnp.zeros((128, count), F)
        for i, keys in enumerate(halves(low, k, zero)):
            p = softmax_keys(scores[i])[0]
            ps.append(p.astype(B))
            dss.append((p * (dps[i] - jnp.sum(p * dps[i], axis=0, keepdims=True))).astype(B))
            dq += mm(keys, dss[i], TN)
        dk = mm(jnp.concatenate(dss, axis=1), jnp.concatenate(halves(low, q, zero), axis=0))
        dv = mm(jnp.concatenate(ps, axis=1), jnp.concatenate(dz, axis=0))
        for i, value in enumerate((dq.T * 0.125, dk, dv)):
            dp_ref[:, i * D + j * 128 : i * D + (j + 1) * 128] = value.astype(B)
    dp = dp_ref[...]
    sums = total(dp.astype(F))
    put_vector(lin, top_ref, qbias, sums[:, :D])
    put_vector(lin, top_ref, vbias, sums[:, 2 * D :])
    hat, inverse = norm_rows(e0_ref[...])
    put_product(lin, top_ref, qkv, turned(hat * vec_ref[1:2, :D] + vec_ref[2:3, :D]), dp)
    loads[1].wait()
    dn = mm(dp, wq[...], NT)
    put_vector(lin, top_ref, g1, total(dn * hat))
    put_vector(lin, top_ref, b1, total(dn))
    de0 = dx1 + norm_back(dn * vec_ref[1:2, :D], hat, inverse)
    put_vector(lin, top_ref, eb, total(de0))
    flush_start(lin, 0, cuts[0], core_ref[0], kept, away, sems.at[2])
    put_product(lin, top_ref, embed, turned(pix_ref[...]), de0.astype(B))
    c = g_qkv_ref.shape[1] // 128
    start = early_of[3]
    most = top_ref[...]
    for i in range(c):
        piece = g_qkv_ref[:, i * 128 : (i + 1) * 128]
        lin[pl.ds(start + i, g_qkv_ref.shape[0], stride=c), :] = piece
        most = jnp.maximum(most, jnp.max(jnp.abs(piece).reshape(-1, 8, 128), axis=0))
    top_ref[...] = most
    one = g_one_ref
    for row, value in zip(
        early_of[:3] + early_of[4:6],
        (one[3:4, :DD], one[0:1, :DD], one[1:2, :DD], one[2:3, :DD], one[2:3, 2 * DD :]),
    ):
        put_vector(lin, top_ref, row, value)
    end = early_of[6]
    lin[pl.ds(end, lin.shape[0] - end), :] = jnp.zeros((lin.shape[0] - end, 128), F)
    flush_start(lin, 0, cuts[1], core_ref[0], kept, away, sems.at[3])
    flush_start(lin, base_early, cuts[2], core_ref[0], kept, away, sems.at[4])
    for i in range(3):
        flush_wait(lin, cuts[i], sems.at[2 + i])


class Flat:
    def __init__(self, sections, wide, narrow, chunks):
        self.wide, self.narrow, self.sections = wide, narrow, sections
        self.spans = [-(-(rows + (0 if rows % 8 == 0 else 7)) // 8) * 8 for unused, rows in sections]
        self.parts = [-(-span // (narrow * 16)) * 16 for span in self.spans]
        self.starts = [sum(self.parts[:i]) for i in range(len(sections))]
        rows = sum(self.parts)
        step = -(-rows // (chunks * 16)) * 16
        self.chunks = [min(step, rows - i * step) for i in range(chunks)]
        self.shapes = [jax.ShapeDtypeStruct((wide, narrow // 2, count, 128), F) for count in self.chunks]

    def segments(self, section, low, high):
        first, rows = self.sections[section]
        part, span, at = self.parts[section], self.spans[section], self.starts[section]
        out = []
        for s in range(self.wide):
            start = first + s * rows // 8 * 8
            for p in range(self.narrow):
                begin = 0
                for k, count in enumerate(self.chunks):
                    lead = start + p * part - at + begin
                    a = max(low, start + p * part, lead)
                    b = min(high, start + span, start + (p + 1) * part, lead + count)
                    if a < b:
                        out.append((a, b - a, s, p // 2, k, p % 2, a - lead))
                    begin += count
        return out

    def reach(self, section):
        first, rows = self.sections[section]
        return first + (self.wide - 1) * rows // 8 * 8 + self.spans[section]

    def offset(self, section, index):
        return lax.rem(index * self.sections[section][1], 8)

    def of(self, piece, section):
        return piece[self.starts[section] : self.starts[section] + self.parts[section]]

    def squares(self, piece, section, index, part):
        value = self.of(piece, section)
        row = part * self.parts[section] + jnp.arange(value.shape[0], dtype=jnp.int32)[:, None]
        at = self.offset(section, index)
        inside = (row >= at) & (row < at + self.sections[section][1])
        return jnp.sum(jnp.where(inside, value * value, 0.0))

    def take(self, window, section, index):
        return lax.dynamic_slice_in_dim(window, self.offset(section, index), self.sections[section][1])


def enc_back_one(core, visible, live, dx0, saved, vec, mats, flat):
    x1, h, x2 = saved[3:]
    wu, wd, wp = mats[3:]
    rows = x1.shape[0]
    pieces = [p[0] for p in table(ENC_SHAPES)]
    end = pieces[-1] + DD // 128 * D
    total_rows = flat.sections[0][1] * flat.wide
    reach = max(flat.reach(0), total_rows)
    rows_of = tuple(pieces[11:]) + (end, reach)
    base, split = pieces[11], pieces[13]
    smem, vmem, hbm = (
        pl.BlockSpec(memory_space=space) for space in (pltpu.SMEM, pltpu.VMEM, pl.ANY)
    )
    top = jax.ShapeDtypeStruct((8, 128), F)
    cuts = (flat.segments(0, split, reach), flat.segments(0, base, split))
    room = max([reach - base] + [sum(seg[1] for seg in cut) for cut in cuts])
    chunks = len(flat.chunks)
    dx1, top, *out = pl.pallas_call(
        functools.partial(enc_back_one_kernel, base, rows_of, cuts),
        in_specs=[smem] * 3 + [vmem] * 5 + [hbm] * 3,
        out_specs=[vmem] * 2 + [hbm] * (2 * chunks),
        out_shape=[jax.ShapeDtypeStruct((rows + 8, D), F), top] + flat.shapes * 2,
        scratch_shapes=[
            pltpu.VMEM((room, 128), F), pltpu.VMEM(wu.shape, B), pltpu.VMEM(wd.shape, B),
            pltpu.VMEM(wp.shape, B), pltpu.VMEM((rows, DD), F),
            pltpu.VMEM((rows, FF), B), pltpu.SemaphoreType.DMA((5,)),
        ],
        compiler_params=pltpu.CompilerParams(vmem_limit_bytes=VMEM_LIMIT),
        cost_estimate=pl.CostEstimate(flops=20 * 10**9, bytes_accessed=30 << 20, transcendentals=0),
        name="enc_back_one",
    )(core, visible, live, dx0, x1, h, x2, vec, wu, wd, wp)
    return dx1, top, out


def enc_back_two(core, dx1, top, out, saved, pixels, marks, vec, mats, g_qkv, g_one, flat):
    e0, qkv, a = saved[:3]
    wq, wo = mats[1:3]
    rows = pixels.shape[0]
    pieces = [p[0] for p in table(ENC_SHAPES)]
    base = pieces[11]
    early_rows = table(DEC_SHAPES[:6])
    first = flat.sections[1][0]
    last = early_rows[-1][0] + early_rows[-1][2]
    early_of = tuple(base + p[0] for p in early_rows) + (base + last,)
    reach = max(flat.reach(1) - first, last)
    cuts = (
        flat.segments(0, pieces[1] // 8 * 8, base), flat.segments(0, 0, pieces[1] // 8 * 8),
        flat.segments(1, first, first + reach),
    )
    room = max([base + reach] + [sum(seg[1] for seg in cut) for cut in cuts])
    smem, vmem, hbm = (
        pl.BlockSpec(memory_space=space) for space in (pltpu.SMEM, pltpu.VMEM, pl.ANY)
    )
    chunks = len(flat.chunks)
    top, *out = pl.pallas_call(
        functools.partial(enc_back_two_kernel, tuple(pieces[:11]), early_of, first - base, cuts),
        in_specs=[smem] + [vmem] * 10 + [hbm] * 2 + [vmem] + [hbm] * (2 * chunks),
        out_specs=[vmem] + [hbm] * (2 * chunks),
        out_shape=[jax.ShapeDtypeStruct((8, 128), F)] + flat.shapes * 2,
        input_output_aliases={14 + i: 1 + i for i in range(2 * chunks)},
        scratch_shapes=[
            pltpu.VMEM((room, 128), F), pltpu.VMEM(wq.shape, B), pltpu.VMEM(wo.shape, B),
            pltpu.VMEM((rows, 3 * D), B), pltpu.SemaphoreType.DMA((5,)),
        ],
        compiler_params=pltpu.CompilerParams(vmem_limit_bytes=VMEM_LIMIT),
        cost_estimate=pl.CostEstimate(flops=15 * 10**9, bytes_accessed=30 << 20, transcendentals=0),
        name="enc_back_two",
    )(core, dx1, pixels, e0, qkv, a, *marks, vec, g_qkv, g_one, wq, wo, top, *out)
    return out[:chunks], out[chunks:], jnp.max(top)


def table(shapes, row=0):
    out = []
    for s in shapes:
        m, c = (s[0], s[1] // 128) if len(s) == 2 else (1, s[0] // 128)
        out.append((row, m, c))
        row += m * c
    return out


def job_rows(m, c, most):
    return max(n for n in range(16, m + 1, 16) if m % n == 0 and n * c <= most)


def split_rows(shard, shares, note):
    out, place, first = [], 0, 0
    for i, share in enumerate(shares):
        rows = -(-shard * share // (100 * 16)) * 16
        used = rows - 1 if note and i == 0 else rows
        out.append((place, first, 4, rows, used))
        place, first = place + 4 * rows, first + 4 * used
    if first < shard:
        rows = -(-(shard - first) // 32) * 16
        out.append((place, first, 2, rows, rows))
    return out


def unpack_kernel(pieces, groups, shard, wide, core_ref, *refs):
    mats = [p for p in pieces if p[1] > 1]
    count = len(groups)
    own, other, refs = refs[:count], refs[count : 2 * count], refs[2 * count :]
    outs, vec_ref = refs[: len(mats)], refs[len(mats)]
    buf, lin, in_sem, out_sem = refs[len(mats) + 1 : len(mats) + 5]
    stages = refs[len(mats) + 5 :]
    core = core_ref[0]
    plan, size = [], 0
    for g, (place, first, parts, rows, used) in enumerate(groups):
        for i in range(parts):
            a, b = first + i * used, min(first + (i + 1) * used, shard)
            if a < b:
                plan.append((g, i, rows, size, a, b - a))
                size += rows

    def fetch(sources, s, entry):
        g, i, rows, to, at, used = entry
        at_source = (i % 2) * rows if groups[g][2] == 4 else 0
        return pltpu.make_async_copy(
            sources[g].at[s, pl.ds(at_source, rows)], buf.at[s, pl.ds(to, rows)], in_sem.at[s]
        )

    for s in range(wide):
        for c in range(2):

            @pl.when(core == c)
            def _():
                for entry in plan:
                    of = entry[1] // 2 if groups[entry[0]][2] == 4 else entry[1]
                    fetch(own if of == c else other, s, entry).start()

    for s in range(wide):
        pltpu.make_async_copy(buf.at[s, pl.ds(0, size)], buf.at[s, pl.ds(0, size)], in_sem.at[s]).wait()
        for g, i, rows, to, at, used in plan:
            lin[pl.ds(s * shard + at, used), :] = buf[s, pl.ds(to, rows), :].astype(F)[:used]

    vec_ref[...] = jnp.zeros_like(vec_ref)
    v = 0
    for row, m, c in pieces:
        if m == 1:
            for j in range(c):
                vec_ref[v : v + 1, j * 128 : (j + 1) * 128] = lin[pl.ds(row + j, 1), :]
            v += 1
    for k, (row, m, c) in enumerate(mats):
        stage, out = stages[k], outs[k]
        n = stage.shape[1]
        jobs = m // n

        def store(j, slot):
            return pltpu.make_async_copy(
                stage.at[slot], out.at[pl.ds(pl.multiple_of(j * n, 16), n)], out_sem.at[slot]
            )

        def job(j, carry):
            slot = lax.rem(j, 2)

            @pl.when(j >= 2)
            def _():
                store(j - 2, slot).wait()

            for i in range(c):
                rows = pl.ds(row + i + j * (n * c), n, stride=c)
                stage[slot, :, i * 128 : (i + 1) * 128] = lin[rows, :].astype(B)
            store(j, slot).start()
            return carry

        lax.fori_loop(0, jobs, job, 0)
        for j in range(max(jobs - 2, 0), jobs):
            store(j, j % 2).wait()


def unpack_flat(own, other, groups, shard, wide, core, shapes, name):
    pieces = table(shapes)
    mats = [s for s in shapes if len(s) == 2]
    vectors = [s for s in shapes if len(s) == 1]
    width = max(s[0] for s in vectors)
    count = -(-len(vectors) // 8) * 8
    hbm = pl.BlockSpec(memory_space=pl.ANY)
    stages = [pltpu.VMEM((2, job_rows(s[0], s[1] // 128, 1152), s[1]), B) for s in mats]
    room = groups[-1][0] + groups[-1][2] * groups[-1][3]
    return pl.pallas_call(
        functools.partial(unpack_kernel, pieces, groups, shard, wide),
        in_specs=[pl.BlockSpec(memory_space=pltpu.SMEM)] + [hbm] * (2 * len(groups)),
        out_specs=[hbm] * len(mats) + [pl.BlockSpec(memory_space=pltpu.VMEM)],
        out_shape=[jax.ShapeDtypeStruct(s, B) for s in mats] + [jax.ShapeDtypeStruct((count, width), F)],
        scratch_shapes=[
            pltpu.VMEM((wide, room, 128), B), pltpu.VMEM((wide * shard, 128), F),
            pltpu.SemaphoreType.DMA((wide,)), pltpu.SemaphoreType.DMA((2,)),
        ] + stages,
        compiler_params=pltpu.CompilerParams(vmem_limit_bytes=VMEM_LIMIT),
        cost_estimate=pl.CostEstimate(flops=0, bytes_accessed=wide * shard * 1536, transcendentals=0),
        name=name,
    )(core, *own, *other)


def pack_kernel(pieces, segments, core_ref, *refs):
    mats = [p for p in pieces if p[1] > 1]
    ins, vec_ref = refs[: len(mats)], refs[len(mats)]
    top_ref, *out = refs[len(mats) + 1 : -2]
    kept, away = out[: len(out) // 2], out[len(out) // 2 :]
    lin, sem = refs[-2:]
    first, end = pieces[0][0], pieces[-1][0] + pieces[-1][1] * pieces[-1][2]
    lin[pl.ds(0, first), :] = jnp.zeros((first, 128), F)
    lin[pl.ds(end, lin.shape[0] - end), :] = jnp.zeros((lin.shape[0] - end, 128), F)
    top_ref[...] = jnp.zeros_like(top_ref)
    k, v = 0, 0
    for row, m, c in pieces:
        if m == 1:
            put_vector(lin, top_ref, row, vec_ref[v : v + 1, : c * 128])
            v += 1
            continue
        most = top_ref[...]
        for i in range(c):
            piece = ins[k][:, i * 128 : (i + 1) * 128]
            lin[pl.ds(row + i, m, stride=c), :] = piece
            most = jnp.maximum(most, jnp.max(jnp.abs(piece).reshape(-1, 8, 128), axis=0))
        top_ref[...] = most
        k += 1
    flush_start(lin, 0, segments, core_ref[0], kept, away, sem)
    flush_wait(lin, segments, sem)


def pack_late(mats, vectors, pieces, flat, core, name):
    hbm, vmem = pl.BlockSpec(memory_space=pl.ANY), pl.BlockSpec(memory_space=pltpu.VMEM)
    segments = flat.segments(0, 0, flat.reach(0))
    room = max(flat.reach(0), flat.wide * flat.sections[0][1], sum(seg[1] for seg in segments))
    chunks = len(flat.chunks)
    unused, *out = pl.pallas_call(
        functools.partial(pack_kernel, pieces, segments),
        in_specs=[pl.BlockSpec(memory_space=pltpu.SMEM)] + [vmem] * (len(mats) + 1),
        out_specs=[vmem] + [hbm] * (2 * chunks),
        out_shape=[jax.ShapeDtypeStruct((8, 128), F)] + flat.shapes * 2,
        scratch_shapes=[pltpu.VMEM((room, 128), F), pltpu.SemaphoreType.DMA],
        compiler_params=pltpu.CompilerParams(vmem_limit_bytes=VMEM_LIMIT),
        cost_estimate=pl.CostEstimate(flops=0, bytes_accessed=30 << 20, transcendentals=0),
        name=name,
    )(core, *mats, vectors)
    return out[:chunks], out[chunks:]


class Links:
    def __init__(self, mesh):
        self.narrow, self.wide = mesh.shape["narrow"], mesh.shape["wide"]
        self.wide_bits = [("wide", b) for b in reversed(range(self.wide.bit_length() - 1))]
        self.x, self.upper = self.wide_bits[-1], self.wide_bits[:-1]
        self.y, self.core = ("narrow", 1), ("narrow", 0)

    def mine(self, bit):
        return (lax.axis_index(bit[0]) >> bit[1]) & 1

    def swap(self, value, bit):
        mask = 1 << bit[1] if bit[0] == "wide" else self.wide << bit[1]
        pairs = [(i, i ^ mask) for i in range(self.narrow * self.wide)]
        return lax.ppermute(value, AXES, pairs)

    def everyone(self, value, how):
        for bit in [self.core, self.x, self.y] + self.upper:
            value = how(value, self.swap(value, bit))
        return value

    def scale(self, top):
        count = self.narrow * self.wide
        return 32768.0 / (count * jnp.maximum(self.everyone(top, jnp.maximum), 1e-30))

    def gather(self, value, axes, order):
        group = Group(self, value, axes, order)
        while group.order:
            group.step()
        return group.value

    def scatter_parts(self, kept, other, scale):
        axes = self.wide_bits + [self.y]
        parts = []
        for i, (one, two) in enumerate(zip(kept, other)):
            first = [self.x, self.y] if i % 2 == 0 else [self.y, self.x]
            shape = (2,) * len(axes) + one.shape[2:]
            parts.append(Part(self, one.reshape(shape), two.reshape(shape), axes, first + self.upper, scale))
        return parts


class Group:
    def __init__(self, links, value, axes, order):
        self.links, self.value, self.axes, self.order, self.have = links, value, axes, list(order), []

    def step(self):
        bit = self.order.pop(0)
        other = self.links.swap(self.value, bit)
        low = self.links.mine(bit) == 0
        self.have.append(bit)
        place = [b for b in self.axes if b in self.have].index(bit)
        pair = [jnp.where(low, self.value, other), jnp.where(low, other, self.value)]
        self.value = jnp.stack(pair, axis=place)


class Part:
    def __init__(self, links, kept, other, axes, order, scale):
        self.links, self.kept, self.other, self.axes, self.order = links, kept, other, list(axes), list(order)
        self.scale = scale

    def away(self):
        bit = self.order[0]
        self.place, self.index = self.axes.index(bit), self.links.mine(bit)
        value = self.take(1 - self.index)
        return value if len(self.order) == 1 or self.scale is None else (value * self.scale).astype(jnp.float16)

    def take(self, index):
        cut = lambda value: lax.dynamic_index_in_dim(value, index, self.place, keepdims=False)
        return cut(self.kept) + cut(self.other)

    def exchange(self, away):
        bit = self.order.pop(0)
        received = self.links.swap(away, bit)
        if received.dtype == jnp.float16:
            received = received.astype(F) * (1.0 / self.scale)
        self.kept, self.other = self.take(self.index), received
        self.axes.pop(self.place)

    def finish(self):
        while self.order:
            self.exchange(self.away())
        return self.kept + self.other


def after(value, *others):
    return lax.optimization_barrier((value,) + others)[0]


def gather_groups(shard, groups, orders, note, links):
    unused, first, parts, rows, used = groups[-1]
    shard = jnp.pad(shard, ((0, first + parts * used - shard.shape[0]), (0, 0)))
    out = []
    for (unused, first, parts, rows, used), order in zip(groups, orders):
        part = links.mine(links.core) if parts == 2 else links.mine(links.core) * 2 + links.mine(links.y)
        value = lax.dynamic_slice_in_dim(shard, first + part * used, used)
        if used < rows:
            value = jnp.concatenate([value, note])
        out.append(Group(links, value, links.wide_bits + ([links.y] if parts == 4 else []), order))
    return out


def gathered(groups, links):
    own = [g.value.reshape(links.wide, -1, 128) for g in groups]
    return own, [links.swap(v, links.core) for v in own]


def gather_params(enc, dec, note, links):
    y_last, x_last = links.upper + [links.x, links.y], links.upper + [links.y, links.x]
    enc_rows, dec_rows = split_rows(enc.shape[0], (8, 8), False), split_rows(dec.shape[0], (13, 13), True)
    enc_groups = gather_groups(
        enc, enc_rows, (y_last, x_last, links.upper[:-1] + [links.x] + links.upper[-1:]), note, links
    )
    one, two, three = enc_groups
    dec_groups = gather_groups(dec, dec_rows, (x_last, y_last), note, links)
    for g in (one, two):
        g.step()
    three.value = after(three.value, one.value, two.value)
    while one.order:
        for g in dec_groups:
            g.value = after(g.value, one.value, two.value)
        for g in (one, two, three):
            if g.order:
                g.step()
        for g in dec_groups:
            g.step()
    return (*gathered(enc_groups, links), enc_rows), dec_groups, dec_rows


def join_shard(piece, links):
    axes = [links.core, links.y]
    return links.gather(piece, axes, [links.y, links.core]).reshape(-1, 128)


def adamw_update(master, gradient, moment_one, moment_two, clip_scale):
    gradient = gradient * clip_scale
    moment_one = BETA_ONE * moment_one + (1.0 - BETA_ONE) * gradient
    moment_two = BETA_TWO * moment_two + (1.0 - BETA_TWO) * gradient * gradient
    first_hat = moment_one / (1.0 - BETA_ONE**STEP)
    second_hat = moment_two / (1.0 - BETA_TWO**STEP)
    updated = master - learn_rate * (
        first_hat / (jnp.sqrt(second_hat) + EPSILON) + weight_decay * master
    )
    return (moment_one, moment_two, updated)


def body(
    links, vis_pixels, target, clip_lens, vis_index, params_enc, m_enc, v_enc, params_dec, m_dec, v_dec
):
    lengths = clip_lens[0]
    visible = vis_index[0]
    mine, core = lax.axis_index("wide"), links.mine(links.core).astype(jnp.int32).reshape(1)
    enc_shard, dec_shard = (v.shape[0] // 128 for v in (params_enc, params_dec))
    segment, clip_place, slot_live, shown_flag, counted = layout(lengths, visible, target.shape[0])

    here = jnp.sum(counted).astype(jnp.int32)
    note = jnp.pad(jnp.stack([here // 64, here % 64]), (0, 126))[None, :].astype(B)
    enc_parts, dec_groups, dec_rows = gather_params(
        params_enc.astype(B).reshape(-1, 128), params_dec.astype(B).reshape(-1, 128), note, links
    )
    *enc_mats, enc_vec = unpack_flat(*enc_parts, enc_shard, links.wide, core, ENC_SHAPES, "unpack_enc")
    for g in dec_groups:
        g.value = after(g.value, enc_vec)
        while g.order:
            g.step()
    dec_own, dec_other = gathered(dec_groups, links)
    last = dec_rows[0][3] - 1
    notes = jnp.stack([v[0].reshape(links.wide, 2, -1, 128)[:, :, last, :2] for v in (dec_own, dec_other)])
    notes = notes.astype(F)
    masked_count = jnp.sum(notes[..., 0]) * 64.0 + jnp.sum(notes[..., 1])
    cotangent = 1.0 / masked_count

    segment, clip_place, shown_flag, counted = (
        v[:ROWS] for v in (segment, clip_place, shown_flag, counted)
    )
    rows = jnp.stack([counted, counted * (cotangent * (2.0 / PIX)), 1.0 - shown_flag], axis=1)
    rows = jnp.pad(rows, ((0, 0), (0, 125)))
    lane = jnp.arange(128, dtype=jnp.int32)[None, :] % 64

    def marks_of(labels):
        mark = lane == labels[:, None]
        return mark.astype(B), jnp.where(mark | (lane > 3), 0.0, -1e30).astype(B)

    q_marks, k_marks = marks_of(segment)
    slot_segment, slot_place = slot_layout(lengths, visible)
    slot_marks = marks_of(slot_segment)

    latent, *saved = enc_forward(vis_pixels, sinusoid(slot_place, D), *slot_marks, enc_vec, enc_mats)
    dec_own = [after(v, latent) for v in dec_own]
    *dec_mats, dec_vec = unpack_flat(
        dec_own, dec_other, dec_rows, dec_shard, links.wide, core, DEC_SHAPES, "unpack_dec"
    )
    w_qkv, w_out, w_up, w_down, w_head = dec_mats
    bias = jnp.concatenate([dec_vec[3, :DD], jnp.zeros((DD,), F), dec_vec[4, :DD]])
    vec_one = stack_rows([dec_vec[1, :DD], dec_vec[2, :DD], bias], 3 * DD)
    vec_two = jnp.concatenate([dec_vec[5:13], jnp.zeros((8, DFF), F)])
    x0, qkv = qkv_forward(
        visible, slot_live, latent, sinusoid(clip_place, DD), rows, w_qkv, vec_one, dec_vec
    )
    a, lse = attend_forward(qkv, q_marks, k_marks)
    da, dx1, dd, g_out, g_up, g_down, g_head, g_two = mlp_both(
        x0, a, target, rows, w_out, w_up, w_down, w_head, vec_two
    )

    late_flat = Flat([(0, dec_shard)], links.wide, links.narrow, 2)
    kept, away = pack_late(
        [g_out, g_up, g_down, g_head], g_two, table(DEC_SHAPES)[6:], late_flat, core, "pack_dec"
    )
    back = lambda da, h: attend_back(qkv, q_marks, k_marks, da, lse, dd, h)
    da, away = lax.optimization_barrier((da, away))
    late = links.scatter_parts(kept, [links.swap(v, links.core) for v in away], None)
    dqkv = [back(da, 0)]
    for h in (1, 2):
        sent = [part.away() for part in late]
        da, sent, dqkv = lax.optimization_barrier((da, sent, dqkv))
        dqkv = dqkv + [back(da, h)]
        for part, value in zip(late, sent):
            part.exchange(value)
    sent = [part.away() for part in late]
    dx1, sent, dqkv = lax.optimization_barrier((dx1, sent, dqkv))
    dx0, g_qkv, g_one = qkv_back(x0, dx1, dqkv, rows, w_qkv, vec_one)
    for part, value in zip(late, sent):
        part.exchange(value)

    early = table(DEC_SHAPES[:6])
    early_count = early[-1][0] + early[-1][2]
    flat = Flat(
        [(0, enc_shard), (enc_shard * links.wide, -(-early_count // links.wide))], links.wide, links.narrow, 4
    )
    dx1, top, out = enc_back_one(core, visible, slot_live, dx0, saved, enc_vec, enc_mats, flat)
    sent = [part.away() for part in late]
    dx1, sent = lax.optimization_barrier((dx1, sent))
    kept, away, top = enc_back_two(
        core, dx1, top, out, saved, vis_pixels, slot_marks, enc_vec, enc_mats, g_qkv, g_one, flat
    )
    for part, value in zip(late, sent):
        part.exchange(value)
    piece_dec = jnp.concatenate([part.finish() for part in late])
    first = [links.swap(v, links.core) for v in away[:2]]
    second = [links.swap(after(v, *first), links.core) for v in away[2:]]
    parts = links.scatter_parts(kept, first + second, links.scale(top))
    piece = jnp.concatenate([part.finish() for part in parts])

    part = links.mine(links.core) * 2 + links.mine(links.y)
    squares = flat.squares(piece, 0, mine, part) + flat.squares(piece, 1, mine, part)
    squares += late_flat.squares(piece_dec, 0, mine, part)
    squares, loss_sum = links.everyone(jnp.stack([squares, jnp.sum(g_two[8]) / PIX]), jnp.add)
    grad_norm = jnp.sqrt(squares)
    clip_scale = jnp.minimum(1.0, clip_norm / (grad_norm + 1e-06))
    narrow_bits = [links.core, links.y]
    joined, joined_late = join_shard(flat.of(piece, 0), links), join_shard(piece_dec, links)
    everywhere = links.gather(
        flat.of(piece, 1), links.wide_bits + narrow_bits, links.upper + [links.x, links.y, links.core]
    ).reshape(links.wide, -1, 128)
    count = flat.sections[1][1]
    early_sum = jnp.concatenate(
        [everywhere[s, s * count % 8 : s * count % 8 + count] for s in range(links.wide)]
    )
    early_sum = jnp.pad(early_sum, ((0, links.wide * dec_shard - links.wide * count), (0, 0)))
    grad_enc = flat.take(joined, 0, mine).reshape(-1)
    grad_dec = late_flat.take(joined_late, 0, mine) + lax.dynamic_slice_in_dim(early_sum, mine * dec_shard, dec_shard)
    enc_one, enc_two, enc_new = adamw_update(params_enc, grad_enc, m_enc, v_enc, clip_scale)
    dec_one, dec_two, dec_new = adamw_update(
        params_dec, grad_dec.reshape(-1), m_dec, v_dec, clip_scale
    )
    return (loss_sum, masked_count, grad_norm, enc_one, enc_two, enc_new, dec_one, dec_two, dec_new)


def solution(mesh):
    placed = (P(AXES, None),) * 4 + (P("wide"),) * 6
    return jax.shard_map(
        functools.partial(body, Links(mesh)),
        mesh=mesh,
        in_specs=placed,
        out_specs=(P(), P(), P()) + (P("wide"),) * 6,
        check_vma=False,
    )
```

time: 1720 us -> 878 us (0.51)
  local copies, waits for them, and re-layouts: 704 us -> 35.7 us
  waiting for transfers between devices: 357 us -> 271 us
  matrix products: 69 us -> 0 us
  other arithmetic: 152 us -> 99.8 us
  Pallas kernels: 324 us -> 376 us
    unnamed x317 -> x69, local copies, waits for them, and re-layouts: 260 us -> 12.8 us
    slice x17 -> x6, local copies, waits for them, and re-layouts: 168 us -> 2.67 us  [the longest x1 0.9 us: body(): vec_two = jnp.concatenate([dec_vec[5:13], jnp.zeros((8, DFF), F)])]
    reshape x22 -> x0, local copies, waits for them, and re-layouts: 166 us -> none  [the longest x2 41.9 us: scatter_grads(): flat.reshape(links.wide, shard)]
    ppermute x59 -> x73, waiting for transfers between devices: 357 us -> 271 us  [swap(): return lax.ppermute(value, AXES, pairs)]
    dot_general x23 -> x0, matrix products: 69 us -> none  [the longest x17 64.2 us: product(): return jnp.dot(left, right, preferred_element_type=F)]
    pallas_call x3 -> x11, Pallas kernels: 242 us -> 297 us  [the longest x3 121 us: attend_back(): pl.pallas_call(functools.partial(attend_back_kernel, h, kc), grid=(nq,),...]
    pad x4 -> x2, local copies, waits for them, and re-layouts: 35.6 us -> 0.01 us  [stack_rows(): rows = [jnp.pad(p.astype(F), (0, width - p.shape[0])) for p in pieces]]
    squeeze x20 -> x1, local copies, waits for them, and re-layouts: 36.8 us -> 1.25 us  [body(): everywhere[s, s * count % 8:s * count % 8 + count]]
  transfers between devices with their start and end apart: 59 -> 73, of which waited for: 35 -> 38; matrix products, arithmetic and copies ran while one was open for 16% -> 12% of each run, Pallas kernels for 0% -> 23%
where the time goes in v3:
time: 878 us; the launch traced here: 874 us
  Pallas kernels  376 us (43%)
  waiting for transfers between devices  271 us (31%)
  other arithmetic  99.8 us (11%)
  starting transfers between devices  77.3 us (9%)
  local copies, waits for them, and re-layouts  35.7 us (4%)
  between operations  13.7 us (2%)
    ppermute x73, waiting for transfers between devices, swap(): return lax.ppermute(value, AXES, pairs)  271 us
    pallas_call x3, Pallas kernels, attend_back(): pl.pallas_call(functools.partial(attend_back_kernel, h, kc), grid=(nq,),...  121 us
    ppermute x73, starting transfers between devices, swap(): return lax.ppermute(value, AXES, pairs)  77.3 us
    pallas_call x1, Pallas kernels, mlp_both(): pl.pallas_call(mlp_kernel, grid=(ROWS // bm,), in_specs=[part(DD), part(D...  65.8 us
    pallas_call x1, Pallas kernels, attend_forward(): pl.pallas_call(attend_kernel, grid=(3, nq), in_specs=[pl.BlockSpec((bq, 1...  63.5 us
    pallas_call x2, Pallas kernels, unpack_flat(): pl.pallas_call(functools.partial(unpack_kernel, pieces, groups, shard, wi...  41.2 us
    add x24, other arithmetic, take(): return cut(self.kept) + cut(self.other)  27.3 us
  transfers between devices with their start and end apart: 73, of which 38 were waited for; matrix products, arithmetic and copies ran while one was open for 12% of the time, Pallas kernels for 23%

profile of v3, /device:TPU:0, one launch (start us, length us, event | category | flops | bytes accessed | tf_op | source)
XLA Modules:
  0.0 874.2 jit_solution(10148575668777534920)
XLA Ops:
  17.5 10.9 %multiply_sine_fusion = (f32[2592,192]{1,0:T(8,128)S(1)}, f32[2592,192]{1,0:T(8,128)S(1)}) fusion(f32[192]{0:T(256)} %multiply_exponential_fusion.1, f32[2592]{0:T(1024)S(1)} %fusion.49), kind=kLoop, calls=%fused_computation.11 | loop fusion | flops 497664 | bytes 3992448 | tf_op jit(solution)/shard_map/sin | solution.py:55
  36.5 14.0 %collective-permute-done.1 = bf16[2,672,128]{2,1,0:T(8,128)(2,1)S(1)} collective-permute-done((bf16[2,672,128]{2,1,0:T(8,128)(2,1)S(1)}, bf16[2,672,128]{2,1,0:T(8,128)(2,1)S(1)}, u32[]{:S(2)}, u32[]{:S(2)}) %collective-permute-start.1) | collective-permute-done | bytes 344096 | tf_op jit(solution)/shard_map/ppermute | solution.py:948
  50.5 5.9 collective-permute-done.5
  62.8 9.9 %collective-permute-done.6 = bf16[2,2,672,128]{3,2,0,1:T(8,128)(2,1)S(1)} collective-permute-done((bf16[2,2,672,128]{3,2,0,1:T(8,128)(2,1)S(1)}, bf16[2,2,672,128]{3,2,0,1:T(8,128)(2,1)S(1)}, u32[]{:S(2)}, u32[]{:S(2)}) %collective-permute-start.6) | collective-permute-done | bytes 688160 | tf_op jit(solution)/shard_map/ppermute | solution.py:948
  81.6 11.7 %collective-permute-done.2 = bf16[2,2,672,128]{3,2,0,1:T(8,128)(2,1)S(1)} collective-permute-done((bf16[2,2,672,128]{3,2,0,1:T(8,128)(2,1)S(1)}, bf16[2,2,672,128]{3,2,0,1:T(8,128)(2,1)S(1)}, u32[]{:S(2)}, u32[]{:S(2)}) %collective-permute-start.2) | collective-permute-done | bytes 688160 | tf_op jit(solution)/shard_map/ppermute | solution.py:948
  94.1 25.8 %collective-permute-done.7 = bf16[2,2,2,672,128]{4,3,0,1,2:T(8,128)(2,1)S(1)} collective-permute-done((bf16[2,2,2,672,128]{4,3,0,1,2:T(8,128)(2,1)S(1)}, bf16[2,2,2,672,128]{4,3,0,1,2:T(8,128)(2,1)S(1)}, u32[]{:S(2)}, u32[]{:S(2)}) %collective-permute-start.7) | collective-permute-done | bytes 1376288 | tf_op jit(solution)/shard_map/ppermute | solution.py:948
  130.4 5.7 collective-permute-done.14
  155.7 30.7 %unpack_enc.1 = (bf16[1536,768]{1,0:T(8,128)(2,1)}, bf16[768,2304]{1,0:T(8,128)(2,1)}, bf16[768,768]{1,0:T(8,128)(2,1)}, bf16[768,3072]{1,0:T(8,128)(2,1)}, bf16...) custom-call(s32[1]{0:T(128)} %bitcast.core_ref, bf16[8,1344,128]{2,1,0:T(8,128)(2,1)} %bitcast.436, ...), custom_call_target="tpu_custom_call" | custom-call | bytes 102776832 | tf_op jit(solution)/shard_map/unpack_enc/pallas_call | solution.py:875
  203.9 14.9 %enc_forward.1 = (f32[256,384]{1,0:T(8,128)}, f32[256,768]{1,0:T(8,128)}, bf16[256,2304]{1,0:T(8,128)(2,1)}, bf16[256,768]{1,0:T(8,128)(2,1)}, f32[256,768]{1,0:...) custom-call(bf16[256,1536]{1,0:T(8,128)(2,1)} %pix_ref.3, f32[256,768]{1,0:T(8,128)} %pad_maximum_fusion.17.place_ref, ...), custom_call_target="tpu_custom_call" | custom-call | flops 15000000512 | bytes 20971520 | tf_op jit(solution)/shard_map/enc_forward/pallas_call | solution.py:457
  219.0 10.5 %unpack_dec.1 = (bf16[384,1152]{1,0:T(8,128)(2,1)}, bf16[384,384]{1,0:T(8,128)(2,1)}, bf16[384,1536]{1,0:T(8,128)(2,1)}, bf16[1536,384]{1,0:T(8,128)(2,1)}, bf16...) custom-call(s32[1]{0:T(128)} %bitcast.core_ref, bf16[8,608,128]{2,1,0:T(8,128)(2,1)} %bitcast.440, ...), custom_call_target="tpu_custom_call" | custom-call | bytes 28409856 | tf_op jit(solution)/shard_map/unpack_dec/pallas_call | solution.py:875
  237.4 13.4 %dec_qkv.1 = (f32[2592,384]{1,0:T(8,128)}, bf16[2592,1152]{1,0:T(8,128)(2,1)}) custom-call(s32[256]{0:T(256)} %bitcast.462, f32[256]{0:T(256)} %copy-done.20, f32[256,384]{1,0:T(8,128)} %get-tuple-element.130.latent_ref, f32[2592,384]{1,0:T(8,128)} %pad_maximum_fusion.1.place_ref, f32[2592,128]{1,0:T(8,128)} %pad.32.row_ref.refs_9_, ...), custom_call_target="tpu_custom_call" | custom-call | flops 10000000000 | bytes 16777216 | tf_op jit(solution)/shard_map/dec_qkv/pallas_call | solution.py:142
  250.8 63.5 %dec_attend.1 = (bf16[2592,384]{1,0:T(8,128)(2,1)}, f32[9,8,864]{2,1,0:T(8,128)}) custom-call(bf16[2592,1152]{1,0:T(8,128)(2,1)} %get-tuple-element.144.q_ref.k_ref.v_ref, bf16[2592,1152]{1,0:T(8,128)(2,1)} %get-tuple-element.144.q_ref.k_ref.v_ref, bf16[2592,1152]{1,0:T(8,128)(2,1)} %get-tuple-element.144.q_ref.k_ref.v_ref, ...), custom_call_target="tpu_custom_call" | custom-call | flops 60000002048 | bytes 16777216 | tf_op jit(solution)/shard_map/dec_attend/pallas_call | solution.py:173
  314.3 65.8 %dec_mlp.1 = (bf16[2592,384]{1,0:T(8,128)(2,1)}, f32[2592,384]{1,0:T(8,128)}, f32[6,8,432]{2,1,0:T(8,128)}, f32[384,384]{1,0:T(8,128)}, f32[384,1536]{1,0:T(8,12...) custom-call(f32[2592,384]{1,0:T(8,128)} %get-tuple-element.143.x_ref, ...), custom_call_target="tpu_custom_call" | custom-call | tf_op jit(solution)/shard_map/dec_mlp/pallas_call | solution.py:331
  380.2 8.2 pack_dec.1
  388.9 40.4 %dec_attend_back.3 = (bf16[2592,128]{1,0:T(8,128)(2,1)}, bf16[2592,128]{1,0:T(8,128)(2,1)}, bf16[2592,128]{1,0:T(8,128)(2,1)}) custom-call(bf16[2592,1152]{1,0:T(8,128)(2,1)} %get-tuple-element.144.q_ref.k_ref.v_ref, bf16[2592,1152]{1,0:T(8,128)(2,1)} %get-tuple-element.144.q_ref.k_ref.v_ref, bf16[2592,1152]{1,0:T(8,128)(2,1)} %get-tuple-element.144.q_ref.k_ref.v_ref, ...), custom_call_target="tpu_custom_call" | custom-call | flops 40000000000 | bytes 8388608 | tf_op jit(solution)/shard_map/dec_attend_back/pallas_call | solution.py:245
  437.6 40.3 %dec_attend_back.4 = (bf16[2592,128]{1,0:T(8,128)(2,1)}, bf16[2592,128]{1,0:T(8,128)(2,1)}, bf16[2592,128]{1,0:T(8,128)(2,1)}) custom-call(bf16[2592,1152]{1,0:T(8,128)(2,1)} %get-tuple-element.144.q_ref.k_ref.v_ref, bf16[2592,1152]{1,0:T(8,128)(2,1)} %get-tuple-element.144.q_ref.k_ref.v_ref, bf16[2592,1152]{1,0:T(8,128)(2,1)} %get-tuple-element.144.q_ref.k_ref.v_ref, ...), custom_call_target="tpu_custom_call" | custom-call | flops 40000000000 | bytes 8388608 | tf_op jit(solution)/shard_map/dec_attend_back/pallas_call | solution.py:245
  484.4 40.2 %dec_attend_back.5 = (bf16[2592,128]{1,0:T(8,128)(2,1)}, bf16[2592,128]{1,0:T(8,128)(2,1)}, bf16[2592,128]{1,0:T(8,128)(2,1)}) custom-call(bf16[2592,1152]{1,0:T(8,128)(2,1)} %get-tuple-element.144.q_ref.k_ref.v_ref, bf16[2592,1152]{1,0:T(8,128)(2,1)} %get-tuple-element.144.q_ref.k_ref.v_ref, bf16[2592,1152]{1,0:T(8,128)(2,1)} %get-tuple-element.144.q_ref.k_ref.v_ref, ...), custom_call_target="tpu_custom_call" | custom-call | flops 40000000000 | bytes 8388608 | tf_op jit(solution)/shard_map/dec_attend_back/pallas_call | solution.py:245
  529.9 14.1 %dec_qkv_back.1 = (f32[2592,384]{1,0:T(8,128)}, f32[384,1152]{1,0:T(8,128)}, f32[8,1152]{1,0:T(8,128)}) custom-call(f32[2592,384]{1,0:T(8,128)} %get-tuple-element.143.x_ref, f32[2592,384]{1,0:T(8,128)} %get-tuple-element.190.dx_ref, bf16[2592,128]{1,0:T(8,128)(2,1)} %get-tuple-element.191.refs_0_, bf16[2592,128]{1,0:T(8,128)(2,1)} %get-tuple-element.192.refs_1_, ...), custom_call_target="tpu_custom_call" | custom-call | flops 15000000512 | bytes 8388608 | tf_op jit(solution)/shard_map/dec_qkv_back/pallas_call | solution.py:372
  544.0 17.3 %enc_back_one.1 = (f32[264,768]{1,0:T(8,128)}, f32[8,128]{1,0:T(8,128)}, f32[8,2,560,128]{3,2,1,0:T(8,128)}, f32[8,2,560,128]{3,2,1,0:T(8,128)}, f32[8,2,560,128...) custom-call(s32[1]{0:T(128)} %bitcast.core_ref, ...), custom_call_target="tpu_custom_call" | custom-call | flops 20000000000 | bytes 31457280 | tf_op jit(solution)/shard_map/enc_back_one/pallas_call | solution.py:714
  561.3 17.0 %enc_back_two.1 = (f32[8,128]{1,0:T(8,128)}, f32[8,2,560,128]{3,2,1,0:T(8,128)}, f32[8,2,560,128]{3,2,1,0:T(8,128)}, f32[8,2,560,128]{3,2,1,0:T(8,128)}, f32[8,2...) custom-call(s32[1]{0:T(128)} %bitcast.core_ref, ...), custom_call_target="tpu_custom_call", output_to_operand_aliasing={{1}: (14, {}), {2}: (15, {}), {3}: (16, {}), {4}: (17, {}),... | custom-call | flops 15000000512 | bytes 31457280 | tf_op jit(solution)/shard_map/enc_back_two/pallas_call | solution.py:751
  579.8 6.7 collective-permute-done.32
  586.5 6.6 collective-permute-done.42
  623.0 5.8 dynamic-slice_add_fusion.2
  640.3 17.3 %collective-permute-done.38 = f16[2,2,2,560,128]{4,3,1,0,2:T(8,128)(2,1)} collective-permute-done((f16[2,2,2,560,128]{4,3,1,0,2:T(8,128)(2,1)}, f16[2,2,2,560,128]{4,3,1,0,2:T(8,128)(2,1)}, u32[]{:S(2)}, u32[]{:S(2)}) %collective-permute-start.38) | collective-permute-done | bytes 1146912 | tf_op jit(solution)/shard_map/ppermute | solution.py:948
  670.5 5.9 collective-permute-done.39
  681.8 15.2 %collective-permute-done.40 = f16[2,560,128]{2,1,0:T(8,128)(2,1)S(1)} collective-permute-done((f16[2,560,128]{2,1,0:T(8,128)(2,1)S(1)}, f16[2,560,128]{2,1,0:T(8,128)(2,1)S(1)}, u32[]{:S(2)}, u32[]{:S(2)}) %collective-permute-start.40) | collective-permute-done | bytes 286752 | tf_op jit(solution)/shard_map/ppermute | solution.py:948
  709.0 29.1 %collective-permute-done.54 = f16[2,2,528,128]{3,2,1,0:T(8,128)(2,1)S(1)} collective-permute-done((f16[2,2,528,128]{3,2,1,0:T(8,128)(2,1)S(1)}, f16[2,2,528,128]{3,2,1,0:T(8,128)(2,1)S(1)}, u32[]{:S(2)}, u32[]{:S(2)}) %collective-permute-start.54) | collective-permute-done | bytes 540704 | tf_op jit(solution)/shard_map/ppermute | solution.py:948
  742.8 8.6 collective-permute-done.55
  761.9 9.2 %collective-permute-done.68 = f32[112,128]{1,0:T(8,128)S(1)} collective-permute-done((f32[112,128]{1,0:T(8,128)S(1)}, f32[112,128]{1,0:T(8,128)S(1)}, u32[]{:S(2)}, u32[]{:S(2)}) %collective-permute-start.68) | collective-permute-done | bytes 57376 | tf_op jit(solution)/shard_map/ppermute | solution.py:948
  796.5 29.1 %collective-permute-done.61 = f32[2]{0:T(128)S(1)} collective-permute-done((f32[2]{0:T(128)S(1)}, f32[2]{0:T(128)S(1)}, u32[]{:S(2)}, u32[]{:S(2)}) %collective-permute-start.61) | collective-permute-done | bytes 40 | tf_op jit(solution)/shard_map/ppermute | solution.py:948
  841.7 13.2 %concatenate.31 = f32[3472,128]{1,0:T(8,128)} concatenate(f32[434,128]{1,0:T(8,128)} %get-tuple-element.305, f32[434,128]{1,0:T(8,128)} %get-tuple-element.304, f32[434,128]{1,0:T(8,128)} %get-tuple-element.303, f32[434,128]{1,0:T(8,128)} %get-tuple-element.302, f32[434,128]{1,0:T(8,128)} %get-tuple-element.301, f32[434,128]{1,0:T(8,128)} %get-tuple-element.300, ...), dimensions={0} | concatenate | bytes 3555328 | tf_op jit(solution)/shard_map/concatenate | solution.py:1188
  865.8 5.8 multiply_subtract_fusion
  (382 shorter events, 247.6 us)
Async XLA Ops:
  3.2 27.9 %collective-permute-start = (bf16[672,128]{1,0:T(8,128)(2,1)S(1)}, bf16[672,128]{1,0:T(8,128)(2,1)S(1)}, u32[]{:S(2)}, u32[]{:S(2)}) collective-permute-start(bf16[672,128]{1,0:T(8,128)(2,1)S(1)} %get-tuple-element.297), channel_id=1, source_target_pairs={{0,4},{1,5},{2,6},{3,7},{4,0},{5,1},{6,2},{7,3},{8,12},{9,13},{10,... | collective-permute-start | bytes 516104 | tf_op jit(solution)/shard_map/ppermute | solution.py:948
  7.3 25.8 %collective-permute-start.4 = (bf16[672,128]{1,0:T(8,128)(2,1)S(1)}, bf16[672,128]{1,0:T(8,128)(2,1)S(1)}, u32[]{:S(2)}, u32[]{:S(2)}) collective-permute-start(bf16[672,128]{1,0:T(8,128)(2,1)S(1)} %get-tuple-element.296), channel_id=1, source_target_pairs={{0,4},{1,5},{2,6},{3,7},{4,0},{5,1},{6,2},{7,3},{8,12},{9,13},{10,... | collective-permute-start | bytes 516104 | tf_op jit(solution)/shard_map/ppermute | solution.py:948
  33.2 23.2 %collective-permute-start.5 = (bf16[2,672,128]{2,1,0:T(8,128)(2,1)S(1)}, bf16[2,672,128]{2,1,0:T(8,128)(2,1)S(1)}, u32[]{:S(2)}, u32[]{:S(2)}) collective-permute-start(bf16[2,672,128]{2,1,0:T(8,128)(2,1)S(1)} %pad_maximum_fusion.26), channel_id=1, source_target_pairs={{0,2},{1,3},{2,0},{3,1},{4,6},{5,7},{6,4},{7,5},{8,10},{9,11},{10,... | collective-permute-start | bytes 1032200 | tf_op jit(solution)/shard_map/ppermute | solution.py:948
  33.6 24.6 %collective-permute-start.8 = (bf16[1504,128]{1,0:T(8,128)(2,1)S(1)}, bf16[1504,128]{1,0:T(8,128)(2,1)S(1)}, u32[]{:S(2)}, u32[]{:S(2)}) collective-permute-start(bf16[1504,128]{1,0:T(8,128)(2,1)S(1)} %pad_dynamic-slice_fusion.1), channel_id=1, source_target_pairs={{0,4},{1,5},{2,6},{3,7},{4,0},{5,1},{6,2},{7,3},{8,12},{9,13},{10,... | collective-permute-start | bytes 1155080 | tf_op jit(solution)/shard_map/ppermute | solution.py:948
  62.2 31.1 %collective-permute-start.2 = (bf16[2,2,672,128]{3,2,0,1:T(8,128)(2,1)S(1)}, bf16[2,2,672,128]{3,2,0,1:T(8,128)(2,1)S(1)}, u32[]{:S(2)}, u32[]{:S(2)}) collective-permute-start(bf16[2,2,672,128]{3,2,0,1:T(8,128)(2,1)S(1)} %pad_maximum_fusion.19), channel_id=1, source_target_pairs={{0,1},{1,0},{2,3},{3,2},{4,5},{5,4},{6,7},{7,6},{8,9},{9,8},{10,11... | collective-permute-start | bytes 2064392 | tf_op jit(solution)/shard_map/ppermute | solution.py:948
  72.9 46.9 %collective-permute-start.7 = (bf16[2,2,2,672,128]{4,3,0,1,2:T(8,128)(2,1)S(1)}, bf16[2,2,2,672,128]{4,3,0,1,2:T(8,128)(2,1)S(1)}, u32[]{:S(2)}, u32[]{:S(2)}) collective-permute-start(bf16[2,2,2,672,128]{4,3,0,1,2:T(8,128)(2,1)S(1)} %pad_maximum_fusion.9), channel_id=1, source_target_pairs={{0,1},{1,0},{2,3},{3,2},{4,5},{5,4},{6,7},{7,6},{8,9},{9,8},{10,11... | collective-permute-start | bytes 4128776 | tf_op jit(solution)/shard_map/ppermute | solution.py:948
  78.8 41.7 %collective-permute-start.10 = (bf16[2,2,1504,128]{3,2,1,0:T(8,128)(2,1)S(1)}, bf16[2,2,1504,128]{3,2,1,0:T(8,128)(2,1)S(1)}, u32[]{:S(2)}, u32[]{:S(2)}) collective-permute-start(bf16[2,2,1504,128]{3,2,1,0:T(8,128)(2,1)S(1)} %pad_maximum_fusion.7), channel_id=1, source_target_pairs={{0,2},{1,3},{2,0},{3,1},{4,6},{5,7},{6,4},{7,5},{8,10},{9,11},{10,... | collective-permute-start | bytes 4620296 | tf_op jit(solution)/shard_map/ppermute | solution.py:948
  93.5 28.9 %collective-permute-start.3 = (bf16[2,2,2,672,128]{4,3,0,1,2:T(8,128)(2,1)S(1)}, bf16[2,2,2,672,128]{4,3,0,1,2:T(8,128)(2,1)S(1)}, u32[]{:S(2)}, u32[]{:S(2)}) collective-permute-start(bf16[2,2,2,672,128]{4,3,0,1,2:T(8,128)(2,1)S(1)} %pad_maximum_fusion.8), channel_id=1, source_target_pairs={{0,16},{1,17},{2,18},{3,19},{4,20},{5,21},{6,22},{7,23},{8,24},{9,... | collective-permute-start | bytes 4128776 | tf_op jit(solution)/shard_map/ppermute | solution.py:948
  120.5 31.1 %collective-permute-start.12 = (bf16[8,1344,128]{2,1,0:T(8,128)(2,1)S(1)}, bf16[8,1344,128]{2,1,0:T(8,128)(2,1)S(1)}, u32[]{:S(2)}, u32[]{:S(2)}) collective-permute-start(bf16[8,1344,128]{2,1,0:T(8,128)(2,1)S(1)} %bitcast.433), channel_id=1, source_target_pairs={{0,8},{1,9},{2,10},{3,11},{4,12},{5,13},{6,14},{7,15},{8,0},{9,1},... | collective-permute-start | bytes 8257544 | tf_op jit(solution)/shard_map/ppermute | solution.py:948
  122.4 29.3 %collective-permute-start.13 = (bf16[8,1504,128]{2,1,0:T(8,128)(2,1)S(1)}, bf16[8,1504,128]{2,1,0:T(8,128)(2,1)S(1)}, u32[]{:S(2)}, u32[]{:S(2)}) collective-permute-start(bf16[8,1504,128]{2,1,0:T(8,128)(2,1)S(1)} %bitcast.431), channel_id=1, source_target_pairs={{0,8},{1,9},{2,10},{3,11},{4,12},{5,13},{6,14},{7,15},{8,0},{9,1},... | collective-permute-start | bytes 9240584 | tf_op jit(solution)/shard_map/ppermute | solution.py:948
  124.5 27.1 %collective-permute-start.11 = (bf16[8,1344,128]{2,1,0:T(8,128)(2,1)S(1)}, bf16[8,1344,128]{2,1,0:T(8,128)(2,1)S(1)}, u32[]{:S(2)}, u32[]{:S(2)}) collective-permute-start(bf16[8,1344,128]{2,1,0:T(8,128)(2,1)S(1)} %bitcast.435), channel_id=1, source_target_pairs={{0,8},{1,9},{2,10},{3,11},{4,12},{5,13},{6,14},{7,15},{8,0},{9,1},... | collective-permute-start | bytes 8257544 | tf_op jit(solution)/shard_map/ppermute | solution.py:948
  147.2 42.1 %collective-permute-start.16 = (bf16[2,2,304,128]{3,2,1,0:T(8,128)(2,1)}, bf16[2,2,304,128]{3,2,1,0:T(8,128)(2,1)}, u32[]{:S(2)}, u32[]{:S(2)}) collective-permute-start(bf16[2,2,304,128]{3,2,1,0:T(8,128)(2,1)} %pad_maximum_fusion.27), channel_id=1, source_target_pairs={{0,16},{1,17},{2,18},{3,19},{4,20},{5,21},{6,22},{7,23},{8,24},{9,... | collective-permute-start | bytes 933896 | tf_op jit(solution)/shard_map/ppermute | solution.py:948
  388.3 41.0 %collective-permute-start.25 = (f32[8,2,288,128]{3,2,1,0:T(8,128)}, f32[8,2,288,128]{3,2,1,0:T(8,128)}, u32[]{:S(2)}, u32[]{:S(2)}) collective-permute-start(f32[8,2,288,128]{3,2,1,0:T(8,128)} %get-tuple-element.163), channel_id=1, source_target_pairs={{0,8},{1,9},{2,10},{3,11},{4,12},{5,13},{6,14},{7,15},{8,0},{9,1},... | collective-permute-start | bytes 7077896 | tf_op jit(solution)/shard_map/ppermute | solution.py:948
  388.7 43.7 %collective-permute-start.24 = (f32[8,2,304,128]{3,2,1,0:T(8,128)}, f32[8,2,304,128]{3,2,1,0:T(8,128)}, u32[]{:S(2)}, u32[]{:S(2)}) collective-permute-start(f32[8,2,304,128]{3,2,1,0:T(8,128)} %get-tuple-element.160), channel_id=1, source_target_pairs={{0,8},{1,9},{2,10},{3,11},{4,12},{5,13},{6,14},{7,15},{8,0},{9,1},... | collective-permute-start | bytes 7471112 | tf_op jit(solution)/shard_map/ppermute | solution.py:948
  435.4 42.4 %collective-permute-start.27 = (f32[2,2,2,288,128]{4,3,2,1,0:T(8,128)}, f32[2,2,2,288,128]{4,3,2,1,0:T(8,128)S(1)}, u32[]{:S(2)}, u32[]{:S(2)}) collective-permute-start(f32[2,2,2,288,128]{4,3,2,1,0:T(8,128)} %get-tuple-element.171), channel_id=1, source_target_pairs={{0,16},{1,17},{2,18},{3,19},{4,20},{5,21},{6,22},{7,23},{8,24},{9,... | collective-permute-start | bytes 3538952 | tf_op jit(solution)/shard_map/ppermute | solution.py:948
  435.8 45.2 %collective-permute-start.26 = (f32[2,2,2,304,128]{4,3,2,1,0:T(8,128)}, f32[2,2,2,304,128]{4,3,2,1,0:T(8,128)}, u32[]{:S(2)}, u32[]{:S(2)}) collective-permute-start(f32[2,2,2,304,128]{4,3,2,1,0:T(8,128)} %get-tuple-element.169), channel_id=1, source_target_pairs={{0,1},{1,0},{2,3},{3,2},{4,5},{5,4},{6,7},{7,6},{8,9},{9,8},{10,11... | collective-permute-start | bytes 3735560 | tf_op jit(solution)/shard_map/ppermute | solution.py:948
  482.4 42.2 %collective-permute-start.29 = (f32[2,2,288,128]{3,2,1,0:T(8,128)}, f32[2,2,288,128]{3,2,1,0:T(8,128)S(1)}, u32[]{:S(2)}, u32[]{:S(2)}) collective-permute-start(f32[2,2,288,128]{3,2,1,0:T(8,128)} %get-tuple-element.179), channel_id=1, source_target_pairs={{0,1},{1,0},{2,3},{3,2},{4,5},{5,4},{6,7},{7,6},{8,9},{9,8},{10,11... | collective-permute-start | bytes 1769480 | tf_op jit(solution)/shard_map/ppermute | solution.py:948
  482.8 43.8 %collective-permute-start.28 = (f32[2,2,304,128]{3,2,1,0:T(8,128)S(1)}, f32[2,2,304,128]{3,2,1,0:T(8,128)S(1)}, u32[]{:S(2)}, u32[]{:S(2)}) collective-permute-start(f32[2,2,304,128]{3,2,1,0:T(8,128)S(1)} %get-tuple-element.178), channel_id=1, source_target_pairs={{0,16},{1,17},{2,18},{3,19},{4,20},{5,21},{6,22},{7,23},{8,24},{9,... | collective-permute-start | bytes 1867784 | tf_op jit(solution)/shard_map/ppermute | solution.py:948
  526.7 34.5 %collective-permute-start.31 = (f32[2,288,128]{2,1,0:T(8,128)S(1)}, f32[2,288,128]{2,1,0:T(8,128)S(1)}, u32[]{:S(2)}, u32[]{:S(2)}) collective-permute-start(f32[2,288,128]{2,1,0:T(8,128)S(1)} %get-tuple-element.206), channel_id=1, source_target_pairs={{0,4},{1,5},{2,6},{3,7},{4,0},{5,1},{6,2},{7,3},{8,12},{9,13},{10,... | collective-permute-start | bytes 884744 | tf_op jit(solution)/shard_map/ppermute | solution.py:948
  529.8 31.5 %collective-permute-start.30 = (f32[2,304,128]{2,1,0:T(8,128)S(1)}, f32[2,304,128]{2,1,0:T(8,128)S(1)}, u32[]{:S(2)}, u32[]{:S(2)}) collective-permute-start(f32[2,304,128]{2,1,0:T(8,128)S(1)} %get-tuple-element.205), channel_id=1, source_target_pairs={{0,4},{1,5},{2,6},{3,7},{4,0},{5,1},{6,2},{7,3},{8,12},{9,13},{10,... | collective-permute-start | bytes 933896 | tf_op jit(solution)/shard_map/ppermute | solution.py:948
  593.0 73.1 %collective-permute-start.52 = (f32[8,2,528,128]{3,2,1,0:T(8,128)}, f32[8,2,528,128]{3,2,1,0:T(8,128)}, u32[]{:S(2)}, u32[]{:S(2)}) collective-permute-start(f32[8,2,528,128]{3,2,1,0:T(8,128)} %get-tuple-element.232), channel_id=1, source_target_pairs={{0,8},{1,9},{2,10},{3,11},{4,12},{5,13},{6,14},{7,15},{8,0},{9,1},... | collective-permute-start | bytes 12976136 | tf_op jit(solution)/shard_map/ppermute | solution.py:948
  622.5 75.1 %collective-permute-start.47 = (f32[8,2,560,128]{3,2,1,0:T(8,128)}, f32[8,2,560,128]{3,2,1,0:T(8,128)}, u32[]{:S(2)}, u32[]{:S(2)}) collective-permute-start(f32[8,2,560,128]{3,2,1,0:T(8,128)} %get-tuple-element.229), channel_id=1, source_target_pairs={{0,8},{1,9},{2,10},{3,11},{4,12},{5,13},{6,14},{7,15},{8,0},{9,1},... | collective-permute-start | bytes 13762568 | tf_op jit(solution)/shard_map/ppermute | solution.py:948
  630.1 27.6 %collective-permute-start.38 = (f16[2,2,2,560,128]{4,3,1,0,2:T(8,128)(2,1)}, f16[2,2,2,560,128]{4,3,1,0,2:T(8,128)(2,1)}, u32[]{:S(2)}, u32[]{:S(2)}) collective-permute-start(f16[2,2,2,560,128]{4,3,1,0,2:T(8,128)(2,1)} %fusion.13), channel_id=1, source_target_pairs={{0,1},{1,0},{2,3},{3,2},{4,5},{5,4},{6,7},{7,6},{8,9},{9,8},{10,11... | collective-permute-start | bytes 3440648 | tf_op jit(solution)/shard_map/ppermute | solution.py:948
  635.7 28.5 %collective-permute-start.43 = (f16[2,2,2,560,128]{4,3,1,0,2:T(8,128)(2,1)}, f16[2,2,2,560,128]{4,3,1,0,2:T(8,128)(2,1)}, u32[]{:S(2)}, u32[]{:S(2)}) collective-permute-start(f16[2,2,2,560,128]{4,3,1,0,2:T(8,128)(2,1)} %fusion.14), channel_id=1, source_target_pairs={{0,16},{1,17},{2,18},{3,19},{4,20},{5,21},{6,22},{7,23},{8,24},{9,... | collective-permute-start | bytes 3440648 | tf_op jit(solution)/shard_map/ppermute | solution.py:948
  669.4 32.0 %collective-permute-start.53 = (f16[2,2,2,528,128]{4,3,1,0,2:T(8,128)(2,1)S(1)}, f16[2,2,2,528,128]{4,3,1,0,2:T(8,128)(2,1)S(1)}, u32[]{:S(2)}, u32[]{:S(2)}) collective-permute-start(f16[2,2,2,528,128]{4,3,1,0,2:T(8,128)(2,1)S(1)} %fusion.20), channel_id=1, source_target_pairs={{0,16},{1,17},{2,18},{3,19},{4,20},{5,21},{6,22},{7,23},{8,24},{9,... | collective-permute-start | bytes 3244040 | tf_op jit(solution)/shard_map/ppermute | solution.py:948
  679.8 23.3 %collective-permute-start.45 = (f16[2,560,128]{2,1,0:T(8,128)(2,1)S(1)}, f16[2,560,128]{2,1,0:T(8,128)(2,1)S(1)}, u32[]{:S(2)}, u32[]{:S(2)}) collective-permute-start(f16[2,560,128]{2,1,0:T(8,128)(2,1)S(1)} %get-tuple-element.289), channel_id=1, source_target_pairs={{0,4},{1,5},{2,6},{3,7},{4,0},{5,1},{6,2},{7,3},{8,12},{9,13},{10,... | collective-permute-start | bytes 860168 | tf_op jit(solution)/shard_map/ppermute | solution.py:948
  700.5 40.8 %collective-permute-start.48 = (f16[2,2,2,560,128]{4,3,2,1,0:T(8,128)(2,1)S(1)}, f16[2,2,2,560,128]{4,3,2,1,0:T(8,128)(2,1)S(1)}, u32[]{:S(2)}, u32[]{:S(2)}) collective-permute-start(f16[2,2,2,560,128]{4,3,2,1,0:T(8,128)(2,1)S(1)} %get-tuple-element.252), channel_id=1, source_target_pairs={{0,1},{1,0},{2,3},{3,2},{4,5},{5,4},{6,7},{7,6},{8,9},{9,8},{10,11... | collective-permute-start | bytes 3440648 | tf_op jit(solution)/shard_map/ppermute | solution.py:948
  701.8 36.3 %collective-permute-start.54 = (f16[2,2,528,128]{3,2,1,0:T(8,128)(2,1)S(1)}, f16[2,2,528,128]{3,2,1,0:T(8,128)(2,1)S(1)}, u32[]{:S(2)}, u32[]{:S(2)}) collective-permute-start(f16[2,2,528,128]{3,2,1,0:T(8,128)(2,1)S(1)} %get-tuple-element.270), channel_id=1, source_target_pairs={{0,1},{1,0},{2,3},{3,2},{4,5},{5,4},{6,7},{7,6},{8,9},{9,8},{10,11... | collective-permute-start | bytes 1622024 | tf_op jit(solution)/shard_map/ppermute | solution.py:948
  703.1 48.4 %collective-permute-start.46 = (f32[560,128]{1,0:T(8,128)S(1)}, f32[560,128]{1,0:T(8,128)S(1)}, u32[]{:S(2)}, u32[]{:S(2)}) collective-permute-start(f32[560,128]{1,0:T(8,128)S(1)} %fusion.43), channel_id=1, source_target_pairs={{0,2},{1,3},{2,0},{3,1},{4,6},{5,7},{6,4},{7,5},{8,10},{9,11},{10,... | collective-permute-start | bytes 860168 | tf_op jit(solution)/shard_map/ppermute | solution.py:948
  789.5 46.6 %collective-permute-start.64 = (f32[2096,128]{1,0:T(8,128)S(1)}, f32[2096,128]{1,0:T(8,128)}, u32[]{:S(2)}, u32[]{:S(2)}) collective-permute-start(f32[2096,128]{1,0:T(8,128)S(1)} %get-tuple-element.248), channel_id=1, source_target_pairs={{0,16},{1,17},{2,18},{3,19},{4,20},{5,21},{6,22},{7,23},{8,24},{9,... | collective-permute-start | bytes 3219464 | tf_op jit(solution)/shard_map/ppermute | solution.py:948
  790.7 44.2 %collective-permute-start.71 = (f32[2,2,2,112,128]{4,3,2,1,0:T(8,128)S(1)}, f32[2,2,2,112,128]{4,3,2,1,0:T(8,128)}, u32[]{:S(2)}, u32[]{:S(2)}) collective-permute-start(f32[2,2,2,112,128]{4,3,2,1,0:T(8,128)S(1)} %pad_maximum_fusion.24), channel_id=1, source_target_pairs={{0,16},{1,17},{2,18},{3,19},{4,20},{5,21},{6,22},{7,23},{8,24},{9,... | collective-permute-start | bytes 1376264 | tf_op jit(solution)/shard_map/ppermute | solution.py:948
  795.5 30.1 %collective-permute-start.61 = (f32[2]{0:T(128)S(1)}, f32[2]{0:T(128)S(1)}, u32[]{:S(2)}, u32[]{:S(2)}) collective-permute-start(f32[2]{0:T(128)S(1)} %fusion.68), channel_id=1, source_target_pairs={{0,16},{1,17},{2,18},{3,19},{4,20},{5,21},{6,22},{7,23},{8,24},{9,... | collective-permute-start | bytes 32 | tf_op jit(solution)/shard_map/ppermute | solution.py:948
  (75 other events, 770.1 us)

commit v4 on v3

--- a/solution.py
+++ b/solution.py
@@ -650,7 +650,7 @@
         self.wide, self.narrow, self.sections = wide, narrow, sections
         self.spans = [-(-(rows + (0 if rows % 8 == 0 else 7)) // 8) * 8 for unused, rows in sections]
         self.parts = [-(-span // (narrow * 16)) * 16 for span in self.spans]
-        self.starts = [sum(self.parts[:i]) for i in range(len(sections))]
+        self.starts = [sum(self.parts[i + 1 :]) for i in range(len(sections))]
         rows = sum(self.parts)
         step = -(-rows // (chunks * 16)) * 16
         self.chunks = [min(step, rows - i * step) for i in range(chunks)]
@@ -762,7 +762,7 @@
         cost_estimate=pl.CostEstimate(flops=15 * 10**9, bytes_accessed=30 << 20, transcendentals=0),
         name="enc_back_two",
     )(core, dx1, pixels, e0, qkv, a, *marks, vec, g_qkv, g_one, wq, wo, top, *out)
-    return out[:chunks], out[chunks:], jnp.max(top)
+    return out[:chunks], out[chunks:], top
 
 
 def table(shapes, row=0):
@@ -780,53 +780,53 @@
 
 def split_rows(shard, shares, note):
     out, place, first = [], 0, 0
-    for i, share in enumerate(shares):
-        rows = -(-shard * share // (100 * 16)) * 16
+    for i in range(len(shares) + 1):
+        rows = shard * shares[i] / 100 if i < len(shares) else (shard - first) / 4
+        rows = math.ceil(rows / 16) * 16
         used = rows - 1 if note and i == 0 else rows
         out.append((place, first, 4, rows, used))
         place, first = place + 4 * rows, first + 4 * used
-    if first < shard:
-        rows = -(-(shard - first) // 32) * 16
-        out.append((place, first, 2, rows, rows))
     return out
 
 
-def unpack_kernel(pieces, groups, shard, wide, core_ref, *refs):
+def unpack_kernel(pieces, groups, leads, ways, span, wide, mine_ref, *refs):
     mats = [p for p in pieces if p[1] > 1]
-    count = len(groups)
-    own, other, refs = refs[:count], refs[count : 2 * count], refs[2 * count :]
+    sources = [refs[4 * g : 4 * g + 4] for g in range(len(groups))]
+    refs = refs[4 * len(groups) :]
     outs, vec_ref = refs[: len(mats)], refs[len(mats)]
     buf, lin, in_sem, out_sem = refs[len(mats) + 1 : len(mats) + 5]
     stages = refs[len(mats) + 5 :]
-    core = core_ref[0]
-    plan, size = [], 0
-    for g, (place, first, parts, rows, used) in enumerate(groups):
+    bits = wide.bit_length()
+    plans, size = [], 0
+    for (place, first, parts, rows, used), lead in zip(groups, leads):
+        plan = []
         for i in range(parts):
-            a, b = first + i * used, min(first + (i + 1) * used, shard)
+            a, b = first + i * used, min(first + (i + 1) * used, span)
             if a < b:
-                plan.append((g, i, rows, size, a, b - a))
+                plan.append((i // 2, i % 2, lead, rows, size, a, b - a))
                 size += rows
-
-    def fetch(sources, s, entry):
-        g, i, rows, to, at, used = entry
-        at_source = (i % 2) * rows if groups[g][2] == 4 else 0
-        return pltpu.make_async_copy(
-            sources[g].at[s, pl.ds(at_source, rows)], buf.at[s, pl.ds(to, rows)], in_sem.at[s]
-        )
-
-    for s in range(wide):
-        for c in range(2):
-
-            @pl.when(core == c)
-            def _():
-                for entry in plan:
-                    of = entry[1] // 2 if groups[entry[0]][2] == 4 else entry[1]
-                    fetch(own if of == c else other, s, entry).start()
+        plans.append(plan)
+
+    for g, (plan, (last, way)) in enumerate(zip(plans, ways)):
+        for core in range(2):
+            for side in range(2):
+
+                @pl.when((mine_ref[0] == core) & (mine_ref[1 + g] == side))
+                def _():
+                    for s in range(wide):
+                        for c, y, low, rows, to, at, count in plan:
+                            index = [s >> (bits - 2 - j) & 1 for j in range(bits - 1)] + [y]
+                            source = sources[g][2 * (c != core) + (index[last] != side)]
+                            index = sum(index[j] << (len(way) - 1 - i) for i, j in enumerate(way))
+                            pltpu.make_async_copy(
+                                source.at[index, pl.ds(low, rows)], buf.at[s, pl.ds(to, rows)], in_sem.at[s]
+                            ).start()
 
     for s in range(wide):
         pltpu.make_async_copy(buf.at[s, pl.ds(0, size)], buf.at[s, pl.ds(0, size)], in_sem.at[s]).wait()
-        for g, i, rows, to, at, used in plan:
-            lin[pl.ds(s * shard + at, used), :] = buf[s, pl.ds(to, rows), :].astype(F)[:used]
+        for plan in plans:
+            for c, y, low, rows, to, at, count in plan:
+                lin[pl.ds(s * span + at, count), :] = buf[s, pl.ds(to, rows), :].astype(F)[:count]
 
     vec_ref[...] = jnp.zeros_like(vec_ref)
     v = 0
@@ -863,7 +863,7 @@
             store(j, j % 2).wait()
 
 
-def unpack_flat(own, other, groups, shard, wide, core, shapes, name):
+def unpack_flat(arrays, groups, leads, ways, mine, span, wide, shapes, name):
     pieces = table(shapes)
     mats = [s for s in shapes if len(s) == 2]
     vectors = [s for s in shapes if len(s) == 1]
@@ -873,18 +873,18 @@
     stages = [pltpu.VMEM((2, job_rows(s[0], s[1] // 128, 1152), s[1]), B) for s in mats]
     room = groups[-1][0] + groups[-1][2] * groups[-1][3]
     return pl.pallas_call(
-        functools.partial(unpack_kernel, pieces, groups, shard, wide),
-        in_specs=[pl.BlockSpec(memory_space=pltpu.SMEM)] + [hbm] * (2 * len(groups)),
+        functools.partial(unpack_kernel, pieces, groups, leads, ways, span, wide),
+        in_specs=[pl.BlockSpec(memory_space=pltpu.SMEM)] + [hbm] * len(arrays),
         out_specs=[hbm] * len(mats) + [pl.BlockSpec(memory_space=pltpu.VMEM)],
         out_shape=[jax.ShapeDtypeStruct(s, B) for s in mats] + [jax.ShapeDtypeStruct((count, width), F)],
         scratch_shapes=[
-            pltpu.VMEM((wide, room, 128), B), pltpu.VMEM((wide * shard, 128), F),
+            pltpu.VMEM((wide, room, 128), B), pltpu.VMEM((wide * span, 128), F),
             pltpu.SemaphoreType.DMA((wide,)), pltpu.SemaphoreType.DMA((2,)),
         ] + stages,
         compiler_params=pltpu.CompilerParams(vmem_limit_bytes=VMEM_LIMIT),
-        cost_estimate=pl.CostEstimate(flops=0, bytes_accessed=wide * shard * 1536, transcendentals=0),
+        cost_estimate=pl.CostEstimate(flops=0, bytes_accessed=wide * span * 1536, transcendentals=0),
         name=name,
-    )(core, *own, *other)
+    )(mine, *arrays)
 
 
 def pack_kernel(pieces, segments, core_ref, *refs):
@@ -947,71 +947,77 @@
         pairs = [(i, i ^ mask) for i in range(self.narrow * self.wide)]
         return lax.ppermute(value, AXES, pairs)
 
-    def everyone(self, value, how):
-        for bit in [self.core, self.x, self.y] + self.upper:
-            value = how(value, self.swap(value, bit))
+    def everyone(self, value, bits):
+        for bit in bits:
+            value = value + self.swap(value, bit)
         return value
 
-    def scale(self, top):
-        count = self.narrow * self.wide
-        return 32768.0 / (count * jnp.maximum(self.everyone(top, jnp.maximum), 1e-30))
-
-    def gather(self, value, axes, order):
-        group = Group(self, value, axes, order)
+    def gather(self, value, order):
+        group = Group(self, value, order)
         while group.order:
             group.step()
         return group.value
 
-    def scatter_parts(self, kept, other, scale):
+    def scatter_parts(self, kept, other, bound=None):
         axes = self.wide_bits + [self.y]
-        parts = []
+        parts, orders = [], [[self.x, self.y] + self.upper, [self.y, self.x] + self.upper]
         for i, (one, two) in enumerate(zip(kept, other)):
-            first = [self.x, self.y] if i % 2 == 0 else [self.y, self.x]
-            shape = (2,) * len(axes) + one.shape[2:]
-            parts.append(Part(self, one.reshape(shape), two.reshape(shape), axes, first + self.upper, scale))
+            one, two = (v.reshape((2,) * len(axes) + v.shape[2:]) for v in (one, two))
+            parts.append(Part(self, one, two, axes, orders[i % 2], bound))
         return parts
 
 
 class Group:
-    def __init__(self, links, value, axes, order):
-        self.links, self.value, self.axes, self.order, self.have = links, value, axes, list(order), []
+    def __init__(self, links, value, order):
+        self.links, self.value, self.order, self.have = links, value, list(order), []
 
     def step(self):
         bit = self.order.pop(0)
         other = self.links.swap(self.value, bit)
         low = self.links.mine(bit) == 0
-        self.have.append(bit)
-        place = [b for b in self.axes if b in self.have].index(bit)
-        pair = [jnp.where(low, self.value, other), jnp.where(low, other, self.value)]
-        self.value = jnp.stack(pair, axis=place)
+        self.have.insert(0, bit)
+        self.value = jnp.stack([jnp.where(low, self.value, other), jnp.where(low, other, self.value)])
 
 
 class Part:
-    def __init__(self, links, kept, other, axes, order, scale):
+    def __init__(self, links, kept, other, axes, order, bound):
         self.links, self.kept, self.other, self.axes, self.order = links, kept, other, list(axes), list(order)
-        self.scale = scale
+        self.bound, self.rows, self.received = bound, kept.shape[-2], None
 
     def away(self):
+        self.arrive()
         bit = self.order[0]
         self.place, self.index = self.axes.index(bit), self.links.mine(bit)
         value = self.take(1 - self.index)
-        return value if len(self.order) == 1 or self.scale is None else (value * self.scale).astype(jnp.float16)
+        if self.bound is None or len(self.order) == 1:
+            return value
+        power = jnp.clip(jnp.floor(14.0 - jnp.log2(jnp.maximum(self.bound, 1e-30))), -100.0, 100.0)
+        note = jnp.broadcast_to(power, value.shape[:-2] + (8, 128))
+        return jnp.concatenate([value * jnp.exp2(power), note], axis=-2).astype(jnp.float16)
 
     def take(self, index):
-        cut = lambda value: lax.dynamic_index_in_dim(value, index, self.place, keepdims=False)
+        cut = lambda value: lax.dynamic_index_in_dim(value, index, self.place, keepdims=False)[..., : self.rows, :]
         return cut(self.kept) + cut(self.other)
 
     def exchange(self, away):
         bit = self.order.pop(0)
-        received = self.links.swap(away, bit)
+        self.kept, self.received = self.take(self.index), self.links.swap(away, bit)
+        self.axes.pop(self.place)
+
+    def arrive(self, token=()):
+        if self.received is None:
+            return
+        received, self.received = after(self.received, *token), None
         if received.dtype == jnp.float16:
-            received = received.astype(F) * (1.0 / self.scale)
-        self.kept, self.other = self.take(self.index), received
-        self.axes.pop(self.place)
+            power = received[(0,) * (received.ndim - 2) + (self.rows, 0)].astype(F)
+            received = received[..., : self.rows, :].astype(F) * jnp.exp2(-power)
+            self.bound = self.bound + jnp.exp2(15.0 - power)
+        self.other = received
 
     def finish(self):
         while self.order:
             self.exchange(self.away())
+        self.arrive()
         return self.kept + self.other
 
 
@@ -1019,49 +1025,41 @@
     return lax.optimization_barrier((value,) + others)[0]
 
 
-def gather_groups(shard, groups, orders, note, links):
-    unused, first, parts, rows, used = groups[-1]
-    shard = jnp.pad(shard, ((0, first + parts * used - shard.shape[0]), (0, 0)))
-    out = []
-    for (unused, first, parts, rows, used), order in zip(groups, orders):
-        part = links.mine(links.core) if parts == 2 else links.mine(links.core) * 2 + links.mine(links.y)
-        value = lax.dynamic_slice_in_dim(shard, first + part * used, used)
-        if used < rows:
-            value = jnp.concatenate([value, note])
-        out.append(Group(links, value, links.wide_bits + ([links.y] if parts == 4 else []), order))
-    return out
-
-
-def gathered(groups, links):
-    own = [g.value.reshape(links.wide, -1, 128) for g in groups]
-    return own, [links.swap(v, links.core) for v in own]
-
-
 def gather_params(enc, dec, note, links):
-    y_last, x_last = links.upper + [links.x, links.y], links.upper + [links.y, links.x]
-    enc_rows, dec_rows = split_rows(enc.shape[0], (8, 8), False), split_rows(dec.shape[0], (13, 13), True)
-    enc_groups = gather_groups(
-        enc, enc_rows, (y_last, x_last, links.upper[:-1] + [links.x] + links.upper[-1:]), note, links
-    )
-    one, two, three = enc_groups
-    dec_groups = gather_groups(dec, dec_rows, (x_last, y_last), note, links)
-    for g in (one, two):
-        g.step()
-    three.value = after(three.value, one.value, two.value)
-    while one.order:
-        for g in dec_groups:
-            g.value = after(g.value, one.value, two.value)
-        for g in (one, two, three):
-            if g.order:
-                g.step()
-        for g in dec_groups:
-            g.step()
-    return (*gathered(enc_groups, links), enc_rows), dec_groups, dec_rows
+    orders = (
+        links.upper[:-1] + [links.x, links.y] + links.upper[-1:],
+        links.upper + [links.x, links.y], links.upper + [links.y, links.x],
+    )
+    tables = split_rows(enc.shape[0], (8.5, 8), False), split_rows(dec.shape[0], (8.5, 8), True)
+    part = links.mine(links.core) * 2 + links.mine(links.y)
+    padded = [
+        jnp.pad(v, ((0, t[-1][1] + 4 * t[-1][4] - v.shape[0]), (0, 0))) for v, t in zip((enc, dec), tables)
+    ]
+    arrays, ways, mine = [], [], [links.mine(links.core)]
+    for g, order in enumerate(orders):
+        pieces = []
+        for v, t in zip(padded, tables):
+            unused, first, parts, rows, used = t[g]
+            pieces.append(lax.dynamic_slice_in_dim(v, first + part * used, used))
+            if used < rows:
+                pieces.append(note)
+        group = Group(links, jnp.concatenate(pieces), order)
+        while len(group.order) > 1:
+            group.step()
+        last = group.order[0]
+        both = [group.value, links.swap(group.value, last)]
+        both += [links.swap(v, links.core) for v in both]
+        arrays += [v.reshape((-1,) + v.shape[-2:]) for v in both]
+        bits = links.wide_bits + [links.y]
+        ways.append((bits.index(last), tuple(bits.index(b) for b in group.have)))
+        mine.append(links.mine(last))
+    at = tables[0][0][3] + tables[1][0][4]
+    notes = sum(jnp.sum(v[:, at, :2].astype(F), axis=0) for v in arrays[:4])
+    return arrays, tables, tuple(ways), jnp.stack(mine).astype(jnp.int32), notes
 
 
 def join_shard(piece, links):
-    axes = [links.core, links.y]
-    return links.gather(piece, axes, [links.y, links.core]).reshape(-1, 128)
+    return links.gather(piece, [links.y, links.core])
 
 
 def adamw_update(master, gradient, moment_one, moment_two, clip_scale):
@@ -1087,19 +1085,13 @@
 
     here = jnp.sum(counted).astype(jnp.int32)
     note = jnp.pad(jnp.stack([here // 64, here % 64]), (0, 126))[None, :].astype(B)
-    enc_parts, dec_groups, dec_rows = gather_params(
+    arrays, tables, ways, sides, notes = gather_params(
         params_enc.astype(B).reshape(-1, 128), params_dec.astype(B).reshape(-1, 128), note, links
     )
-    *enc_mats, enc_vec = unpack_flat(*enc_parts, enc_shard, links.wide, core, ENC_SHAPES, "unpack_enc")
-    for g in dec_groups:
-        g.value = after(g.value, enc_vec)
-        while g.order:
-            g.step()
-    dec_own, dec_other = gathered(dec_groups, links)
-    last = dec_rows[0][3] - 1
-    notes = jnp.stack([v[0].reshape(links.wide, 2, -1, 128)[:, :, last, :2] for v in (dec_own, dec_other)])
-    notes = notes.astype(F)
-    masked_count = jnp.sum(notes[..., 0]) * 64.0 + jnp.sum(notes[..., 1])
+    *enc_mats, enc_vec = unpack_flat(
+        arrays, tables[0], (0, 0, 0), ways, sides, enc_shard, links.wide, ENC_SHAPES, "unpack_enc"
+    )
+    masked_count = notes[0] * 64.0 + notes[1]
     cotangent = 1.0 / masked_count
 
     segment, clip_place, shown_flag, counted = (
@@ -1118,9 +1110,9 @@
     slot_marks = marks_of(slot_segment)
 
     latent, *saved = enc_forward(vis_pixels, sinusoid(slot_place, D), *slot_marks, enc_vec, enc_mats)
-    dec_own = [after(v, latent) for v in dec_own]
+    arrays[0] = after(arrays[0], latent)
     *dec_mats, dec_vec = unpack_flat(
-        dec_own, dec_other, dec_rows, dec_shard, links.wide, core, DEC_SHAPES, "unpack_dec"
+        arrays, tables[1], tuple(t[3] for t in tables[0]), ways, sides, dec_shard, links.wide, DEC_SHAPES, "unpack_dec"
     )
     w_qkv, w_out, w_up, w_down, w_head = dec_mats
     bias = jnp.concatenate([dec_vec[3, :DD], jnp.zeros((DD,), F), dec_vec[4, :DD]])
@@ -1140,7 +1132,7 @@
     )
     back = lambda da, h: attend_back(qkv, q_marks, k_marks, da, lse, dd, h)
     da, away = lax.optimization_barrier((da, away))
-    late = links.scatter_parts(kept, [links.swap(v, links.core) for v in away], None)
+    late = links.scatter_parts(kept, [links.swap(v, links.core) for v in away])
     dqkv = [back(da, 0)]
     for h in (1, 2):
         sent = [part.away() for part in late]
@@ -1157,7 +1149,7 @@
     early = table(DEC_SHAPES[:6])
     early_count = early[-1][0] + early[-1][2]
     flat = Flat(
-        [(0, enc_shard), (enc_shard * links.wide, -(-early_count // links.wide))], links.wide, links.narrow, 4
+        [(0, enc_shard), (enc_shard * links.wide, -(-early_count // (8 * links.wide)) * 8)], links.wide, links.narrow, 2
     )
     dx1, top, out = enc_back_one(core, visible, slot_live, dx0, saved, enc_vec, enc_mats, flat)
     sent = [part.away() for part in late]
@@ -1167,30 +1159,44 @@
     )
     for part, value in zip(late, sent):
         part.exchange(value)
+    beside = links.swap(top, links.core)
+    first = [links.swap(after(v, beside), links.core) for v in away[:1]]
+    second = [links.swap(after(v, *first), links.core) for v in away[1:]]
+    parts = links.scatter_parts(kept, first + second, jnp.max(top + beside))
+    for unused in range(len(parts[0].order)):
+        for part in parts:
+            part.exchange(part.away())
     piece_dec = jnp.concatenate([part.finish() for part in late])
-    first = [links.swap(v, links.core) for v in away[:2]]
-    second = [links.swap(after(v, *first), links.core) for v in away[2:]]
-    parts = links.scatter_parts(kept, first + second, links.scale(top))
-    piece = jnp.concatenate([part.finish() for part in parts])
+    chunks = [part.finish() for part in parts]
+    piece = jnp.concatenate(chunks)
 
     part = links.mine(links.core) * 2 + links.mine(links.y)
     squares = flat.squares(piece, 0, mine, part) + flat.squares(piece, 1, mine, part)
     squares += late_flat.squares(piece_dec, 0, mine, part)
-    squares, loss_sum = links.everyone(jnp.stack([squares, jnp.sum(g_two[8]) / PIX]), jnp.add)
+    sums = links.everyone(jnp.stack([squares, jnp.sum(g_two[8]) / PIX]), [links.y])
+    chunks[-1] = after(chunks[-1], sums)
+    sides = [links.swap(chunk, links.y) for chunk in chunks]
+    sums = links.everyone(sums, [links.core] + links.wide_bits[:-1])
+    sides[-1] = after(sides[-1], sums)
+    squares, loss_sum = links.everyone(sums, links.wide_bits[-1:])
+    low = links.mine(links.y) == 0
+    joined = [
+        jnp.stack([jnp.where(low, one, two), jnp.where(low, two, one)]) for one, two in zip(chunks, sides)
+    ]
+    joined = jnp.concatenate([links.gather(v, [links.core]) for v in joined], axis=2)
+    joined = joined[:, :, flat.starts[0] :].reshape(-1, 128)
+    joined_late = join_shard(piece_dec, links).reshape(-1, 128)
     grad_norm = jnp.sqrt(squares)
     clip_scale = jnp.minimum(1.0, clip_norm / (grad_norm + 1e-06))
-    narrow_bits = [links.core, links.y]
-    joined, joined_late = join_shard(flat.of(piece, 0), links), join_shard(piece_dec, links)
-    everywhere = links.gather(
-        flat.of(piece, 1), links.wide_bits + narrow_bits, links.upper + [links.x, links.y, links.core]
-    ).reshape(links.wide, -1, 128)
-    count = flat.sections[1][1]
-    early_sum = jnp.concatenate(
-        [everywhere[s, s * count % 8 : s * count % 8 + count] for s in range(links.wide)]
-    )
-    early_sum = jnp.pad(early_sum, ((0, links.wide * dec_shard - links.wide * count), (0, 0)))
+    order = links.upper + [links.x, links.y, links.core]
+    everywhere = links.gather(chunks[0][: flat.parts[1]], order)
+    places = [order[::-1].index(bit) for bit in links.wide_bits + [links.core, links.y]]
+    everywhere = everywhere.transpose(places + [len(places), len(places) + 1]).reshape(links.wide, -1, 128)
+    early_sum = everywhere[:, : flat.sections[1][1]].reshape(-1, 128)
+    early_sum = jnp.pad(early_sum, ((0, dec_shard), (0, 0)))
+    start = jnp.minimum(mine * dec_shard, early_sum.shape[0] - dec_shard)
     grad_enc = flat.take(joined, 0, mine).reshape(-1)
-    grad_dec = late_flat.take(joined_late, 0, mine) + lax.dynamic_slice_in_dim(early_sum, mine * dec_shard, dec_shard)
+    grad_dec = late_flat.take(joined_late, 0, mine) + lax.dynamic_slice_in_dim(early_sum, start, dec_shard)
     enc_one, enc_two, enc_new = adamw_update(params_enc, grad_enc, m_enc, v_enc, clip_scale)
     dec_one, dec_two, dec_new = adamw_update(
         params_dec, grad_dec.reshape(-1), m_dec, v_dec, clip_scale

time: 878 us -> 834 us (0.950)
  waiting for transfers between devices: 271 us -> 219 us
  other arithmetic: 99.8 us -> 129 us
  starting transfers between devices: 77.3 us -> 56.3 us
    ppermute x73 -> x55, waiting for transfers between devices: 271 us -> 219 us  [swap(): return lax.ppermute(value, AXES, pairs)]
    ppermute x73 -> x55, starting transfers between devices: 77.3 us -> 56.3 us  [swap(): return lax.ppermute(value, AXES, pairs)]
    add x24 -> x15, other arithmetic: 27.3 us -> 38.3 us  [take(): return cut(self.kept) + cut(self.other)]
    another operation x55 -> x40, other arithmetic: 14.8 us -> 25.5 us  [the longest x34 22.4 us: step(): jnp.stack([jnp.where(low, self.value, other), jnp.where(low, other, self....]
    mul x12 -> x8, other arithmetic: 3.57 us -> 12.7 us  [the longest x6 11.5 us: arrive(): received = received[..., :self.rows, :].astype(F) * jnp.exp2(-power)]
  transfers between devices with their start and end apart: 73 -> 55, of which waited for: 38 -> 28; matrix products, arithmetic and copies ran while one was open for 12% -> 16% of each run, Pallas kernels for 23% -> 18%
where the time goes in v4:
time: 834 us; the launch traced here: 827 us
  Pallas kernels  378 us (45%)
  waiting for transfers between devices  219 us (26%)
  other arithmetic  129 us (15%)
  starting transfers between devices  56.3 us (7%)
  local copies, waits for them, and re-layouts  27.1 us (3%)
  between operations  16.6 us (2%)
    ppermute x55, waiting for transfers between devices, swap(): return lax.ppermute(value, AXES, pairs)  219 us
    pallas_call x3, Pallas kernels, attend_back(): pl.pallas_call(functools.partial(attend_back_kernel, h, kc), grid=(nq,),...  121 us
    pallas_call x1, Pallas kernels, mlp_both(): pl.pallas_call(mlp_kernel, grid=(ROWS // bm,), in_specs=[part(DD), part(D...  65.9 us
    pallas_call x1, Pallas kernels, attend_forward(): pl.pallas_call(attend_kernel, grid=(3, nq), in_specs=[pl.BlockSpec((bq, 1...  63.1 us
    ppermute x55, starting transfers between devices, swap(): return lax.ppermute(value, AXES, pairs)  56.3 us
    pallas_call x2, Pallas kernels, unpack_flat(): pl.pallas_call(functools.partial(unpack_kernel, pieces, groups, leads, wa...  43.6 us
    add x15, other arithmetic, take(): return cut(self.kept) + cut(self.other)  38.3 us
    another operation x34, other arithmetic, step(): jnp.stack([jnp.where(low, self.value, other), jnp.where(low, other, self....  22.4 us
  transfers between devices with their start and end apart: 55, of which 28 were waited for; matrix products, arithmetic and copies ran while one was open for 16% of the time, Pallas kernels for 18%

profile of v4, /device:TPU:0, one launch (start us, length us, event | category | flops | bytes accessed | tf_op | source)
XLA Modules:
  0.0 826.6 jit_solution(14263054099170897637)
XLA Ops:
  21.0 14.6 %collective-permute-done.6 = bf16[864,128]{1,0:T(8,128)(2,1)} collective-permute-done((bf16[864,128]{1,0:T(8,128)(2,1)}, bf16[864,128]{1,0:T(8,128)(2,1)}, u32[]{:S(2)}, u32[]{:S(2)}) %collective-permute-start.6) | collective-permute-done | bytes 221216 | tf_op jit(solution)/shard_map/ppermute | solution.py:948
  43.0 6.8 collective-permute-done.7
  62.0 9.7 %collective-permute-done.8 = bf16[2,2,864,128]{3,2,1,0:T(8,128)(2,1)} collective-permute-done((bf16[2,2,864,128]{3,2,1,0:T(8,128)(2,1)}, bf16[2,2,864,128]{3,2,1,0:T(8,128)(2,1)}, u32[]{:S(2)}, u32[]{:S(2)}) %collective-permute-start.8) | collective-permute-done | bytes 884768 | tf_op jit(solution)/shard_map/ppermute | solution.py:948
  80.3 13.3 %collective-permute-done.14 = bf16[2,2,896,128]{3,2,1,0:T(8,128)(2,1)S(1)} collective-permute-done((bf16[2,2,896,128]{3,2,1,0:T(8,128)(2,1)S(1)}, bf16[2,2,896,128]{3,2,1,0:T(8,128)(2,1)S(1)}, u32[]{:S(2)}, u32[]{:S(2)}) %collective-permute-start.14) | collective-permute-done | bytes 917536 | tf_op jit(solution)/shard_map/ppermute | solution.py:948
  100.1 10.3 %multiply_sine_fusion = (f32[2592,192]{1,0:T(8,128)S(1)}, f32[2592,192]{1,0:T(8,128)S(1)}) fusion(f32[192]{0:T(256)S(1)} %multiply_exponential_fusion.1, f32[2592]{0:T(1024)S(1)} %fusion.36), kind=kLoop, calls=%fused_computation.22 | loop fusion | flops 497664 | bytes 3992448 | tf_op jit(solution)/shard_map/sin | solution.py:55
  118.8 19.9 %collective-permute-done.9 = bf16[2,2,2,864,128]{4,3,2,1,0:T(8,128)(2,1)} collective-permute-done((bf16[2,2,2,864,128]{4,3,2,1,0:T(8,128)(2,1)}, bf16[2,2,2,864,128]{4,3,2,1,0:T(8,128)(2,1)}, u32[]{:S(2)}, u32[]{:S(2)}) %collective-permute-start.9) | collective-permute-done | bytes 1769504 | tf_op jit(solution)/shard_map/ppermute | solution.py:948
  148.0 31.7 %unpack_enc.1 = (bf16[1536,768]{1,0:T(8,128)(2,1)}, bf16[768,2304]{1,0:T(8,128)(2,1)}, bf16[768,768]{1,0:T(8,128)(2,1)}, bf16[768,3072]{1,0:T(8,128)(2,1)}, bf16...) custom-call(s32[4]{0:T(128)} %pad_add_fusion.mine_ref, bf16[8,928,128]{2,1,0:T(8,128)(2,1)} %bitcast.310, ...), custom_call_target="tpu_custom_call" | custom-call | bytes 102776832 | tf_op jit(solution)/shard_map/unpack_enc/pallas_call | solution.py:875
  179.7 14.6 %enc_forward.1 = (f32[256,384]{1,0:T(8,128)}, f32[256,768]{1,0:T(8,128)}, bf16[256,2304]{1,0:T(8,128)(2,1)}, bf16[256,768]{1,0:T(8,128)(2,1)}, f32[256,768]{1,0:...) custom-call(bf16[256,1536]{1,0:T(8,128)(2,1)} %pix_ref.3, f32[256,768]{1,0:T(8,128)} %pad_maximum_fusion.15.place_ref, ...), custom_call_target="tpu_custom_call" | custom-call | flops 15000000512 | bytes 20971520 | tf_op jit(solution)/shard_map/enc_forward/pallas_call | solution.py:457
  194.4 11.8 %unpack_dec.1 = (bf16[384,1152]{1,0:T(8,128)(2,1)}, bf16[384,384]{1,0:T(8,128)(2,1)}, bf16[384,1536]{1,0:T(8,128)(2,1)}, bf16[1536,384]{1,0:T(8,128)(2,1)}, bf16...) custom-call(s32[4]{0:T(128)} %pad_add_fusion.mine_ref, bf16[8,928,128]{2,1,0:T(8,128)(2,1)} %bitcast.311, ...), custom_call_target="tpu_custom_call" | custom-call | bytes 28409856 | tf_op jit(solution)/shard_map/unpack_dec/pallas_call | solution.py:875
  213.0 13.4 %dec_qkv.1 = (f32[2592,384]{1,0:T(8,128)}, bf16[2592,1152]{1,0:T(8,128)(2,1)}) custom-call(s32[256]{0:T(256)} %bitcast.326, f32[256]{0:T(256)} %copy-done.23, f32[256,384]{1,0:T(8,128)} %get-tuple-element.113.latent_ref, f32[2592,384]{1,0:T(8,128)} %pad_maximum_fusion.2.place_ref, f32[2592,128]{1,0:T(8,128)} %pad.44.row_ref.refs_9_, ...), custom_call_target="tpu_custom_call" | custom-call | flops 10000000000 | bytes 16777216 | tf_op jit(solution)/shard_map/dec_qkv/pallas_call | solution.py:142
  226.4 63.1 %dec_attend.1 = (bf16[2592,384]{1,0:T(8,128)(2,1)}, f32[9,8,864]{2,1,0:T(8,128)}) custom-call(bf16[2592,1152]{1,0:T(8,128)(2,1)} %get-tuple-element.118.q_ref.k_ref.v_ref, bf16[2592,1152]{1,0:T(8,128)(2,1)} %get-tuple-element.118.q_ref.k_ref.v_ref, bf16[2592,1152]{1,0:T(8,128)(2,1)} %get-tuple-element.118.q_ref.k_ref.v_ref, ...), custom_call_target="tpu_custom_call" | custom-call | flops 60000002048 | bytes 16777216 | tf_op jit(solution)/shard_map/dec_attend/pallas_call | solution.py:173
  289.5 65.9 %dec_mlp.1 = (bf16[2592,384]{1,0:T(8,128)(2,1)}, f32[2592,384]{1,0:T(8,128)}, f32[6,8,432]{2,1,0:T(8,128)}, f32[384,384]{1,0:T(8,128)}, f32[384,1536]{1,0:T(8,12...) custom-call(f32[2592,384]{1,0:T(8,128)} %get-tuple-element.117.x_ref, ...), custom_call_target="tpu_custom_call" | custom-call | tf_op jit(solution)/shard_map/dec_mlp/pallas_call | solution.py:331
  355.3 8.2 pack_dec.1
  364.1 40.3 %dec_attend_back.3 = (bf16[2592,128]{1,0:T(8,128)(2,1)}, bf16[2592,128]{1,0:T(8,128)(2,1)}, bf16[2592,128]{1,0:T(8,128)(2,1)}) custom-call(bf16[2592,1152]{1,0:T(8,128)(2,1)} %get-tuple-element.118.q_ref.k_ref.v_ref, bf16[2592,1152]{1,0:T(8,128)(2,1)} %get-tuple-element.118.q_ref.k_ref.v_ref, bf16[2592,1152]{1,0:T(8,128)(2,1)} %get-tuple-element.118.q_ref.k_ref.v_ref, ...), custom_call_target="tpu_custom_call" | custom-call | flops 40000000000 | bytes 8388608 | tf_op jit(solution)/shard_map/dec_attend_back/pallas_call | solution.py:245
  415.4 40.4 %dec_attend_back.4 = (bf16[2592,128]{1,0:T(8,128)(2,1)}, bf16[2592,128]{1,0:T(8,128)(2,1)}, bf16[2592,128]{1,0:T(8,128)(2,1)}) custom-call(bf16[2592,1152]{1,0:T(8,128)(2,1)} %get-tuple-element.118.q_ref.k_ref.v_ref, bf16[2592,1152]{1,0:T(8,128)(2,1)} %get-tuple-element.118.q_ref.k_ref.v_ref, bf16[2592,1152]{1,0:T(8,128)(2,1)} %get-tuple-element.118.q_ref.k_ref.v_ref, ...), custom_call_target="tpu_custom_call" | custom-call | flops 40000000000 | bytes 8388608 | tf_op jit(solution)/shard_map/dec_attend_back/pallas_call | solution.py:245
  461.8 40.1 %dec_attend_back.5 = (bf16[2592,128]{1,0:T(8,128)(2,1)}, bf16[2592,128]{1,0:T(8,128)(2,1)}, bf16[2592,128]{1,0:T(8,128)(2,1)}) custom-call(bf16[2592,1152]{1,0:T(8,128)(2,1)} %get-tuple-element.118.q_ref.k_ref.v_ref, bf16[2592,1152]{1,0:T(8,128)(2,1)} %get-tuple-element.118.q_ref.k_ref.v_ref, bf16[2592,1152]{1,0:T(8,128)(2,1)} %get-tuple-element.118.q_ref.k_ref.v_ref, ...), custom_call_target="tpu_custom_call" | custom-call | flops 40000000000 | bytes 8388608 | tf_op jit(solution)/shard_map/dec_attend_back/pallas_call | solution.py:245
  505.0 14.1 %dec_qkv_back.1 = (f32[2592,384]{1,0:T(8,128)}, f32[384,1152]{1,0:T(8,128)}, f32[8,1152]{1,0:T(8,128)}) custom-call(f32[2592,384]{1,0:T(8,128)} %get-tuple-element.117.x_ref, f32[2592,384]{1,0:T(8,128)} %get-tuple-element.164.dx_ref, bf16[2592,128]{1,0:T(8,128)(2,1)} %get-tuple-element.165.refs_0_, bf16[2592,128]{1,0:T(8,128)(2,1)} %get-tuple-element.166.refs_1_, ...), custom_call_target="tpu_custom_call" | custom-call | flops 15000000512 | bytes 8388608 | tf_op jit(solution)/shard_map/dec_qkv_back/pallas_call | solution.py:372
  519.1 17.4 %enc_back_one.1 = (f32[264,768]{1,0:T(8,128)}, f32[8,128]{1,0:T(8,128)}, f32[8,2,1104,128]{3,2,1,0:T(8,128)}, f32[8,2,1104,128]{3,2,1,0:T(8,128)}, f32[8,2,1104,...) custom-call(s32[1]{0:T(128)} %bitcast.core_ref, s32[256]{0:T(256)} %bitcast.327, f32[256]{0:T(256)} %copy-done.23, ...), custom_call_target="tpu_custom_call" | custom-call | flops 20000000000 | bytes 31457280 | tf_op jit(solution)/shard_map/enc_back_one/pallas_call | solution.py:714
  537.3 17.3 %enc_back_two.1 = (f32[8,128]{1,0:T(8,128)}, f32[8,2,1104,128]{3,2,1,0:T(8,128)}, f32[8,2,1104,128]{3,2,1,0:T(8,128)}, f32[8,2,1104,128]{3,2,1,0:T(8,128)}, f32[8,2,1104,128]{3,2,1,0:T(8,128)}) custom-call(s32[1]{0:T(128)} %bitcast.core_ref, ...), custom_call_target="tpu_custom_call", output_to_operand_aliasing={{1}: (14, {}), {2}: (15, {}), {3}: (16, {}), {4}: (17, {})} | custom-call | flops 15000000512 | bytes 31457280 | tf_op jit(solution)/shard_map/enc_back_two/pallas_call | solution.py:751
  556.2 14.3 %collective-permute-done.27 = f32[8,2,1104,128]{3,2,1,0:T(8,128)} collective-permute-done((f32[8,2,1104,128]{3,2,1,0:T(8,128)}, f32[8,2,1104,128]{3,2,1,0:T(8,128)}, u32[]{:S(2)}, u32[]{:S(2)}) %collective-permute-start.27) | collective-permute-done | bytes 9044000 | tf_op jit(solution)/shard_map/ppermute | solution.py:948
  572.7 9.1 %dynamic-slice_add_fusion.1 = (f32[2,2,1,2,1104,128]{5,4,3,2,1,0:T(8,128)}, f32[2,2,1,2,1104,128]{5,4,3,2,1,0:T(8,128)S(1)}, f32[2,2,1,2,1104,128]{5,4,3,2,1,0:T(8,128)S(1)}) fusion(f32[2,2,2,2,1104,128]{5,4,3,2,1,0:T(8,128)} %bitcast.71, s32[]{:T(128)S(6)} %select_n.467, f32[2,2,2,2,1104,128]{5,4,3,2,1,0:T(8,128)} %bitcast.312, s32[]{:T(128)S(6)} %select_n.469), kind=kLoop, calls=%fused_computation.11 | loop fusion | flops 1130496 | bytes 31653896 | tf_op jit(solution)/shard_map/add | solution.py:1000
  585.0 5.9 dynamic-slice_add_fusion
  598.1 4.9 collective-permute-done.38
  603.0 31.8 %collective-permute-done.28 = f16[2,2,2,1112,128]{4,3,1,0,2:T(8,128)(2,1)} collective-permute-done((f16[2,2,2,1112,128]{4,3,1,0,2:T(8,128)(2,1)S(1)}, f16[2,2,2,1112,128]{4,3,1,0,2:T(8,128)(2,1)}, u32[]{:S(2)}, u32[]{:S(2)}) %collective-permute-start.28) | collective-permute-done | bytes 2277408 | tf_op jit(solution)/shard_map/ppermute | solution.py:948
  651.9 5.5 bitcast_add_fusion.1
  664.0 7.9 collective-permute-done.29
  676.8 8.5 %collective-permute-done.34 = f16[2,2,1112,128]{3,2,1,0:T(8,128)(2,1)} collective-permute-done((f16[2,2,1112,128]{3,2,1,0:T(8,128)(2,1)}, f16[2,2,1112,128]{3,2,1,0:T(8,128)(2,1)}, u32[]{:S(2)}, u32[]{:S(2)}) %collective-permute-start.34) | collective-permute-done | bytes 1138720 | tf_op jit(solution)/shard_map/ppermute | solution.py:948
  703.1 31.9 %collective-permute-done.30 = f16[2,1112,128]{2,1,0:T(8,128)(2,1)} collective-permute-done((f16[2,1112,128]{2,1,0:T(8,128)(2,1)}, f16[2,1112,128]{2,1,0:T(8,128)(2,1)}, u32[]{:S(2)}, u32[]{:S(2)}) %collective-permute-start.30) | collective-permute-done | bytes 569376 | tf_op jit(solution)/shard_map/ppermute | solution.py:948
  738.3 6.4 collective-permute-done.35
  748.9 7.8 collective-permute-done.31
  760.1 9.9 %collective-permute-done.36 = f32[1104,128]{1,0:T(8,128)S(1)} collective-permute-done((f32[1104,128]{1,0:T(8,128)S(1)}, f32[1104,128]{1,0:T(8,128)S(1)}, u32[]{:S(2)}, u32[]{:S(2)}) %collective-permute-start.36) | collective-permute-done | bytes 565280 | tf_op jit(solution)/shard_map/ppermute | solution.py:948
  810.9 7.7 multiply_subtract_fusion
  (318 shorter events, 205.6 us)
Async XLA Ops:
  5.3 31.4 %collective-permute-start.12 = (bf16[896,128]{1,0:T(8,128)(2,1)}, bf16[896,128]{1,0:T(8,128)(2,1)}, u32[]{:S(2)}, u32[]{:S(2)}) collective-permute-start(bf16[896,128]{1,0:T(8,128)(2,1)} %pad_maximum_fusion.23), channel_id=1, source_target_pairs={{0,4},{1,5},{2,6},{3,7},{4,0},{5,1},{6,2},{7,3},{8,12},{9,13},{10,... | collective-permute-start | bytes 688136 | tf_op jit(solution)/shard_map/ppermute | solution.py:948
  10.1 25.5 %collective-permute-start.6 = (bf16[864,128]{1,0:T(8,128)(2,1)}, bf16[864,128]{1,0:T(8,128)(2,1)}, u32[]{:S(2)}, u32[]{:S(2)}) collective-permute-start(bf16[864,128]{1,0:T(8,128)(2,1)} %pad_maximum_fusion.25), channel_id=1, source_target_pairs={{0,4},{1,5},{2,6},{3,7},{4,0},{5,1},{6,2},{7,3},{8,12},{9,13},{10,... | collective-permute-start | bytes 663560 | tf_op jit(solution)/shard_map/ppermute | solution.py:948
  16.1 23.7 %collective-permute-start = (bf16[928,128]{1,0:T(8,128)(2,1)S(1)}, bf16[928,128]{1,0:T(8,128)(2,1)S(1)}, u32[]{:S(2)}, u32[]{:S(2)}) collective-permute-start(bf16[928,128]{1,0:T(8,128)(2,1)S(1)} %pad_maximum_fusion.22), channel_id=1, source_target_pairs={{0,4},{1,5},{2,6},{3,7},{4,0},{5,1},{6,2},{7,3},{8,12},{9,13},{10,... | collective-permute-start | bytes 712712 | tf_op jit(solution)/shard_map/ppermute | solution.py:948
  50.9 20.8 %collective-permute-start.8 = (bf16[2,2,864,128]{3,2,1,0:T(8,128)(2,1)}, bf16[2,2,864,128]{3,2,1,0:T(8,128)(2,1)}, u32[]{:S(2)}, u32[]{:S(2)}) collective-permute-start(bf16[2,2,864,128]{3,2,1,0:T(8,128)(2,1)} %pad_maximum_fusion.14), channel_id=1, source_target_pairs={{0,1},{1,0},{2,3},{3,2},{4,5},{5,4},{6,7},{7,6},{8,9},{9,8},{10,11... | collective-permute-start | bytes 2654216 | tf_op jit(solution)/shard_map/ppermute | solution.py:948
  52.9 24.2 %collective-permute-start.2 = (bf16[2,2,928,128]{3,2,1,0:T(8,128)(2,1)S(1)}, bf16[2,2,928,128]{3,2,1,0:T(8,128)(2,1)}, u32[]{:S(2)}, u32[]{:S(2)}) collective-permute-start(bf16[2,2,928,128]{3,2,1,0:T(8,128)(2,1)S(1)} %pad_maximum_fusion.11), channel_id=1, source_target_pairs={{0,16},{1,17},{2,18},{3,19},{4,20},{5,21},{6,22},{7,23},{8,24},{9,... | collective-permute-start | bytes 2850824 | tf_op jit(solution)/shard_map/ppermute | solution.py:948
  60.3 33.3 %collective-permute-start.14 = (bf16[2,2,896,128]{3,2,1,0:T(8,128)(2,1)S(1)}, bf16[2,2,896,128]{3,2,1,0:T(8,128)(2,1)S(1)}, u32[]{:S(2)}, u32[]{:S(2)}) collective-permute-start(bf16[2,2,896,128]{3,2,1,0:T(8,128)(2,1)S(1)} %pad_maximum_fusion.12), channel_id=1, source_target_pairs={{0,16},{1,17},{2,18},{3,19},{4,20},{5,21},{6,22},{7,23},{8,24},{9,... | collective-permute-start | bytes 2752520 | tf_op jit(solution)/shard_map/ppermute | solution.py:948
  78.6 38.2 %collective-permute-start.3 = (bf16[2,2,2,928,128]{4,3,2,1,0:T(8,128)(2,1)S(1)}, bf16[2,2,2,928,128]{4,3,2,1,0:T(8,128)(2,1)}, u32[]{:S(2)}, u32[]{:S(2)}) collective-permute-start(bf16[2,2,2,928,128]{4,3,2,1,0:T(8,128)(2,1)S(1)} %pad_maximum_fusion.3), channel_id=1, source_target_pairs={{0,2},{1,3},{2,0},{3,1},{4,6},{5,7},{6,4},{7,5},{8,10},{9,11},{10,... | collective-permute-start | bytes 5701640 | tf_op jit(solution)/shard_map/ppermute | solution.py:948
  95.2 43.5 %collective-permute-start.15 = (bf16[2,2,2,896,128]{4,3,2,1,0:T(8,128)(2,1)}, bf16[2,2,2,896,128]{4,3,2,1,0:T(8,128)(2,1)}, u32[]{:S(2)}, u32[]{:S(2)}) collective-permute-start(bf16[2,2,2,896,128]{4,3,2,1,0:T(8,128)(2,1)} %pad_maximum_fusion.4), channel_id=1, source_target_pairs={{0,1},{1,0},{2,3},{3,2},{4,5},{5,4},{6,7},{7,6},{8,9},{9,8},{10,11... | collective-permute-start | bytes 5505032 | tf_op jit(solution)/shard_map/ppermute | solution.py:948
  96.0 43.2 %collective-permute-start.4 = (bf16[2,2,2,928,128]{4,3,2,1,0:T(8,128)(2,1)S(1)}, bf16[2,2,2,928,128]{4,3,2,1,0:T(8,128)(2,1)}, u32[]{:S(2)}, u32[]{:S(2)}) collective-permute-start(bf16[2,2,2,928,128]{4,3,2,1,0:T(8,128)(2,1)S(1)} %pad_maximum_fusion.3), channel_id=1, source_target_pairs={{0,8},{1,9},{2,10},{3,11},{4,12},{5,13},{6,14},{7,15},{8,0},{9,1},... | collective-permute-start | bytes 5701640 | tf_op jit(solution)/shard_map/ppermute | solution.py:948
  97.4 41.3 %collective-permute-start.9 = (bf16[2,2,2,864,128]{4,3,2,1,0:T(8,128)(2,1)}, bf16[2,2,2,864,128]{4,3,2,1,0:T(8,128)(2,1)}, u32[]{:S(2)}, u32[]{:S(2)}) collective-permute-start(bf16[2,2,2,864,128]{4,3,2,1,0:T(8,128)(2,1)} %pad_maximum_fusion.6), channel_id=1, source_target_pairs={{0,16},{1,17},{2,18},{3,19},{4,20},{5,21},{6,22},{7,23},{8,24},{9,... | collective-permute-start | bytes 5308424 | tf_op jit(solution)/shard_map/ppermute | solution.py:948
  116.7 27.9 %collective-permute-start.5 = (bf16[2,2,2,928,128]{4,3,2,1,0:T(8,128)(2,1)}, bf16[2,2,2,928,128]{4,3,2,1,0:T(8,128)(2,1)}, u32[]{:S(2)}, u32[]{:S(2)}) collective-permute-start(bf16[2,2,2,928,128]{4,3,2,1,0:T(8,128)(2,1)} %collective-permute-done.3), channel_id=1, source_target_pairs={{0,8},{1,9},{2,10},{3,11},{4,12},{5,13},{6,14},{7,15},{8,0},{9,1},... | collective-permute-start | bytes 5701640 | tf_op jit(solution)/shard_map/ppermute | solution.py:948
  118.3 27.1 %collective-permute-start.10 = (bf16[2,2,2,864,128]{4,3,2,1,0:T(8,128)(2,1)}, bf16[2,2,2,864,128]{4,3,2,1,0:T(8,128)(2,1)}, u32[]{:S(2)}, u32[]{:S(2)}) collective-permute-start(bf16[2,2,2,864,128]{4,3,2,1,0:T(8,128)(2,1)} %pad_maximum_fusion.6), channel_id=1, source_target_pairs={{0,8},{1,9},{2,10},{3,11},{4,12},{5,13},{6,14},{7,15},{8,0},{9,1},... | collective-permute-start | bytes 5308424 | tf_op jit(solution)/shard_map/ppermute | solution.py:948
  363.5 40.9 %collective-permute-start.19 = (f32[8,2,288,128]{3,2,1,0:T(8,128)}, f32[8,2,288,128]{3,2,1,0:T(8,128)S(1)}, u32[]{:S(2)}, u32[]{:S(2)}) collective-permute-start(f32[8,2,288,128]{3,2,1,0:T(8,128)} %get-tuple-element.137), channel_id=1, source_target_pairs={{0,8},{1,9},{2,10},{3,11},{4,12},{5,13},{6,14},{7,15},{8,0},{9,1},... | collective-permute-start | bytes 7077896 | tf_op jit(solution)/shard_map/ppermute | solution.py:948
  364.0 45.6 %collective-permute-start.18 = (f32[8,2,304,128]{3,2,1,0:T(8,128)}, f32[8,2,304,128]{3,2,1,0:T(8,128)}, u32[]{:S(2)}, u32[]{:S(2)}) collective-permute-start(f32[8,2,304,128]{3,2,1,0:T(8,128)} %get-tuple-element.134), channel_id=1, source_target_pairs={{0,8},{1,9},{2,10},{3,11},{4,12},{5,13},{6,14},{7,15},{8,0},{9,1},... | collective-permute-start | bytes 7471112 | tf_op jit(solution)/shard_map/ppermute | solution.py:948
  412.6 43.2 %collective-permute-start.21 = (f32[2,2,2,288,128]{4,3,2,1,0:T(8,128)}, f32[2,2,2,288,128]{4,3,2,1,0:T(8,128)S(1)}, u32[]{:S(2)}, u32[]{:S(2)}) collective-permute-start(f32[2,2,2,288,128]{4,3,2,1,0:T(8,128)} %get-tuple-element.145), channel_id=1, source_target_pairs={{0,16},{1,17},{2,18},{3,19},{4,20},{5,21},{6,22},{7,23},{8,24},{9,... | collective-permute-start | bytes 3538952 | tf_op jit(solution)/shard_map/ppermute | solution.py:948
  413.9 44.3 %collective-permute-start.20 = (f32[2,2,2,304,128]{4,3,2,1,0:T(8,128)}, f32[2,2,2,304,128]{4,3,2,1,0:T(8,128)}, u32[]{:S(2)}, u32[]{:S(2)}) collective-permute-start(f32[2,2,2,304,128]{4,3,2,1,0:T(8,128)} %get-tuple-element.143), channel_id=1, source_target_pairs={{0,1},{1,0},{2,3},{3,2},{4,5},{5,4},{6,7},{7,6},{8,9},{9,8},{10,11... | collective-permute-start | bytes 3735560 | tf_op jit(solution)/shard_map/ppermute | solution.py:948
  460.5 41.3 %collective-permute-start.23 = (f32[2,2,288,128]{3,2,1,0:T(8,128)S(1)}, f32[2,2,288,128]{3,2,1,0:T(8,128)S(1)}, u32[]{:S(2)}, u32[]{:S(2)}) collective-permute-start(f32[2,2,288,128]{3,2,1,0:T(8,128)S(1)} %get-tuple-element.153), channel_id=1, source_target_pairs={{0,1},{1,0},{2,3},{3,2},{4,5},{5,4},{6,7},{7,6},{8,9},{9,8},{10,11... | collective-permute-start | bytes 1769480 | tf_op jit(solution)/shard_map/ppermute | solution.py:948
  461.0 40.9 %collective-permute-start.22 = (f32[2,2,304,128]{3,2,1,0:T(8,128)}, f32[2,2,304,128]{3,2,1,0:T(8,128)S(1)}, u32[]{:S(2)}, u32[]{:S(2)}) collective-permute-start(f32[2,2,304,128]{3,2,1,0:T(8,128)} %get-tuple-element.152), channel_id=1, source_target_pairs={{0,16},{1,17},{2,18},{3,19},{4,20},{5,21},{6,22},{7,23},{8,24},{9,... | collective-permute-start | bytes 1867784 | tf_op jit(solution)/shard_map/ppermute | solution.py:948
  502.0 34.5 %collective-permute-start.25 = (f32[2,288,128]{2,1,0:T(8,128)S(1)}, f32[2,288,128]{2,1,0:T(8,128)S(1)}, u32[]{:S(2)}, u32[]{:S(2)}) collective-permute-start(f32[2,288,128]{2,1,0:T(8,128)S(1)} %get-tuple-element.180), channel_id=1, source_target_pairs={{0,4},{1,5},{2,6},{3,7},{4,0},{5,1},{6,2},{7,3},{8,12},{9,13},{10,... | collective-permute-start | bytes 884744 | tf_op jit(solution)/shard_map/ppermute | solution.py:948
  504.7 32.6 %collective-permute-start.24 = (f32[2,304,128]{2,1,0:T(8,128)S(1)}, f32[2,304,128]{2,1,0:T(8,128)S(1)}, u32[]{:S(2)}, u32[]{:S(2)}) collective-permute-start(f32[2,304,128]{2,1,0:T(8,128)S(1)} %get-tuple-element.179), channel_id=1, source_target_pairs={{0,4},{1,5},{2,6},{3,7},{4,0},{5,1},{6,2},{7,3},{8,12},{9,13},{10,... | collective-permute-start | bytes 933896 | tf_op jit(solution)/shard_map/ppermute | solution.py:948
  582.9 51.9 %collective-permute-start.28 = (f16[2,2,2,1112,128]{4,3,1,0,2:T(8,128)(2,1)S(1)}, f16[2,2,2,1112,128]{4,3,1,0,2:T(8,128)(2,1)}, u32[]{:S(2)}, u32[]{:S(2)}) collective-permute-start(f16[2,2,2,1112,128]{4,3,1,0,2:T(8,128)(2,1)S(1)} %concatenate.55), channel_id=1, source_target_pairs={{0,1},{1,0},{2,3},{3,2},{4,5},{5,4},{6,7},{7,6},{8,9},{9,8},{10,11... | collective-permute-start | bytes 6832136 | tf_op jit(solution)/shard_map/ppermute | solution.py:948
  593.3 51.9 %collective-permute-start.33 = (f16[2,2,2,1112,128]{4,3,1,0,2:T(8,128)(2,1)}, f16[2,2,2,1112,128]{4,3,1,0,2:T(8,128)(2,1)}, u32[]{:S(2)}, u32[]{:S(2)}) collective-permute-start(f16[2,2,2,1112,128]{4,3,1,0,2:T(8,128)(2,1)} %concatenate.58), channel_id=1, source_target_pairs={{0,16},{1,17},{2,18},{3,19},{4,20},{5,21},{6,22},{7,23},{8,24},{9,... | collective-permute-start | bytes 6832136 | tf_op jit(solution)/shard_map/ppermute | solution.py:948
  598.0 62.8 %collective-permute-start.37 = (f32[304,128]{1,0:T(8,128)S(1)}, f32[304,128]{1,0:T(8,128)}, u32[]{:S(2)}, u32[]{:S(2)}) collective-permute-start(f32[304,128]{1,0:T(8,128)S(1)} %fusion.34), channel_id=1, source_target_pairs={{0,2},{1,3},{2,0},{3,1},{4,6},{5,7},{6,4},{7,5},{8,10},{9,11},{10,... | collective-permute-start | bytes 466952 | tf_op jit(solution)/shard_map/ppermute | solution.py:948
  643.6 28.3 %collective-permute-start.29 = (f16[2,2,1112,128]{3,2,1,0:T(8,128)(2,1)}, f16[2,2,1112,128]{3,2,1,0:T(8,128)(2,1)}, u32[]{:S(2)}, u32[]{:S(2)}) collective-permute-start(f16[2,2,1112,128]{3,2,1,0:T(8,128)(2,1)} %concatenate.56), channel_id=1, source_target_pairs={{0,16},{1,17},{2,18},{3,19},{4,20},{5,21},{6,22},{7,23},{8,24},{9,... | collective-permute-start | bytes 3416072 | tf_op jit(solution)/shard_map/ppermute | solution.py:948
  658.6 26.6 %collective-permute-start.34 = (f16[2,2,1112,128]{3,2,1,0:T(8,128)(2,1)}, f16[2,2,1112,128]{3,2,1,0:T(8,128)(2,1)}, u32[]{:S(2)}, u32[]{:S(2)}) collective-permute-start(f16[2,2,1112,128]{3,2,1,0:T(8,128)(2,1)} %concatenate.59), channel_id=1, source_target_pairs={{0,1},{1,0},{2,3},{3,2},{4,5},{5,4},{6,7},{7,6},{8,9},{9,8},{10,11... | collective-permute-start | bytes 3416072 | tf_op jit(solution)/shard_map/ppermute | solution.py:948
  662.5 36.3 %collective-permute-start.48 = (f32[592,128]{1,0:T(8,128)}, f32[592,128]{1,0:T(8,128)}, u32[]{:S(2)}, u32[]{:S(2)}) collective-permute-start(f32[592,128]{1,0:T(8,128)} %pad_maximum_fusion.21), channel_id=1, source_target_pairs={{0,16},{1,17},{2,18},{3,19},{4,20},{5,21},{6,22},{7,23},{8,24},{9,... | collective-permute-start | bytes 909320 | tf_op jit(solution)/shard_map/ppermute | solution.py:948
  693.6 41.4 %collective-permute-start.30 = (f16[2,1112,128]{2,1,0:T(8,128)(2,1)}, f16[2,1112,128]{2,1,0:T(8,128)(2,1)}, u32[]{:S(2)}, u32[]{:S(2)}) collective-permute-start(f16[2,1112,128]{2,1,0:T(8,128)(2,1)} %concatenate.57), channel_id=1, source_target_pairs={{0,4},{1,5},{2,6},{3,7},{4,0},{5,1},{6,2},{7,3},{8,12},{9,13},{10,... | collective-permute-start | bytes 1708040 | tf_op jit(solution)/shard_map/ppermute | solution.py:948
  701.6 45.2 %collective-permute-start.49 = (f32[2,592,128]{2,1,0:T(8,128)}, f32[2,592,128]{2,1,0:T(8,128)}, u32[]{:S(2)}, u32[]{:S(2)}) collective-permute-start(f32[2,592,128]{2,1,0:T(8,128)} %pad_maximum_fusion.16), channel_id=1, source_target_pairs={{0,8},{1,9},{2,10},{3,11},{4,12},{5,13},{6,14},{7,15},{8,0},{9,1},... | collective-permute-start | bytes 1818632 | tf_op jit(solution)/shard_map/ppermute | solution.py:948
  702.8 41.9 %collective-permute-start.35 = (f16[2,1112,128]{2,1,0:T(8,128)(2,1)S(1)}, f16[2,1112,128]{2,1,0:T(8,128)(2,1)S(1)}, u32[]{:S(2)}, u32[]{:S(2)}) collective-permute-start(f16[2,1112,128]{2,1,0:T(8,128)(2,1)S(1)} %concatenate.60), channel_id=1, source_target_pairs={{0,4},{1,5},{2,6},{3,7},{4,0},{5,1},{6,2},{7,3},{8,12},{9,13},{10,... | collective-permute-start | bytes 1708040 | tf_op jit(solution)/shard_map/ppermute | solution.py:948
  738.2 18.5 %collective-permute-start.31 = (f32[1104,128]{1,0:T(8,128)S(1)}, f32[1104,128]{1,0:T(8,128)S(1)}, u32[]{:S(2)}, u32[]{:S(2)}) collective-permute-start(f32[1104,128]{1,0:T(8,128)S(1)} %fusion.31), channel_id=1, source_target_pairs={{0,2},{1,3},{2,0},{3,1},{4,6},{5,7},{6,4},{7,5},{8,10},{9,11},{10,... | collective-permute-start | bytes 1695752 | tf_op jit(solution)/shard_map/ppermute | solution.py:948
  746.0 23.9 %collective-permute-start.36 = (f32[1104,128]{1,0:T(8,128)S(1)}, f32[1104,128]{1,0:T(8,128)S(1)}, u32[]{:S(2)}, u32[]{:S(2)}) collective-permute-start(f32[1104,128]{1,0:T(8,128)S(1)} %fusion.30), channel_id=1, source_target_pairs={{0,2},{1,3},{2,0},{3,1},{4,6},{5,7},{6,4},{7,5},{8,10},{9,11},{10,... | collective-permute-start | bytes 1695752 | tf_op jit(solution)/shard_map/ppermute | solution.py:948
  756.9 34.8 %collective-permute-start.44 = (f32[1104,128]{1,0:T(8,128)S(1)}, f32[1104,128]{1,0:T(8,128)S(1)}, u32[]{:S(2)}, u32[]{:S(2)}) collective-permute-start(f32[1104,128]{1,0:T(8,128)S(1)} %bitcast_add_fusion.16), channel_id=1, source_target_pairs={{0,16},{1,17},{2,18},{3,19},{4,20},{5,21},{6,22},{7,23},{8,24},{9,... | collective-permute-start | bytes 1695752 | tf_op jit(solution)/shard_map/ppermute | solution.py:948
  (55 other events, 594.4 us)

commit v5 on v4

--- a/solution.py
+++ b/solution.py
@@ -32,6 +32,7 @@
 NN = (((1,), (0,)), ((), ()))
 TN = (((0,), (0,)), ((), ()))
 VMEM_LIMIT = 60 << 20
+SLOTS = 4
 
 
 def mm(left, right, dims=NN):
@@ -324,7 +325,7 @@
     )
 
 
-def mlp_both(x, a, target, rows, wo, wu, wd, wh, vec, bm=432):
+def mlp_both(x, a, target, rows, wo, wu, wd, wh, vec, bm=864):
     full = lambda shape: pl.BlockSpec(shape, lambda i: (0, 0))
     part = lambda width: pl.BlockSpec((bm, width), lambda i: (i, 0))
     sums = [wo.shape, wu.shape, wd.shape, wh.shape, vec.shape]
@@ -835,22 +836,23 @@
             for j in range(c):
                 vec_ref[v : v + 1, j * 128 : (j + 1) * 128] = lin[pl.ds(row + j, 1), :]
             v += 1
+    open_stores = []
     for k, (row, m, c) in enumerate(mats):
         stage, out = stages[k], outs[k]
         n = stage.shape[1]
         jobs = m // n
 
-        def store(j, slot):
+        def store(j, slot, k=k, stage=stage, out=out, n=n):
             return pltpu.make_async_copy(
-                stage.at[slot], out.at[pl.ds(pl.multiple_of(j * n, 16), n)], out_sem.at[slot]
+                stage.at[slot], out.at[pl.ds(pl.multiple_of(j * n, 16), n)], out_sem.at[k, slot]
             )
 
         def job(j, carry):
-            slot = lax.rem(j, 2)
-
-            @pl.when(j >= 2)
+            slot = lax.rem(j, SLOTS)
+
+            @pl.when(j >= SLOTS)
             def _():
-                store(j - 2, slot).wait()
+                store(j - SLOTS, slot).wait()
 
             for i in range(c):
                 rows = pl.ds(row + i + j * (n * c), n, stride=c)
@@ -859,8 +861,9 @@
             return carry
 
         lax.fori_loop(0, jobs, job, 0)
-        for j in range(max(jobs - 2, 0), jobs):
-            store(j, j % 2).wait()
+        open_stores += [(store, j) for j in range(max(jobs - SLOTS, 0), jobs)]
+    for store, j in open_stores:
+        store(j, j % SLOTS).wait()
 
 
 def unpack_flat(arrays, groups, leads, ways, mine, span, wide, shapes, name):
@@ -870,7 +873,7 @@
     width = max(s[0] for s in vectors)
     count = -(-len(vectors) // 8) * 8
     hbm = pl.BlockSpec(memory_space=pl.ANY)
-    stages = [pltpu.VMEM((2, job_rows(s[0], s[1] // 128, 1152), s[1]), B) for s in mats]
+    stages = [pltpu.VMEM((SLOTS, job_rows(s[0], s[1] // 128, 1152), s[1]), B) for s in mats]
     room = groups[-1][0] + groups[-1][2] * groups[-1][3]
     return pl.pallas_call(
         functools.partial(unpack_kernel, pieces, groups, leads, ways, span, wide),
@@ -879,7 +882,7 @@
         out_shape=[jax.ShapeDtypeStruct(s, B) for s in mats] + [jax.ShapeDtypeStruct((count, width), F)],
         scratch_shapes=[
             pltpu.VMEM((wide, room, 128), B), pltpu.VMEM((wide * span, 128), F),
-            pltpu.SemaphoreType.DMA((wide,)), pltpu.SemaphoreType.DMA((2,)),
+            pltpu.SemaphoreType.DMA((wide,)), pltpu.SemaphoreType.DMA((len(mats), SLOTS)),
         ] + stages,
         compiler_params=pltpu.CompilerParams(vmem_limit_bytes=VMEM_LIMIT),
         cost_estimate=pl.CostEstimate(flops=0, bytes_accessed=wide * span * 1536, transcendentals=0),

time: 834 us -> 812 us (0.974)
  Pallas kernels: 378 us -> 356 us
    pallas_call x2, Pallas kernels: 43.6 us -> 24.8 us  [unpack_flat(): pl.pallas_call(functools.partial(unpack_kernel, pieces, groups, leads, wa...]
  transfers between devices with their start and end apart: 55 -> 55, of which waited for: 28 -> 28; matrix products, arithmetic and copies ran while one was open for 16% -> 16% of each run, Pallas kernels for 18% -> 19%
where the time goes in v5:
time: 812 us; the launch traced here: 804 us
  Pallas kernels  356 us (44%)
  waiting for transfers between devices  219 us (27%)
  other arithmetic  129 us (16%)
  starting transfers between devices  56.1 us (7%)
  local copies, waits for them, and re-layouts  27.1 us (3%)
  between operations  16.6 us (2%)
    ppermute x55, waiting for transfers between devices, swap(): return lax.ppermute(value, AXES, pairs)  219 us
    pallas_call x3, Pallas kernels, attend_back(): pl.pallas_call(functools.partial(attend_back_kernel, h, kc), grid=(nq,),...  120 us
    pallas_call x1, Pallas kernels, attend_forward(): pl.pallas_call(attend_kernel, grid=(3, nq), in_specs=[pl.BlockSpec((bq, 1...  63.1 us
    pallas_call x1, Pallas kernels, mlp_both(): pl.pallas_call(mlp_kernel, grid=(ROWS // bm,), in_specs=[part(DD), part(D...  62.4 us
    ppermute x55, starting transfers between devices, swap(): return lax.ppermute(value, AXES, pairs)  56.1 us
    add x15, other arithmetic, take(): return cut(self.kept) + cut(self.other)  38.3 us
    pallas_call x2, Pallas kernels, unpack_flat(): pl.pallas_call(functools.partial(unpack_kernel, pieces, groups, leads, wa...  24.8 us
    another operation x34, other arithmetic, step(): jnp.stack([jnp.where(low, self.value, other), jnp.where(low, other, self....  22.4 us
  transfers between devices with their start and end apart: 55, of which 28 were waited for; matrix products, arithmetic and copies ran while one was open for 16% of the time, Pallas kernels for 19%

profile of v5, /device:TPU:0, one launch (start us, length us, event | category | flops | bytes accessed | tf_op | source)
XLA Modules:
  0.0 804.0 jit_solution(642327489119214025)
XLA Ops:
  21.0 14.6 %collective-permute-done.6 = bf16[864,128]{1,0:T(8,128)(2,1)} collective-permute-done((bf16[864,128]{1,0:T(8,128)(2,1)}, bf16[864,128]{1,0:T(8,128)(2,1)}, u32[]{:S(2)}, u32[]{:S(2)}) %collective-permute-start.6) | collective-permute-done | bytes 221216 | tf_op jit(solution)/shard_map/ppermute | solution.py:951
  43.0 6.8 collective-permute-done.7
  62.0 9.7 %collective-permute-done.8 = bf16[2,2,864,128]{3,2,1,0:T(8,128)(2,1)} collective-permute-done((bf16[2,2,864,128]{3,2,1,0:T(8,128)(2,1)}, bf16[2,2,864,128]{3,2,1,0:T(8,128)(2,1)}, u32[]{:S(2)}, u32[]{:S(2)}) %collective-permute-start.8) | collective-permute-done | bytes 884768 | tf_op jit(solution)/shard_map/ppermute | solution.py:951
  80.3 13.3 %collective-permute-done.14 = bf16[2,2,896,128]{3,2,1,0:T(8,128)(2,1)S(1)} collective-permute-done((bf16[2,2,896,128]{3,2,1,0:T(8,128)(2,1)S(1)}, bf16[2,2,896,128]{3,2,1,0:T(8,128)(2,1)S(1)}, u32[]{:S(2)}, u32[]{:S(2)}) %collective-permute-start.14) | collective-permute-done | bytes 917536 | tf_op jit(solution)/shard_map/ppermute | solution.py:951
  100.1 10.3 %multiply_sine_fusion = (f32[2592,192]{1,0:T(8,128)S(1)}, f32[2592,192]{1,0:T(8,128)S(1)}) fusion(f32[192]{0:T(256)S(1)} %multiply_exponential_fusion.1, f32[2592]{0:T(1024)S(1)} %fusion.36), kind=kLoop, calls=%fused_computation.22 | loop fusion | flops 497664 | bytes 3992448 | tf_op jit(solution)/shard_map/sin | solution.py:56
  118.8 19.9 %collective-permute-done.9 = bf16[2,2,2,864,128]{4,3,2,1,0:T(8,128)(2,1)} collective-permute-done((bf16[2,2,2,864,128]{4,3,2,1,0:T(8,128)(2,1)}, bf16[2,2,2,864,128]{4,3,2,1,0:T(8,128)(2,1)}, u32[]{:S(2)}, u32[]{:S(2)}) %collective-permute-start.9) | collective-permute-done | bytes 1769504 | tf_op jit(solution)/shard_map/ppermute | solution.py:951
  148.0 18.4 %unpack_enc.1 = (bf16[1536,768]{1,0:T(8,128)(2,1)}, bf16[768,2304]{1,0:T(8,128)(2,1)}, bf16[768,768]{1,0:T(8,128)(2,1)}, bf16[768,3072]{1,0:T(8,128)(2,1)}, bf16...) custom-call(s32[4]{0:T(128)} %pad_add_fusion.mine_ref, bf16[8,928,128]{2,1,0:T(8,128)(2,1)} %bitcast.310, ...), custom_call_target="tpu_custom_call" | custom-call | bytes 102776832 | tf_op jit(solution)/shard_map/unpack_enc/pallas_call | solution.py:878
  166.4 14.6 %enc_forward.1 = (f32[256,384]{1,0:T(8,128)}, f32[256,768]{1,0:T(8,128)}, bf16[256,2304]{1,0:T(8,128)(2,1)}, bf16[256,768]{1,0:T(8,128)(2,1)}, f32[256,768]{1,0:...) custom-call(bf16[256,1536]{1,0:T(8,128)(2,1)} %pix_ref.3, f32[256,768]{1,0:T(8,128)} %pad_maximum_fusion.15.place_ref, ...), custom_call_target="tpu_custom_call" | custom-call | flops 15000000512 | bytes 20971520 | tf_op jit(solution)/shard_map/enc_forward/pallas_call | solution.py:458
  181.0 6.4 unpack_dec.1
  194.2 13.4 %dec_qkv.1 = (f32[2592,384]{1,0:T(8,128)}, bf16[2592,1152]{1,0:T(8,128)(2,1)}) custom-call(s32[256]{0:T(256)} %bitcast.326, f32[256]{0:T(256)} %copy-done.23, f32[256,384]{1,0:T(8,128)} %get-tuple-element.113.latent_ref, f32[2592,384]{1,0:T(8,128)} %pad_maximum_fusion.2.place_ref, f32[2592,128]{1,0:T(8,128)} %pad.44.row_ref.refs_9_, ...), custom_call_target="tpu_custom_call" | custom-call | flops 10000000000 | bytes 16777216 | tf_op jit(solution)/shard_map/dec_qkv/pallas_call | solution.py:143
  207.6 63.1 %dec_attend.1 = (bf16[2592,384]{1,0:T(8,128)(2,1)}, f32[9,8,864]{2,1,0:T(8,128)}) custom-call(bf16[2592,1152]{1,0:T(8,128)(2,1)} %get-tuple-element.118.q_ref.k_ref.v_ref, bf16[2592,1152]{1,0:T(8,128)(2,1)} %get-tuple-element.118.q_ref.k_ref.v_ref, bf16[2592,1152]{1,0:T(8,128)(2,1)} %get-tuple-element.118.q_ref.k_ref.v_ref, ...), custom_call_target="tpu_custom_call" | custom-call | flops 60000002048 | bytes 16777216 | tf_op jit(solution)/shard_map/dec_attend/pallas_call | solution.py:174
  270.7 62.4 %dec_mlp.1 = (bf16[2592,384]{1,0:T(8,128)(2,1)}, f32[2592,384]{1,0:T(8,128)}, f32[3,8,864]{2,1,0:T(8,128)}, f32[384,384]{1,0:T(8,128)}, f32[384,1536]{1,0:T(8,12...) custom-call(f32[2592,384]{1,0:T(8,128)} %get-tuple-element.117.x_ref, ...), custom_call_target="tpu_custom_call" | custom-call | tf_op jit(solution)/shard_map/dec_mlp/pallas_call | solution.py:332
  333.2 8.2 %pack_dec.1 = (f32[8,128]{1,0:T(8,128)}, f32[8,2,304,128]{3,2,1,0:T(8,128)}, f32[8,2,288,128]{3,2,1,0:T(8,128)}, f32[8,2,304,128]{3,2,1,0:T(8,128)}, f32[8,2,288,128]{3,2,1,0:T(8,128)}) custom-call(s32[1]{0:T(128)} %bitcast.core_ref, f32[384,384]{1,0:T(8,128)} %get-tuple-element.125.refs_0_, f32[384,1536]{1,0:T(8,128)} %get-tuple-element.126.refs_1_, ...), custom_call_target="tpu_custom_call" | custom-call | bytes 31457280 | tf_op jit(solution)/shard_map/pack_dec/pallas_call | solution.py:925
  341.9 39.9 %dec_attend_back.3 = (bf16[2592,128]{1,0:T(8,128)(2,1)}, bf16[2592,128]{1,0:T(8,128)(2,1)}, bf16[2592,128]{1,0:T(8,128)(2,1)}) custom-call(bf16[2592,1152]{1,0:T(8,128)(2,1)} %get-tuple-element.118.q_ref.k_ref.v_ref, bf16[2592,1152]{1,0:T(8,128)(2,1)} %get-tuple-element.118.q_ref.k_ref.v_ref, bf16[2592,1152]{1,0:T(8,128)(2,1)} %get-tuple-element.118.q_ref.k_ref.v_ref, ...), custom_call_target="tpu_custom_call" | custom-call | flops 40000000000 | bytes 8388608 | tf_op jit(solution)/shard_map/dec_attend_back/pallas_call | solution.py:246
  392.8 40.0 %dec_attend_back.4 = (bf16[2592,128]{1,0:T(8,128)(2,1)}, bf16[2592,128]{1,0:T(8,128)(2,1)}, bf16[2592,128]{1,0:T(8,128)(2,1)}) custom-call(bf16[2592,1152]{1,0:T(8,128)(2,1)} %get-tuple-element.118.q_ref.k_ref.v_ref, bf16[2592,1152]{1,0:T(8,128)(2,1)} %get-tuple-element.118.q_ref.k_ref.v_ref, bf16[2592,1152]{1,0:T(8,128)(2,1)} %get-tuple-element.118.q_ref.k_ref.v_ref, ...), custom_call_target="tpu_custom_call" | custom-call | flops 40000000000 | bytes 8388608 | tf_op jit(solution)/shard_map/dec_attend_back/pallas_call | solution.py:246
  438.7 40.4 %dec_attend_back.5 = (bf16[2592,128]{1,0:T(8,128)(2,1)}, bf16[2592,128]{1,0:T(8,128)(2,1)}, bf16[2592,128]{1,0:T(8,128)(2,1)}) custom-call(bf16[2592,1152]{1,0:T(8,128)(2,1)} %get-tuple-element.118.q_ref.k_ref.v_ref, bf16[2592,1152]{1,0:T(8,128)(2,1)} %get-tuple-element.118.q_ref.k_ref.v_ref, bf16[2592,1152]{1,0:T(8,128)(2,1)} %get-tuple-element.118.q_ref.k_ref.v_ref, ...), custom_call_target="tpu_custom_call" | custom-call | flops 40000000000 | bytes 8388608 | tf_op jit(solution)/shard_map/dec_attend_back/pallas_call | solution.py:246
  482.3 14.1 %dec_qkv_back.1 = (f32[2592,384]{1,0:T(8,128)}, f32[384,1152]{1,0:T(8,128)}, f32[8,1152]{1,0:T(8,128)}) custom-call(f32[2592,384]{1,0:T(8,128)} %get-tuple-element.117.x_ref, f32[2592,384]{1,0:T(8,128)} %get-tuple-element.164.dx_ref, bf16[2592,128]{1,0:T(8,128)(2,1)} %get-tuple-element.165.refs_0_, bf16[2592,128]{1,0:T(8,128)(2,1)} %get-tuple-element.166.refs_1_, ...), custom_call_target="tpu_custom_call" | custom-call | flops 15000000512 | bytes 8388608 | tf_op jit(solution)/shard_map/dec_qkv_back/pallas_call | solution.py:373
  496.4 17.4 %enc_back_one.1 = (f32[264,768]{1,0:T(8,128)}, f32[8,128]{1,0:T(8,128)}, f32[8,2,1104,128]{3,2,1,0:T(8,128)}, f32[8,2,1104,128]{3,2,1,0:T(8,128)}, f32[8,2,1104,...) custom-call(s32[1]{0:T(128)} %bitcast.core_ref, s32[256]{0:T(256)} %bitcast.327, f32[256]{0:T(256)} %copy-done.23, ...), custom_call_target="tpu_custom_call" | custom-call | flops 20000000000 | bytes 31457280 | tf_op jit(solution)/shard_map/enc_back_one/pallas_call | solution.py:715
  514.6 17.3 %enc_back_two.1 = (f32[8,128]{1,0:T(8,128)}, f32[8,2,1104,128]{3,2,1,0:T(8,128)}, f32[8,2,1104,128]{3,2,1,0:T(8,128)}, f32[8,2,1104,128]{3,2,1,0:T(8,128)}, f32[8,2,1104,128]{3,2,1,0:T(8,128)}) custom-call(s32[1]{0:T(128)} %bitcast.core_ref, ...), custom_call_target="tpu_custom_call", output_to_operand_aliasing={{1}: (14, {}), {2}: (15, {}), {3}: (16, {}), {4}: (17, {})} | custom-call | flops 15000000512 | bytes 31457280 | tf_op jit(solution)/shard_map/enc_back_two/pallas_call | solution.py:752
  533.6 14.3 %collective-permute-done.27 = f32[8,2,1104,128]{3,2,1,0:T(8,128)} collective-permute-done((f32[8,2,1104,128]{3,2,1,0:T(8,128)}, f32[8,2,1104,128]{3,2,1,0:T(8,128)}, u32[]{:S(2)}, u32[]{:S(2)}) %collective-permute-start.27) | collective-permute-done | bytes 9044000 | tf_op jit(solution)/shard_map/ppermute | solution.py:951
  550.1 9.1 %dynamic-slice_add_fusion.1 = (f32[2,2,1,2,1104,128]{5,4,3,2,1,0:T(8,128)}, f32[2,2,1,2,1104,128]{5,4,3,2,1,0:T(8,128)S(1)}, f32[2,2,1,2,1104,128]{5,4,3,2,1,0:T(8,128)S(1)}) fusion(f32[2,2,2,2,1104,128]{5,4,3,2,1,0:T(8,128)} %bitcast.71, s32[]{:T(128)S(6)} %select_n.467, f32[2,2,2,2,1104,128]{5,4,3,2,1,0:T(8,128)} %bitcast.312, s32[]{:T(128)S(6)} %select_n.469), kind=kLoop, calls=%fused_computation.11 | loop fusion | flops 1130496 | bytes 31653896 | tf_op jit(solution)/shard_map/add | solution.py:1003
  562.3 5.9 dynamic-slice_add_fusion
  575.5 4.9 collective-permute-done.38
  580.3 31.8 %collective-permute-done.28 = f16[2,2,2,1112,128]{4,3,1,0,2:T(8,128)(2,1)} collective-permute-done((f16[2,2,2,1112,128]{4,3,1,0,2:T(8,128)(2,1)S(1)}, f16[2,2,2,1112,128]{4,3,1,0,2:T(8,128)(2,1)}, u32[]{:S(2)}, u32[]{:S(2)}) %collective-permute-start.28) | collective-permute-done | bytes 2277408 | tf_op jit(solution)/shard_map/ppermute | solution.py:951
  629.2 5.5 bitcast_add_fusion.1
  641.3 8.0 collective-permute-done.29
  654.1 8.5 %collective-permute-done.34 = f16[2,2,1112,128]{3,2,1,0:T(8,128)(2,1)} collective-permute-done((f16[2,2,1112,128]{3,2,1,0:T(8,128)(2,1)}, f16[2,2,1112,128]{3,2,1,0:T(8,128)(2,1)}, u32[]{:S(2)}, u32[]{:S(2)}) %collective-permute-start.34) | collective-permute-done | bytes 1138720 | tf_op jit(solution)/shard_map/ppermute | solution.py:951
  680.5 31.9 %collective-permute-done.30 = f16[2,1112,128]{2,1,0:T(8,128)(2,1)} collective-permute-done((f16[2,1112,128]{2,1,0:T(8,128)(2,1)}, f16[2,1112,128]{2,1,0:T(8,128)(2,1)}, u32[]{:S(2)}, u32[]{:S(2)}) %collective-permute-start.30) | collective-permute-done | bytes 569376 | tf_op jit(solution)/shard_map/ppermute | solution.py:951
  715.6 6.4 collective-permute-done.35
  726.3 7.8 collective-permute-done.31
  737.3 10.0 %collective-permute-done.36 = f32[1104,128]{1,0:T(8,128)S(1)} collective-permute-done((f32[1104,128]{1,0:T(8,128)S(1)}, f32[1104,128]{1,0:T(8,128)S(1)}, u32[]{:S(2)}, u32[]{:S(2)}) %collective-permute-start.36) | collective-permute-done | bytes 565280 | tf_op jit(solution)/shard_map/ppermute | solution.py:951
  788.2 7.7 multiply_subtract_fusion
  (318 shorter events, 205.5 us)
Async XLA Ops:
  5.3 31.4 %collective-permute-start.12 = (bf16[896,128]{1,0:T(8,128)(2,1)}, bf16[896,128]{1,0:T(8,128)(2,1)}, u32[]{:S(2)}, u32[]{:S(2)}) collective-permute-start(bf16[896,128]{1,0:T(8,128)(2,1)} %pad_maximum_fusion.23), channel_id=1, source_target_pairs={{0,4},{1,5},{2,6},{3,7},{4,0},{5,1},{6,2},{7,3},{8,12},{9,13},{10,... | collective-permute-start | bytes 688136 | tf_op jit(solution)/shard_map/ppermute | solution.py:951
  10.1 25.5 %collective-permute-start.6 = (bf16[864,128]{1,0:T(8,128)(2,1)}, bf16[864,128]{1,0:T(8,128)(2,1)}, u32[]{:S(2)}, u32[]{:S(2)}) collective-permute-start(bf16[864,128]{1,0:T(8,128)(2,1)} %pad_maximum_fusion.25), channel_id=1, source_target_pairs={{0,4},{1,5},{2,6},{3,7},{4,0},{5,1},{6,2},{7,3},{8,12},{9,13},{10,... | collective-permute-start | bytes 663560 | tf_op jit(solution)/shard_map/ppermute | solution.py:951
  16.1 23.7 %collective-permute-start = (bf16[928,128]{1,0:T(8,128)(2,1)S(1)}, bf16[928,128]{1,0:T(8,128)(2,1)S(1)}, u32[]{:S(2)}, u32[]{:S(2)}) collective-permute-start(bf16[928,128]{1,0:T(8,128)(2,1)S(1)} %pad_maximum_fusion.22), channel_id=1, source_target_pairs={{0,4},{1,5},{2,6},{3,7},{4,0},{5,1},{6,2},{7,3},{8,12},{9,13},{10,... | collective-permute-start | bytes 712712 | tf_op jit(solution)/shard_map/ppermute | solution.py:951
  50.9 20.8 %collective-permute-start.8 = (bf16[2,2,864,128]{3,2,1,0:T(8,128)(2,1)}, bf16[2,2,864,128]{3,2,1,0:T(8,128)(2,1)}, u32[]{:S(2)}, u32[]{:S(2)}) collective-permute-start(bf16[2,2,864,128]{3,2,1,0:T(8,128)(2,1)} %pad_maximum_fusion.14), channel_id=1, source_target_pairs={{0,1},{1,0},{2,3},{3,2},{4,5},{5,4},{6,7},{7,6},{8,9},{9,8},{10,11... | collective-permute-start | bytes 2654216 | tf_op jit(solution)/shard_map/ppermute | solution.py:951
  52.9 24.2 %collective-permute-start.2 = (bf16[2,2,928,128]{3,2,1,0:T(8,128)(2,1)S(1)}, bf16[2,2,928,128]{3,2,1,0:T(8,128)(2,1)}, u32[]{:S(2)}, u32[]{:S(2)}) collective-permute-start(bf16[2,2,928,128]{3,2,1,0:T(8,128)(2,1)S(1)} %pad_maximum_fusion.11), channel_id=1, source_target_pairs={{0,16},{1,17},{2,18},{3,19},{4,20},{5,21},{6,22},{7,23},{8,24},{9,... | collective-permute-start | bytes 2850824 | tf_op jit(solution)/shard_map/ppermute | solution.py:951
  60.3 33.3 %collective-permute-start.14 = (bf16[2,2,896,128]{3,2,1,0:T(8,128)(2,1)S(1)}, bf16[2,2,896,128]{3,2,1,0:T(8,128)(2,1)S(1)}, u32[]{:S(2)}, u32[]{:S(2)}) collective-permute-start(bf16[2,2,896,128]{3,2,1,0:T(8,128)(2,1)S(1)} %pad_maximum_fusion.12), channel_id=1, source_target_pairs={{0,16},{1,17},{2,18},{3,19},{4,20},{5,21},{6,22},{7,23},{8,24},{9,... | collective-permute-start | bytes 2752520 | tf_op jit(solution)/shard_map/ppermute | solution.py:951
  78.6 38.2 %collective-permute-start.3 = (bf16[2,2,2,928,128]{4,3,2,1,0:T(8,128)(2,1)S(1)}, bf16[2,2,2,928,128]{4,3,2,1,0:T(8,128)(2,1)}, u32[]{:S(2)}, u32[]{:S(2)}) collective-permute-start(bf16[2,2,2,928,128]{4,3,2,1,0:T(8,128)(2,1)S(1)} %pad_maximum_fusion.3), channel_id=1, source_target_pairs={{0,2},{1,3},{2,0},{3,1},{4,6},{5,7},{6,4},{7,5},{8,10},{9,11},{10,... | collective-permute-start | bytes 5701640 | tf_op jit(solution)/shard_map/ppermute | solution.py:951
  95.2 43.5 %collective-permute-start.15 = (bf16[2,2,2,896,128]{4,3,2,1,0:T(8,128)(2,1)}, bf16[2,2,2,896,128]{4,3,2,1,0:T(8,128)(2,1)}, u32[]{:S(2)}, u32[]{:S(2)}) collective-permute-start(bf16[2,2,2,896,128]{4,3,2,1,0:T(8,128)(2,1)} %pad_maximum_fusion.4), channel_id=1, source_target_pairs={{0,1},{1,0},{2,3},{3,2},{4,5},{5,4},{6,7},{7,6},{8,9},{9,8},{10,11... | collective-permute-start | bytes 5505032 | tf_op jit(solution)/shard_map/ppermute | solution.py:951
  96.0 43.2 %collective-permute-start.4 = (bf16[2,2,2,928,128]{4,3,2,1,0:T(8,128)(2,1)S(1)}, bf16[2,2,2,928,128]{4,3,2,1,0:T(8,128)(2,1)}, u32[]{:S(2)}, u32[]{:S(2)}) collective-permute-start(bf16[2,2,2,928,128]{4,3,2,1,0:T(8,128)(2,1)S(1)} %pad_maximum_fusion.3), channel_id=1, source_target_pairs={{0,8},{1,9},{2,10},{3,11},{4,12},{5,13},{6,14},{7,15},{8,0},{9,1},... | collective-permute-start | bytes 5701640 | tf_op jit(solution)/shard_map/ppermute | solution.py:951
  97.4 41.3 %collective-permute-start.9 = (bf16[2,2,2,864,128]{4,3,2,1,0:T(8,128)(2,1)}, bf16[2,2,2,864,128]{4,3,2,1,0:T(8,128)(2,1)}, u32[]{:S(2)}, u32[]{:S(2)}) collective-permute-start(bf16[2,2,2,864,128]{4,3,2,1,0:T(8,128)(2,1)} %pad_maximum_fusion.6), channel_id=1, source_target_pairs={{0,16},{1,17},{2,18},{3,19},{4,20},{5,21},{6,22},{7,23},{8,24},{9,... | collective-permute-start | bytes 5308424 | tf_op jit(solution)/shard_map/ppermute | solution.py:951
  116.7 27.9 %collective-permute-start.5 = (bf16[2,2,2,928,128]{4,3,2,1,0:T(8,128)(2,1)}, bf16[2,2,2,928,128]{4,3,2,1,0:T(8,128)(2,1)}, u32[]{:S(2)}, u32[]{:S(2)}) collective-permute-start(bf16[2,2,2,928,128]{4,3,2,1,0:T(8,128)(2,1)} %collective-permute-done.3), channel_id=1, source_target_pairs={{0,8},{1,9},{2,10},{3,11},{4,12},{5,13},{6,14},{7,15},{8,0},{9,1},... | collective-permute-start | bytes 5701640 | tf_op jit(solution)/shard_map/ppermute | solution.py:951
  118.3 27.1 %collective-permute-start.10 = (bf16[2,2,2,864,128]{4,3,2,1,0:T(8,128)(2,1)}, bf16[2,2,2,864,128]{4,3,2,1,0:T(8,128)(2,1)}, u32[]{:S(2)}, u32[]{:S(2)}) collective-permute-start(bf16[2,2,2,864,128]{4,3,2,1,0:T(8,128)(2,1)} %pad_maximum_fusion.6), channel_id=1, source_target_pairs={{0,8},{1,9},{2,10},{3,11},{4,12},{5,13},{6,14},{7,15},{8,0},{9,1},... | collective-permute-start | bytes 5308424 | tf_op jit(solution)/shard_map/ppermute | solution.py:951
  341.3 40.4 %collective-permute-start.19 = (f32[8,2,288,128]{3,2,1,0:T(8,128)}, f32[8,2,288,128]{3,2,1,0:T(8,128)S(1)}, u32[]{:S(2)}, u32[]{:S(2)}) collective-permute-start(f32[8,2,288,128]{3,2,1,0:T(8,128)} %get-tuple-element.137), channel_id=1, source_target_pairs={{0,8},{1,9},{2,10},{3,11},{4,12},{5,13},{6,14},{7,15},{8,0},{9,1},... | collective-permute-start | bytes 7077896 | tf_op jit(solution)/shard_map/ppermute | solution.py:951
  341.7 45.3 %collective-permute-start.18 = (f32[8,2,304,128]{3,2,1,0:T(8,128)}, f32[8,2,304,128]{3,2,1,0:T(8,128)}, u32[]{:S(2)}, u32[]{:S(2)}) collective-permute-start(f32[8,2,304,128]{3,2,1,0:T(8,128)} %get-tuple-element.134), channel_id=1, source_target_pairs={{0,8},{1,9},{2,10},{3,11},{4,12},{5,13},{6,14},{7,15},{8,0},{9,1},... | collective-permute-start | bytes 7471112 | tf_op jit(solution)/shard_map/ppermute | solution.py:951
  390.0 42.8 %collective-permute-start.21 = (f32[2,2,2,288,128]{4,3,2,1,0:T(8,128)}, f32[2,2,2,288,128]{4,3,2,1,0:T(8,128)S(1)}, u32[]{:S(2)}, u32[]{:S(2)}) collective-permute-start(f32[2,2,2,288,128]{4,3,2,1,0:T(8,128)} %get-tuple-element.145), channel_id=1, source_target_pairs={{0,16},{1,17},{2,18},{3,19},{4,20},{5,21},{6,22},{7,23},{8,24},{9,... | collective-permute-start | bytes 3538952 | tf_op jit(solution)/shard_map/ppermute | solution.py:951
  391.3 43.9 %collective-permute-start.20 = (f32[2,2,2,304,128]{4,3,2,1,0:T(8,128)}, f32[2,2,2,304,128]{4,3,2,1,0:T(8,128)}, u32[]{:S(2)}, u32[]{:S(2)}) collective-permute-start(f32[2,2,2,304,128]{4,3,2,1,0:T(8,128)} %get-tuple-element.143), channel_id=1, source_target_pairs={{0,1},{1,0},{2,3},{3,2},{4,5},{5,4},{6,7},{7,6},{8,9},{9,8},{10,11... | collective-permute-start | bytes 3735560 | tf_op jit(solution)/shard_map/ppermute | solution.py:951
  437.4 41.8 %collective-permute-start.23 = (f32[2,2,288,128]{3,2,1,0:T(8,128)S(1)}, f32[2,2,288,128]{3,2,1,0:T(8,128)S(1)}, u32[]{:S(2)}, u32[]{:S(2)}) collective-permute-start(f32[2,2,288,128]{3,2,1,0:T(8,128)S(1)} %get-tuple-element.153), channel_id=1, source_target_pairs={{0,1},{1,0},{2,3},{3,2},{4,5},{5,4},{6,7},{7,6},{8,9},{9,8},{10,11... | collective-permute-start | bytes 1769480 | tf_op jit(solution)/shard_map/ppermute | solution.py:951
  438.0 41.3 %collective-permute-start.22 = (f32[2,2,304,128]{3,2,1,0:T(8,128)}, f32[2,2,304,128]{3,2,1,0:T(8,128)S(1)}, u32[]{:S(2)}, u32[]{:S(2)}) collective-permute-start(f32[2,2,304,128]{3,2,1,0:T(8,128)} %get-tuple-element.152), channel_id=1, source_target_pairs={{0,16},{1,17},{2,18},{3,19},{4,20},{5,21},{6,22},{7,23},{8,24},{9,... | collective-permute-start | bytes 1867784 | tf_op jit(solution)/shard_map/ppermute | solution.py:951
  479.4 34.5 %collective-permute-start.25 = (f32[2,288,128]{2,1,0:T(8,128)S(1)}, f32[2,288,128]{2,1,0:T(8,128)S(1)}, u32[]{:S(2)}, u32[]{:S(2)}) collective-permute-start(f32[2,288,128]{2,1,0:T(8,128)S(1)} %get-tuple-element.180), channel_id=1, source_target_pairs={{0,4},{1,5},{2,6},{3,7},{4,0},{5,1},{6,2},{7,3},{8,12},{9,13},{10,... | collective-permute-start | bytes 884744 | tf_op jit(solution)/shard_map/ppermute | solution.py:951
  482.1 32.5 %collective-permute-start.24 = (f32[2,304,128]{2,1,0:T(8,128)S(1)}, f32[2,304,128]{2,1,0:T(8,128)S(1)}, u32[]{:S(2)}, u32[]{:S(2)}) collective-permute-start(f32[2,304,128]{2,1,0:T(8,128)S(1)} %get-tuple-element.179), channel_id=1, source_target_pairs={{0,4},{1,5},{2,6},{3,7},{4,0},{5,1},{6,2},{7,3},{8,12},{9,13},{10,... | collective-permute-start | bytes 933896 | tf_op jit(solution)/shard_map/ppermute | solution.py:951
  560.2 51.9 %collective-permute-start.28 = (f16[2,2,2,1112,128]{4,3,1,0,2:T(8,128)(2,1)S(1)}, f16[2,2,2,1112,128]{4,3,1,0,2:T(8,128)(2,1)}, u32[]{:S(2)}, u32[]{:S(2)}) collective-permute-start(f16[2,2,2,1112,128]{4,3,1,0,2:T(8,128)(2,1)S(1)} %concatenate.55), channel_id=1, source_target_pairs={{0,1},{1,0},{2,3},{3,2},{4,5},{5,4},{6,7},{7,6},{8,9},{9,8},{10,11... | collective-permute-start | bytes 6832136 | tf_op jit(solution)/shard_map/ppermute | solution.py:951
  570.6 51.9 %collective-permute-start.33 = (f16[2,2,2,1112,128]{4,3,1,0,2:T(8,128)(2,1)}, f16[2,2,2,1112,128]{4,3,1,0,2:T(8,128)(2,1)}, u32[]{:S(2)}, u32[]{:S(2)}) collective-permute-start(f16[2,2,2,1112,128]{4,3,1,0,2:T(8,128)(2,1)} %concatenate.58), channel_id=1, source_target_pairs={{0,16},{1,17},{2,18},{3,19},{4,20},{5,21},{6,22},{7,23},{8,24},{9,... | collective-permute-start | bytes 6832136 | tf_op jit(solution)/shard_map/ppermute | solution.py:951
  575.3 62.8 %collective-permute-start.37 = (f32[304,128]{1,0:T(8,128)S(1)}, f32[304,128]{1,0:T(8,128)}, u32[]{:S(2)}, u32[]{:S(2)}) collective-permute-start(f32[304,128]{1,0:T(8,128)S(1)} %fusion.34), channel_id=1, source_target_pairs={{0,2},{1,3},{2,0},{3,1},{4,6},{5,7},{6,4},{7,5},{8,10},{9,11},{10,... | collective-permute-start | bytes 466952 | tf_op jit(solution)/shard_map/ppermute | solution.py:951
  621.0 28.3 %collective-permute-start.29 = (f16[2,2,1112,128]{3,2,1,0:T(8,128)(2,1)}, f16[2,2,1112,128]{3,2,1,0:T(8,128)(2,1)}, u32[]{:S(2)}, u32[]{:S(2)}) collective-permute-start(f16[2,2,1112,128]{3,2,1,0:T(8,128)(2,1)} %concatenate.56), channel_id=1, source_target_pairs={{0,16},{1,17},{2,18},{3,19},{4,20},{5,21},{6,22},{7,23},{8,24},{9,... | collective-permute-start | bytes 3416072 | tf_op jit(solution)/shard_map/ppermute | solution.py:951
  635.9 26.6 %collective-permute-start.34 = (f16[2,2,1112,128]{3,2,1,0:T(8,128)(2,1)}, f16[2,2,1112,128]{3,2,1,0:T(8,128)(2,1)}, u32[]{:S(2)}, u32[]{:S(2)}) collective-permute-start(f16[2,2,1112,128]{3,2,1,0:T(8,128)(2,1)} %concatenate.59), channel_id=1, source_target_pairs={{0,1},{1,0},{2,3},{3,2},{4,5},{5,4},{6,7},{7,6},{8,9},{9,8},{10,11... | collective-permute-start | bytes 3416072 | tf_op jit(solution)/shard_map/ppermute | solution.py:951
  639.9 36.3 %collective-permute-start.48 = (f32[592,128]{1,0:T(8,128)}, f32[592,128]{1,0:T(8,128)}, u32[]{:S(2)}, u32[]{:S(2)}) collective-permute-start(f32[592,128]{1,0:T(8,128)} %pad_maximum_fusion.21), channel_id=1, source_target_pairs={{0,16},{1,17},{2,18},{3,19},{4,20},{5,21},{6,22},{7,23},{8,24},{9,... | collective-permute-start | bytes 909320 | tf_op jit(solution)/shard_map/ppermute | solution.py:951
  671.0 41.4 %collective-permute-start.30 = (f16[2,1112,128]{2,1,0:T(8,128)(2,1)}, f16[2,1112,128]{2,1,0:T(8,128)(2,1)}, u32[]{:S(2)}, u32[]{:S(2)}) collective-permute-start(f16[2,1112,128]{2,1,0:T(8,128)(2,1)} %concatenate.57), channel_id=1, source_target_pairs={{0,4},{1,5},{2,6},{3,7},{4,0},{5,1},{6,2},{7,3},{8,12},{9,13},{10,... | collective-permute-start | bytes 1708040 | tf_op jit(solution)/shard_map/ppermute | solution.py:951
  679.0 45.2 %collective-permute-start.49 = (f32[2,592,128]{2,1,0:T(8,128)}, f32[2,592,128]{2,1,0:T(8,128)}, u32[]{:S(2)}, u32[]{:S(2)}) collective-permute-start(f32[2,592,128]{2,1,0:T(8,128)} %pad_maximum_fusion.16), channel_id=1, source_target_pairs={{0,8},{1,9},{2,10},{3,11},{4,12},{5,13},{6,14},{7,15},{8,0},{9,1},... | collective-permute-start | bytes 1818632 | tf_op jit(solution)/shard_map/ppermute | solution.py:951
  680.1 41.9 %collective-permute-start.35 = (f16[2,1112,128]{2,1,0:T(8,128)(2,1)S(1)}, f16[2,1112,128]{2,1,0:T(8,128)(2,1)S(1)}, u32[]{:S(2)}, u32[]{:S(2)}) collective-permute-start(f16[2,1112,128]{2,1,0:T(8,128)(2,1)S(1)} %concatenate.60), channel_id=1, source_target_pairs={{0,4},{1,5},{2,6},{3,7},{4,0},{5,1},{6,2},{7,3},{8,12},{9,13},{10,... | collective-permute-start | bytes 1708040 | tf_op jit(solution)/shard_map/ppermute | solution.py:951
  715.5 18.5 %collective-permute-start.31 = (f32[1104,128]{1,0:T(8,128)S(1)}, f32[1104,128]{1,0:T(8,128)S(1)}, u32[]{:S(2)}, u32[]{:S(2)}) collective-permute-start(f32[1104,128]{1,0:T(8,128)S(1)} %fusion.31), channel_id=1, source_target_pairs={{0,2},{1,3},{2,0},{3,1},{4,6},{5,7},{6,4},{7,5},{8,10},{9,11},{10,... | collective-permute-start | bytes 1695752 | tf_op jit(solution)/shard_map/ppermute | solution.py:951
  723.4 23.9 %collective-permute-start.36 = (f32[1104,128]{1,0:T(8,128)S(1)}, f32[1104,128]{1,0:T(8,128)S(1)}, u32[]{:S(2)}, u32[]{:S(2)}) collective-permute-start(f32[1104,128]{1,0:T(8,128)S(1)} %fusion.30), channel_id=1, source_target_pairs={{0,2},{1,3},{2,0},{3,1},{4,6},{5,7},{6,4},{7,5},{8,10},{9,11},{10,... | collective-permute-start | bytes 1695752 | tf_op jit(solution)/shard_map/ppermute | solution.py:951
  734.2 34.8 %collective-permute-start.44 = (f32[1104,128]{1,0:T(8,128)S(1)}, f32[1104,128]{1,0:T(8,128)S(1)}, u32[]{:S(2)}, u32[]{:S(2)}) collective-permute-start(f32[1104,128]{1,0:T(8,128)S(1)} %bitcast_add_fusion.16), channel_id=1, source_target_pairs={{0,16},{1,17},{2,18},{3,19},{4,20},{5,21},{6,22},{7,23},{8,24},{9,... | collective-permute-start | bytes 1695752 | tf_op jit(solution)/shard_map/ppermute | solution.py:951
  (55 other events, 594.6 us)

commit v6 on v5

--- a/solution.py
+++ b/solution.py
@@ -126,7 +126,7 @@
         return carry
 
     lax.fori_loop(0, latent_ref.shape[0], add_slot, 0, unroll=8)
-    bm = 432
+    bm = 864
 
     def block(i, carry):
         part = pl.ds(pl.multiple_of(i * bm, 16), bm)
@@ -367,7 +367,7 @@
     gv_ref[3:4, :DD] += total(dx * row_ref[:, 2:3])
 
 
-def qkv_back(x, dx, dqkv, rows, w, vec, bm=432):
+def qkv_back(x, dx, dqkv, rows, w, vec, bm=864):
     full = lambda shape: pl.BlockSpec(shape, lambda i: (0, 0))
     part = lambda width: pl.BlockSpec((bm, width), lambda i: (i, 0))
     return pl.pallas_call(

time: 812 us -> 810 us (level)
  no operation moved by 1% of the time
where the time goes in v6:
time: 810 us; the launch traced here: 802 us
  Pallas kernels  355 us (44%)
  waiting for transfers between devices  219 us (27%)
  other arithmetic  129 us (16%)
  starting transfers between devices  56.4 us (7%)
  local copies, waits for them, and re-layouts  27.1 us (3%)
  between operations  16.4 us (2%)
    ppermute x55, waiting for transfers between devices, swap(): return lax.ppermute(value, AXES, pairs)  219 us
    pallas_call x3, Pallas kernels, attend_back(): pl.pallas_call(functools.partial(attend_back_kernel, h, kc), grid=(nq,),...  120 us
    pallas_call x1, Pallas kernels, attend_forward(): pl.pallas_call(attend_kernel, grid=(3, nq), in_specs=[pl.BlockSpec((bq, 1...  63.1 us
    pallas_call x1, Pallas kernels, mlp_both(): pl.pallas_call(mlp_kernel, grid=(ROWS // bm,), in_specs=[part(DD), part(D...  62.5 us
    ppermute x55, starting transfers between devices, swap(): return lax.ppermute(value, AXES, pairs)  56.4 us
    add x15, other arithmetic, take(): return cut(self.kept) + cut(self.other)  38.2 us
    pallas_call x2, Pallas kernels, unpack_flat(): pl.pallas_call(functools.partial(unpack_kernel, pieces, groups, leads, wa...  25 us
    another operation x34, other arithmetic, step(): jnp.stack([jnp.where(low, self.value, other), jnp.where(low, other, self....  22.4 us
  transfers between devices with their start and end apart: 55, of which 28 were waited for; matrix products, arithmetic and copies ran while one was open for 16% of the time, Pallas kernels for 19%

profile of v6, /device:TPU:0, one launch (start us, length us, event | category | flops | bytes accessed | tf_op | source)
XLA Modules:
  0.0 802.5 jit_solution(14446390730358378540)
XLA Ops:
  21.0 14.6 %collective-permute-done.6 = bf16[864,128]{1,0:T(8,128)(2,1)} collective-permute-done((bf16[864,128]{1,0:T(8,128)(2,1)}, bf16[864,128]{1,0:T(8,128)(2,1)}, u32[]{:S(2)}, u32[]{:S(2)}) %collective-permute-start.6) | collective-permute-done | bytes 221216 | tf_op jit(solution)/shard_map/ppermute | solution.py:951
  43.0 6.8 collective-permute-done.7
  62.0 9.7 %collective-permute-done.8 = bf16[2,2,864,128]{3,2,1,0:T(8,128)(2,1)} collective-permute-done((bf16[2,2,864,128]{3,2,1,0:T(8,128)(2,1)}, bf16[2,2,864,128]{3,2,1,0:T(8,128)(2,1)}, u32[]{:S(2)}, u32[]{:S(2)}) %collective-permute-start.8) | collective-permute-done | bytes 884768 | tf_op jit(solution)/shard_map/ppermute | solution.py:951
  80.3 13.3 %collective-permute-done.14 = bf16[2,2,896,128]{3,2,1,0:T(8,128)(2,1)S(1)} collective-permute-done((bf16[2,2,896,128]{3,2,1,0:T(8,128)(2,1)S(1)}, bf16[2,2,896,128]{3,2,1,0:T(8,128)(2,1)S(1)}, u32[]{:S(2)}, u32[]{:S(2)}) %collective-permute-start.14) | collective-permute-done | bytes 917536 | tf_op jit(solution)/shard_map/ppermute | solution.py:951
  100.1 10.6 %multiply_sine_fusion = (f32[2592,192]{1,0:T(8,128)S(1)}, f32[2592,192]{1,0:T(8,128)S(1)}) fusion(f32[192]{0:T(256)S(1)} %multiply_exponential_fusion.1, f32[2592]{0:T(1024)S(1)} %fusion.36), kind=kLoop, calls=%fused_computation.22 | loop fusion | flops 497664 | bytes 3992448 | tf_op jit(solution)/shard_map/sin | solution.py:56
  118.8 19.9 %collective-permute-done.9 = bf16[2,2,2,864,128]{4,3,2,1,0:T(8,128)(2,1)} collective-permute-done((bf16[2,2,2,864,128]{4,3,2,1,0:T(8,128)(2,1)}, bf16[2,2,2,864,128]{4,3,2,1,0:T(8,128)(2,1)}, u32[]{:S(2)}, u32[]{:S(2)}) %collective-permute-start.9) | collective-permute-done | bytes 1769504 | tf_op jit(solution)/shard_map/ppermute | solution.py:951
  148.0 18.4 %unpack_enc.1 = (bf16[1536,768]{1,0:T(8,128)(2,1)}, bf16[768,2304]{1,0:T(8,128)(2,1)}, bf16[768,768]{1,0:T(8,128)(2,1)}, bf16[768,3072]{1,0:T(8,128)(2,1)}, bf16...) custom-call(s32[4]{0:T(128)} %pad_add_fusion.mine_ref, bf16[8,928,128]{2,1,0:T(8,128)(2,1)} %bitcast.310, ...), custom_call_target="tpu_custom_call" | custom-call | bytes 102776832 | tf_op jit(solution)/shard_map/unpack_enc/pallas_call | solution.py:878
  166.4 14.6 %enc_forward.1 = (f32[256,384]{1,0:T(8,128)}, f32[256,768]{1,0:T(8,128)}, bf16[256,2304]{1,0:T(8,128)(2,1)}, bf16[256,768]{1,0:T(8,128)(2,1)}, f32[256,768]{1,0:...) custom-call(bf16[256,1536]{1,0:T(8,128)(2,1)} %pix_ref.3, f32[256,768]{1,0:T(8,128)} %pad_maximum_fusion.15.place_ref, ...), custom_call_target="tpu_custom_call" | custom-call | flops 15000000512 | bytes 20971520 | tf_op jit(solution)/shard_map/enc_forward/pallas_call | solution.py:458
  181.0 6.6 unpack_dec.1
  194.4 11.8 %dec_qkv.1 = (f32[2592,384]{1,0:T(8,128)}, bf16[2592,1152]{1,0:T(8,128)(2,1)}) custom-call(s32[256]{0:T(256)} %bitcast.326, f32[256]{0:T(256)} %copy-done.23, f32[256,384]{1,0:T(8,128)} %get-tuple-element.113.latent_ref, f32[2592,384]{1,0:T(8,128)} %pad_maximum_fusion.2.place_ref, f32[2592,128]{1,0:T(8,128)} %pad.44.row_ref.refs_9_, ...), custom_call_target="tpu_custom_call" | custom-call | flops 10000000000 | bytes 16777216 | tf_op jit(solution)/shard_map/dec_qkv/pallas_call | solution.py:143
  206.3 63.1 %dec_attend.1 = (bf16[2592,384]{1,0:T(8,128)(2,1)}, f32[9,8,864]{2,1,0:T(8,128)}) custom-call(bf16[2592,1152]{1,0:T(8,128)(2,1)} %get-tuple-element.118.q_ref.k_ref.v_ref, bf16[2592,1152]{1,0:T(8,128)(2,1)} %get-tuple-element.118.q_ref.k_ref.v_ref, bf16[2592,1152]{1,0:T(8,128)(2,1)} %get-tuple-element.118.q_ref.k_ref.v_ref, ...), custom_call_target="tpu_custom_call" | custom-call | flops 60000002048 | bytes 16777216 | tf_op jit(solution)/shard_map/dec_attend/pallas_call | solution.py:174
  269.4 62.5 %dec_mlp.1 = (bf16[2592,384]{1,0:T(8,128)(2,1)}, f32[2592,384]{1,0:T(8,128)}, f32[3,8,864]{2,1,0:T(8,128)}, f32[384,384]{1,0:T(8,128)}, f32[384,1536]{1,0:T(8,12...) custom-call(f32[2592,384]{1,0:T(8,128)} %get-tuple-element.117.x_ref, ...), custom_call_target="tpu_custom_call" | custom-call | tf_op jit(solution)/shard_map/dec_mlp/pallas_call | solution.py:332
  331.9 8.2 %pack_dec.1 = (f32[8,128]{1,0:T(8,128)}, f32[8,2,304,128]{3,2,1,0:T(8,128)}, f32[8,2,288,128]{3,2,1,0:T(8,128)}, f32[8,2,304,128]{3,2,1,0:T(8,128)}, f32[8,2,288,128]{3,2,1,0:T(8,128)}) custom-call(s32[1]{0:T(128)} %bitcast.core_ref, f32[384,384]{1,0:T(8,128)} %get-tuple-element.125.refs_0_, f32[384,1536]{1,0:T(8,128)} %get-tuple-element.126.refs_1_, ...), custom_call_target="tpu_custom_call" | custom-call | bytes 31457280 | tf_op jit(solution)/shard_map/pack_dec/pallas_call | solution.py:925
  340.6 39.9 %dec_attend_back.3 = (bf16[2592,128]{1,0:T(8,128)(2,1)}, bf16[2592,128]{1,0:T(8,128)(2,1)}, bf16[2592,128]{1,0:T(8,128)(2,1)}) custom-call(bf16[2592,1152]{1,0:T(8,128)(2,1)} %get-tuple-element.118.q_ref.k_ref.v_ref, bf16[2592,1152]{1,0:T(8,128)(2,1)} %get-tuple-element.118.q_ref.k_ref.v_ref, bf16[2592,1152]{1,0:T(8,128)(2,1)} %get-tuple-element.118.q_ref.k_ref.v_ref, ...), custom_call_target="tpu_custom_call" | custom-call | flops 40000000000 | bytes 8388608 | tf_op jit(solution)/shard_map/dec_attend_back/pallas_call | solution.py:246
  391.5 40.2 %dec_attend_back.4 = (bf16[2592,128]{1,0:T(8,128)(2,1)}, bf16[2592,128]{1,0:T(8,128)(2,1)}, bf16[2592,128]{1,0:T(8,128)(2,1)}) custom-call(bf16[2592,1152]{1,0:T(8,128)(2,1)} %get-tuple-element.118.q_ref.k_ref.v_ref, bf16[2592,1152]{1,0:T(8,128)(2,1)} %get-tuple-element.118.q_ref.k_ref.v_ref, bf16[2592,1152]{1,0:T(8,128)(2,1)} %get-tuple-element.118.q_ref.k_ref.v_ref, ...), custom_call_target="tpu_custom_call" | custom-call | flops 40000000000 | bytes 8388608 | tf_op jit(solution)/shard_map/dec_attend_back/pallas_call | solution.py:246
  437.7 40.2 %dec_attend_back.5 = (bf16[2592,128]{1,0:T(8,128)(2,1)}, bf16[2592,128]{1,0:T(8,128)(2,1)}, bf16[2592,128]{1,0:T(8,128)(2,1)}) custom-call(bf16[2592,1152]{1,0:T(8,128)(2,1)} %get-tuple-element.118.q_ref.k_ref.v_ref, bf16[2592,1152]{1,0:T(8,128)(2,1)} %get-tuple-element.118.q_ref.k_ref.v_ref, bf16[2592,1152]{1,0:T(8,128)(2,1)} %get-tuple-element.118.q_ref.k_ref.v_ref, ...), custom_call_target="tpu_custom_call" | custom-call | flops 40000000000 | bytes 8388608 | tf_op jit(solution)/shard_map/dec_attend_back/pallas_call | solution.py:246
  481.1 14.1 %dec_qkv_back.1 = (f32[2592,384]{1,0:T(8,128)}, f32[384,1152]{1,0:T(8,128)}, f32[8,1152]{1,0:T(8,128)}) custom-call(f32[2592,384]{1,0:T(8,128)} %get-tuple-element.117.x_ref, f32[2592,384]{1,0:T(8,128)} %get-tuple-element.164.dx_ref, bf16[2592,128]{1,0:T(8,128)(2,1)} %get-tuple-element.165.refs_0_, bf16[2592,128]{1,0:T(8,128)(2,1)} %get-tuple-element.166.refs_1_, ...), custom_call_target="tpu_custom_call" | custom-call | flops 15000000512 | bytes 8388608 | tf_op jit(solution)/shard_map/dec_qkv_back/pallas_call | solution.py:373
  495.2 17.4 %enc_back_one.1 = (f32[264,768]{1,0:T(8,128)}, f32[8,128]{1,0:T(8,128)}, f32[8,2,1104,128]{3,2,1,0:T(8,128)}, f32[8,2,1104,128]{3,2,1,0:T(8,128)}, f32[8,2,1104,...) custom-call(s32[1]{0:T(128)} %bitcast.core_ref, s32[256]{0:T(256)} %bitcast.327, f32[256]{0:T(256)} %copy-done.23, ...), custom_call_target="tpu_custom_call" | custom-call | flops 20000000000 | bytes 31457280 | tf_op jit(solution)/shard_map/enc_back_one/pallas_call | solution.py:715
  513.4 17.5 %enc_back_two.1 = (f32[8,128]{1,0:T(8,128)}, f32[8,2,1104,128]{3,2,1,0:T(8,128)}, f32[8,2,1104,128]{3,2,1,0:T(8,128)}, f32[8,2,1104,128]{3,2,1,0:T(8,128)}, f32[8,2,1104,128]{3,2,1,0:T(8,128)}) custom-call(s32[1]{0:T(128)} %bitcast.core_ref, ...), custom_call_target="tpu_custom_call", output_to_operand_aliasing={{1}: (14, {}), {2}: (15, {}), {3}: (16, {}), {4}: (17, {})} | custom-call | flops 15000000512 | bytes 31457280 | tf_op jit(solution)/shard_map/enc_back_two/pallas_call | solution.py:752
  532.5 14.3 %collective-permute-done.27 = f32[8,2,1104,128]{3,2,1,0:T(8,128)} collective-permute-done((f32[8,2,1104,128]{3,2,1,0:T(8,128)}, f32[8,2,1104,128]{3,2,1,0:T(8,128)}, u32[]{:S(2)}, u32[]{:S(2)}) %collective-permute-start.27) | collective-permute-done | bytes 9044000 | tf_op jit(solution)/shard_map/ppermute | solution.py:951
  549.0 9.1 %dynamic-slice_add_fusion.1 = (f32[2,2,1,2,1104,128]{5,4,3,2,1,0:T(8,128)}, f32[2,2,1,2,1104,128]{5,4,3,2,1,0:T(8,128)S(1)}, f32[2,2,1,2,1104,128]{5,4,3,2,1,0:T(8,128)S(1)}) fusion(f32[2,2,2,2,1104,128]{5,4,3,2,1,0:T(8,128)} %bitcast.71, s32[]{:T(128)S(6)} %select_n.467, f32[2,2,2,2,1104,128]{5,4,3,2,1,0:T(8,128)} %bitcast.312, s32[]{:T(128)S(6)} %select_n.469), kind=kLoop, calls=%fused_computation.11 | loop fusion | flops 1130496 | bytes 31653896 | tf_op jit(solution)/shard_map/add | solution.py:1003
  561.2 5.8 dynamic-slice_add_fusion
  574.3 4.9 collective-permute-done.38
  579.2 31.9 %collective-permute-done.28 = f16[2,2,2,1112,128]{4,3,1,0,2:T(8,128)(2,1)} collective-permute-done((f16[2,2,2,1112,128]{4,3,1,0,2:T(8,128)(2,1)S(1)}, f16[2,2,2,1112,128]{4,3,1,0,2:T(8,128)(2,1)}, u32[]{:S(2)}, u32[]{:S(2)}) %collective-permute-start.28) | collective-permute-done | bytes 2277408 | tf_op jit(solution)/shard_map/ppermute | solution.py:951
  628.1 5.5 bitcast_add_fusion.1
  640.3 8.0 collective-permute-done.29
  653.0 8.4 %collective-permute-done.34 = f16[2,2,1112,128]{3,2,1,0:T(8,128)(2,1)} collective-permute-done((f16[2,2,1112,128]{3,2,1,0:T(8,128)(2,1)}, f16[2,2,1112,128]{3,2,1,0:T(8,128)(2,1)}, u32[]{:S(2)}, u32[]{:S(2)}) %collective-permute-start.34) | collective-permute-done | bytes 1138720 | tf_op jit(solution)/shard_map/ppermute | solution.py:951
  679.3 31.9 %collective-permute-done.30 = f16[2,1112,128]{2,1,0:T(8,128)(2,1)} collective-permute-done((f16[2,1112,128]{2,1,0:T(8,128)(2,1)}, f16[2,1112,128]{2,1,0:T(8,128)(2,1)}, u32[]{:S(2)}, u32[]{:S(2)}) %collective-permute-start.30) | collective-permute-done | bytes 569376 | tf_op jit(solution)/shard_map/ppermute | solution.py:951
  714.5 6.4 collective-permute-done.35
  725.1 7.8 collective-permute-done.31
  736.3 9.9 %collective-permute-done.36 = f32[1104,128]{1,0:T(8,128)S(1)} collective-permute-done((f32[1104,128]{1,0:T(8,128)S(1)}, f32[1104,128]{1,0:T(8,128)S(1)}, u32[]{:S(2)}, u32[]{:S(2)}) %collective-permute-start.36) | collective-permute-done | bytes 565280 | tf_op jit(solution)/shard_map/ppermute | solution.py:951
  787.1 7.6 multiply_subtract_fusion
  (318 shorter events, 205.2 us)
Async XLA Ops:
  5.3 31.4 %collective-permute-start.12 = (bf16[896,128]{1,0:T(8,128)(2,1)}, bf16[896,128]{1,0:T(8,128)(2,1)}, u32[]{:S(2)}, u32[]{:S(2)}) collective-permute-start(bf16[896,128]{1,0:T(8,128)(2,1)} %pad_maximum_fusion.23), channel_id=1, source_target_pairs={{0,4},{1,5},{2,6},{3,7},{4,0},{5,1},{6,2},{7,3},{8,12},{9,13},{10,... | collective-permute-start | bytes 688136 | tf_op jit(solution)/shard_map/ppermute | solution.py:951
  10.1 25.5 %collective-permute-start.6 = (bf16[864,128]{1,0:T(8,128)(2,1)}, bf16[864,128]{1,0:T(8,128)(2,1)}, u32[]{:S(2)}, u32[]{:S(2)}) collective-permute-start(bf16[864,128]{1,0:T(8,128)(2,1)} %pad_maximum_fusion.25), channel_id=1, source_target_pairs={{0,4},{1,5},{2,6},{3,7},{4,0},{5,1},{6,2},{7,3},{8,12},{9,13},{10,... | collective-permute-start | bytes 663560 | tf_op jit(solution)/shard_map/ppermute | solution.py:951
  16.1 23.7 %collective-permute-start = (bf16[928,128]{1,0:T(8,128)(2,1)S(1)}, bf16[928,128]{1,0:T(8,128)(2,1)S(1)}, u32[]{:S(2)}, u32[]{:S(2)}) collective-permute-start(bf16[928,128]{1,0:T(8,128)(2,1)S(1)} %pad_maximum_fusion.22), channel_id=1, source_target_pairs={{0,4},{1,5},{2,6},{3,7},{4,0},{5,1},{6,2},{7,3},{8,12},{9,13},{10,... | collective-permute-start | bytes 712712 | tf_op jit(solution)/shard_map/ppermute | solution.py:951
  50.9 20.8 %collective-permute-start.8 = (bf16[2,2,864,128]{3,2,1,0:T(8,128)(2,1)}, bf16[2,2,864,128]{3,2,1,0:T(8,128)(2,1)}, u32[]{:S(2)}, u32[]{:S(2)}) collective-permute-start(bf16[2,2,864,128]{3,2,1,0:T(8,128)(2,1)} %pad_maximum_fusion.14), channel_id=1, source_target_pairs={{0,1},{1,0},{2,3},{3,2},{4,5},{5,4},{6,7},{7,6},{8,9},{9,8},{10,11... | collective-permute-start | bytes 2654216 | tf_op jit(solution)/shard_map/ppermute | solution.py:951
  52.9 24.2 %collective-permute-start.2 = (bf16[2,2,928,128]{3,2,1,0:T(8,128)(2,1)S(1)}, bf16[2,2,928,128]{3,2,1,0:T(8,128)(2,1)}, u32[]{:S(2)}, u32[]{:S(2)}) collective-permute-start(bf16[2,2,928,128]{3,2,1,0:T(8,128)(2,1)S(1)} %pad_maximum_fusion.11), channel_id=1, source_target_pairs={{0,16},{1,17},{2,18},{3,19},{4,20},{5,21},{6,22},{7,23},{8,24},{9,... | collective-permute-start | bytes 2850824 | tf_op jit(solution)/shard_map/ppermute | solution.py:951
  60.3 33.3 %collective-permute-start.14 = (bf16[2,2,896,128]{3,2,1,0:T(8,128)(2,1)S(1)}, bf16[2,2,896,128]{3,2,1,0:T(8,128)(2,1)S(1)}, u32[]{:S(2)}, u32[]{:S(2)}) collective-permute-start(bf16[2,2,896,128]{3,2,1,0:T(8,128)(2,1)S(1)} %pad_maximum_fusion.12), channel_id=1, source_target_pairs={{0,16},{1,17},{2,18},{3,19},{4,20},{5,21},{6,22},{7,23},{8,24},{9,... | collective-permute-start | bytes 2752520 | tf_op jit(solution)/shard_map/ppermute | solution.py:951
  78.6 38.2 %collective-permute-start.3 = (bf16[2,2,2,928,128]{4,3,2,1,0:T(8,128)(2,1)S(1)}, bf16[2,2,2,928,128]{4,3,2,1,0:T(8,128)(2,1)}, u32[]{:S(2)}, u32[]{:S(2)}) collective-permute-start(bf16[2,2,2,928,128]{4,3,2,1,0:T(8,128)(2,1)S(1)} %pad_maximum_fusion.3), channel_id=1, source_target_pairs={{0,2},{1,3},{2,0},{3,1},{4,6},{5,7},{6,4},{7,5},{8,10},{9,11},{10,... | collective-permute-start | bytes 5701640 | tf_op jit(solution)/shard_map/ppermute | solution.py:951
  95.2 43.5 %collective-permute-start.15 = (bf16[2,2,2,896,128]{4,3,2,1,0:T(8,128)(2,1)}, bf16[2,2,2,896,128]{4,3,2,1,0:T(8,128)(2,1)}, u32[]{:S(2)}, u32[]{:S(2)}) collective-permute-start(bf16[2,2,2,896,128]{4,3,2,1,0:T(8,128)(2,1)} %pad_maximum_fusion.4), channel_id=1, source_target_pairs={{0,1},{1,0},{2,3},{3,2},{4,5},{5,4},{6,7},{7,6},{8,9},{9,8},{10,11... | collective-permute-start | bytes 5505032 | tf_op jit(solution)/shard_map/ppermute | solution.py:951
  96.0 43.2 %collective-permute-start.4 = (bf16[2,2,2,928,128]{4,3,2,1,0:T(8,128)(2,1)S(1)}, bf16[2,2,2,928,128]{4,3,2,1,0:T(8,128)(2,1)}, u32[]{:S(2)}, u32[]{:S(2)}) collective-permute-start(bf16[2,2,2,928,128]{4,3,2,1,0:T(8,128)(2,1)S(1)} %pad_maximum_fusion.3), channel_id=1, source_target_pairs={{0,8},{1,9},{2,10},{3,11},{4,12},{5,13},{6,14},{7,15},{8,0},{9,1},... | collective-permute-start | bytes 5701640 | tf_op jit(solution)/shard_map/ppermute | solution.py:951
  97.4 41.3 %collective-permute-start.9 = (bf16[2,2,2,864,128]{4,3,2,1,0:T(8,128)(2,1)}, bf16[2,2,2,864,128]{4,3,2,1,0:T(8,128)(2,1)}, u32[]{:S(2)}, u32[]{:S(2)}) collective-permute-start(bf16[2,2,2,864,128]{4,3,2,1,0:T(8,128)(2,1)} %pad_maximum_fusion.6), channel_id=1, source_target_pairs={{0,16},{1,17},{2,18},{3,19},{4,20},{5,21},{6,22},{7,23},{8,24},{9,... | collective-permute-start | bytes 5308424 | tf_op jit(solution)/shard_map/ppermute | solution.py:951
  116.7 27.9 %collective-permute-start.5 = (bf16[2,2,2,928,128]{4,3,2,1,0:T(8,128)(2,1)}, bf16[2,2,2,928,128]{4,3,2,1,0:T(8,128)(2,1)}, u32[]{:S(2)}, u32[]{:S(2)}) collective-permute-start(bf16[2,2,2,928,128]{4,3,2,1,0:T(8,128)(2,1)} %collective-permute-done.3), channel_id=1, source_target_pairs={{0,8},{1,9},{2,10},{3,11},{4,12},{5,13},{6,14},{7,15},{8,0},{9,1},... | collective-permute-start | bytes 5701640 | tf_op jit(solution)/shard_map/ppermute | solution.py:951
  118.3 27.1 %collective-permute-start.10 = (bf16[2,2,2,864,128]{4,3,2,1,0:T(8,128)(2,1)}, bf16[2,2,2,864,128]{4,3,2,1,0:T(8,128)(2,1)}, u32[]{:S(2)}, u32[]{:S(2)}) collective-permute-start(bf16[2,2,2,864,128]{4,3,2,1,0:T(8,128)(2,1)} %pad_maximum_fusion.6), channel_id=1, source_target_pairs={{0,8},{1,9},{2,10},{3,11},{4,12},{5,13},{6,14},{7,15},{8,0},{9,1},... | collective-permute-start | bytes 5308424 | tf_op jit(solution)/shard_map/ppermute | solution.py:951
  340.0 40.4 %collective-permute-start.19 = (f32[8,2,288,128]{3,2,1,0:T(8,128)}, f32[8,2,288,128]{3,2,1,0:T(8,128)S(1)}, u32[]{:S(2)}, u32[]{:S(2)}) collective-permute-start(f32[8,2,288,128]{3,2,1,0:T(8,128)} %get-tuple-element.137), channel_id=1, source_target_pairs={{0,8},{1,9},{2,10},{3,11},{4,12},{5,13},{6,14},{7,15},{8,0},{9,1},... | collective-permute-start | bytes 7077896 | tf_op jit(solution)/shard_map/ppermute | solution.py:951
  340.5 45.2 %collective-permute-start.18 = (f32[8,2,304,128]{3,2,1,0:T(8,128)}, f32[8,2,304,128]{3,2,1,0:T(8,128)}, u32[]{:S(2)}, u32[]{:S(2)}) collective-permute-start(f32[8,2,304,128]{3,2,1,0:T(8,128)} %get-tuple-element.134), channel_id=1, source_target_pairs={{0,8},{1,9},{2,10},{3,11},{4,12},{5,13},{6,14},{7,15},{8,0},{9,1},... | collective-permute-start | bytes 7471112 | tf_op jit(solution)/shard_map/ppermute | solution.py:951
  388.7 43.1 %collective-permute-start.21 = (f32[2,2,2,288,128]{4,3,2,1,0:T(8,128)}, f32[2,2,2,288,128]{4,3,2,1,0:T(8,128)S(1)}, u32[]{:S(2)}, u32[]{:S(2)}) collective-permute-start(f32[2,2,2,288,128]{4,3,2,1,0:T(8,128)} %get-tuple-element.145), channel_id=1, source_target_pairs={{0,16},{1,17},{2,18},{3,19},{4,20},{5,21},{6,22},{7,23},{8,24},{9,... | collective-permute-start | bytes 3538952 | tf_op jit(solution)/shard_map/ppermute | solution.py:951
  390.0 44.1 %collective-permute-start.20 = (f32[2,2,2,304,128]{4,3,2,1,0:T(8,128)}, f32[2,2,2,304,128]{4,3,2,1,0:T(8,128)}, u32[]{:S(2)}, u32[]{:S(2)}) collective-permute-start(f32[2,2,2,304,128]{4,3,2,1,0:T(8,128)} %get-tuple-element.143), channel_id=1, source_target_pairs={{0,1},{1,0},{2,3},{3,2},{4,5},{5,4},{6,7},{7,6},{8,9},{9,8},{10,11... | collective-permute-start | bytes 3735560 | tf_op jit(solution)/shard_map/ppermute | solution.py:951
  436.4 41.5 %collective-permute-start.23 = (f32[2,2,288,128]{3,2,1,0:T(8,128)S(1)}, f32[2,2,288,128]{3,2,1,0:T(8,128)S(1)}, u32[]{:S(2)}, u32[]{:S(2)}) collective-permute-start(f32[2,2,288,128]{3,2,1,0:T(8,128)S(1)} %get-tuple-element.153), channel_id=1, source_target_pairs={{0,1},{1,0},{2,3},{3,2},{4,5},{5,4},{6,7},{7,6},{8,9},{9,8},{10,11... | collective-permute-start | bytes 1769480 | tf_op jit(solution)/shard_map/ppermute | solution.py:951
  437.0 41.1 %collective-permute-start.22 = (f32[2,2,304,128]{3,2,1,0:T(8,128)}, f32[2,2,304,128]{3,2,1,0:T(8,128)S(1)}, u32[]{:S(2)}, u32[]{:S(2)}) collective-permute-start(f32[2,2,304,128]{3,2,1,0:T(8,128)} %get-tuple-element.152), channel_id=1, source_target_pairs={{0,16},{1,17},{2,18},{3,19},{4,20},{5,21},{6,22},{7,23},{8,24},{9,... | collective-permute-start | bytes 1867784 | tf_op jit(solution)/shard_map/ppermute | solution.py:951
  478.1 34.5 %collective-permute-start.25 = (f32[2,288,128]{2,1,0:T(8,128)S(1)}, f32[2,288,128]{2,1,0:T(8,128)S(1)}, u32[]{:S(2)}, u32[]{:S(2)}) collective-permute-start(f32[2,288,128]{2,1,0:T(8,128)S(1)} %get-tuple-element.180), channel_id=1, source_target_pairs={{0,4},{1,5},{2,6},{3,7},{4,0},{5,1},{6,2},{7,3},{8,12},{9,13},{10,... | collective-permute-start | bytes 884744 | tf_op jit(solution)/shard_map/ppermute | solution.py:951
  480.8 32.5 %collective-permute-start.24 = (f32[2,304,128]{2,1,0:T(8,128)S(1)}, f32[2,304,128]{2,1,0:T(8,128)S(1)}, u32[]{:S(2)}, u32[]{:S(2)}) collective-permute-start(f32[2,304,128]{2,1,0:T(8,128)S(1)} %get-tuple-element.179), channel_id=1, source_target_pairs={{0,4},{1,5},{2,6},{3,7},{4,0},{5,1},{6,2},{7,3},{8,12},{9,13},{10,... | collective-permute-start | bytes 933896 | tf_op jit(solution)/shard_map/ppermute | solution.py:951
  559.2 51.9 %collective-permute-start.28 = (f16[2,2,2,1112,128]{4,3,1,0,2:T(8,128)(2,1)S(1)}, f16[2,2,2,1112,128]{4,3,1,0,2:T(8,128)(2,1)}, u32[]{:S(2)}, u32[]{:S(2)}) collective-permute-start(f16[2,2,2,1112,128]{4,3,1,0,2:T(8,128)(2,1)S(1)} %concatenate.55), channel_id=1, source_target_pairs={{0,1},{1,0},{2,3},{3,2},{4,5},{5,4},{6,7},{7,6},{8,9},{9,8},{10,11... | collective-permute-start | bytes 6832136 | tf_op jit(solution)/shard_map/ppermute | solution.py:951
  569.5 51.9 %collective-permute-start.33 = (f16[2,2,2,1112,128]{4,3,1,0,2:T(8,128)(2,1)}, f16[2,2,2,1112,128]{4,3,1,0,2:T(8,128)(2,1)}, u32[]{:S(2)}, u32[]{:S(2)}) collective-permute-start(f16[2,2,2,1112,128]{4,3,1,0,2:T(8,128)(2,1)} %concatenate.58), channel_id=1, source_target_pairs={{0,16},{1,17},{2,18},{3,19},{4,20},{5,21},{6,22},{7,23},{8,24},{9,... | collective-permute-start | bytes 6832136 | tf_op jit(solution)/shard_map/ppermute | solution.py:951
  574.2 62.8 %collective-permute-start.37 = (f32[304,128]{1,0:T(8,128)S(1)}, f32[304,128]{1,0:T(8,128)}, u32[]{:S(2)}, u32[]{:S(2)}) collective-permute-start(f32[304,128]{1,0:T(8,128)S(1)} %fusion.34), channel_id=1, source_target_pairs={{0,2},{1,3},{2,0},{3,1},{4,6},{5,7},{6,4},{7,5},{8,10},{9,11},{10,... | collective-permute-start | bytes 466952 | tf_op jit(solution)/shard_map/ppermute | solution.py:951
  619.9 28.3 %collective-permute-start.29 = (f16[2,2,1112,128]{3,2,1,0:T(8,128)(2,1)}, f16[2,2,1112,128]{3,2,1,0:T(8,128)(2,1)}, u32[]{:S(2)}, u32[]{:S(2)}) collective-permute-start(f16[2,2,1112,128]{3,2,1,0:T(8,128)(2,1)} %concatenate.56), channel_id=1, source_target_pairs={{0,16},{1,17},{2,18},{3,19},{4,20},{5,21},{6,22},{7,23},{8,24},{9,... | collective-permute-start | bytes 3416072 | tf_op jit(solution)/shard_map/ppermute | solution.py:951
  634.8 26.6 %collective-permute-start.34 = (f16[2,2,1112,128]{3,2,1,0:T(8,128)(2,1)}, f16[2,2,1112,128]{3,2,1,0:T(8,128)(2,1)}, u32[]{:S(2)}, u32[]{:S(2)}) collective-permute-start(f16[2,2,1112,128]{3,2,1,0:T(8,128)(2,1)} %concatenate.59), channel_id=1, source_target_pairs={{0,1},{1,0},{2,3},{3,2},{4,5},{5,4},{6,7},{7,6},{8,9},{9,8},{10,11... | collective-permute-start | bytes 3416072 | tf_op jit(solution)/shard_map/ppermute | solution.py:951
  638.8 36.3 %collective-permute-start.48 = (f32[592,128]{1,0:T(8,128)}, f32[592,128]{1,0:T(8,128)}, u32[]{:S(2)}, u32[]{:S(2)}) collective-permute-start(f32[592,128]{1,0:T(8,128)} %pad_maximum_fusion.21), channel_id=1, source_target_pairs={{0,16},{1,17},{2,18},{3,19},{4,20},{5,21},{6,22},{7,23},{8,24},{9,... | collective-permute-start | bytes 909320 | tf_op jit(solution)/shard_map/ppermute | solution.py:951
  669.8 41.4 %collective-permute-start.30 = (f16[2,1112,128]{2,1,0:T(8,128)(2,1)}, f16[2,1112,128]{2,1,0:T(8,128)(2,1)}, u32[]{:S(2)}, u32[]{:S(2)}) collective-permute-start(f16[2,1112,128]{2,1,0:T(8,128)(2,1)} %concatenate.57), channel_id=1, source_target_pairs={{0,4},{1,5},{2,6},{3,7},{4,0},{5,1},{6,2},{7,3},{8,12},{9,13},{10,... | collective-permute-start | bytes 1708040 | tf_op jit(solution)/shard_map/ppermute | solution.py:951
  677.8 45.1 %collective-permute-start.49 = (f32[2,592,128]{2,1,0:T(8,128)}, f32[2,592,128]{2,1,0:T(8,128)}, u32[]{:S(2)}, u32[]{:S(2)}) collective-permute-start(f32[2,592,128]{2,1,0:T(8,128)} %pad_maximum_fusion.16), channel_id=1, source_target_pairs={{0,8},{1,9},{2,10},{3,11},{4,12},{5,13},{6,14},{7,15},{8,0},{9,1},... | collective-permute-start | bytes 1818632 | tf_op jit(solution)/shard_map/ppermute | solution.py:951
  679.0 41.8 %collective-permute-start.35 = (f16[2,1112,128]{2,1,0:T(8,128)(2,1)S(1)}, f16[2,1112,128]{2,1,0:T(8,128)(2,1)S(1)}, u32[]{:S(2)}, u32[]{:S(2)}) collective-permute-start(f16[2,1112,128]{2,1,0:T(8,128)(2,1)S(1)} %concatenate.60), channel_id=1, source_target_pairs={{0,4},{1,5},{2,6},{3,7},{4,0},{5,1},{6,2},{7,3},{8,12},{9,13},{10,... | collective-permute-start | bytes 1708040 | tf_op jit(solution)/shard_map/ppermute | solution.py:951
  714.4 18.5 %collective-permute-start.31 = (f32[1104,128]{1,0:T(8,128)S(1)}, f32[1104,128]{1,0:T(8,128)S(1)}, u32[]{:S(2)}, u32[]{:S(2)}) collective-permute-start(f32[1104,128]{1,0:T(8,128)S(1)} %fusion.31), channel_id=1, source_target_pairs={{0,2},{1,3},{2,0},{3,1},{4,6},{5,7},{6,4},{7,5},{8,10},{9,11},{10,... | collective-permute-start | bytes 1695752 | tf_op jit(solution)/shard_map/ppermute | solution.py:951
  722.2 23.9 %collective-permute-start.36 = (f32[1104,128]{1,0:T(8,128)S(1)}, f32[1104,128]{1,0:T(8,128)S(1)}, u32[]{:S(2)}, u32[]{:S(2)}) collective-permute-start(f32[1104,128]{1,0:T(8,128)S(1)} %fusion.30), channel_id=1, source_target_pairs={{0,2},{1,3},{2,0},{3,1},{4,6},{5,7},{6,4},{7,5},{8,10},{9,11},{10,... | collective-permute-start | bytes 1695752 | tf_op jit(solution)/shard_map/ppermute | solution.py:951
  733.1 34.8 %collective-permute-start.44 = (f32[1104,128]{1,0:T(8,128)S(1)}, f32[1104,128]{1,0:T(8,128)S(1)}, u32[]{:S(2)}, u32[]{:S(2)}) collective-permute-start(f32[1104,128]{1,0:T(8,128)S(1)} %bitcast_add_fusion.16), channel_id=1, source_target_pairs={{0,16},{1,17},{2,18},{3,19},{4,20},{5,21},{6,22},{7,23},{8,24},{9,... | collective-permute-start | bytes 1695752 | tf_op jit(solution)/shard_map/ppermute | solution.py:951
  (55 other events, 594.5 us)
